TPU v7x, 128 devices: a whole 4x4x4 slice. The times are simulated.
128 devices in a mesh: dp: 16 (over x, y_lo, core), ctx: 8 (over z, y_hi).
Axes of the slice: x: 4, y: 4 (y_hi: 2, y_lo: 2; y = y_hi * 2 + y_lo), z: 4, core: 2. Of those that a mesh axis runs over, the one named last changes fastest.
Arguments:
- tokens: bfloat16 [32, 1024, 1280], P('dp', 'ctx'), may hold values from -6 to 6
- lengths: int32 [32], P('dp'), may hold values from 256 to 1024, as said below
- cotangent: bfloat16 [32, 1024, 1280], P('dp', 'ctx'), may hold values from -6 to 6
- ln1_gain: bfloat16 [1280], P(('dp', 'ctx')), may hold values from 0.25 to 1.75
- ln1_bias: bfloat16 [1280], P(('dp', 'ctx')), may hold values from -1.75 to 1.75
- w_qkv: bfloat16 [1280, 3840], P(('dp', 'ctx')), may hold values from -0.15625 to 0.15625
- q_bias: bfloat16 [1280], P(('dp', 'ctx')), may hold values from -1.75 to 1.75
- v_bias: bfloat16 [1280], P(('dp', 'ctx')), may hold values from -0.625 to 0.625
- w_proj: bfloat16 [1280, 1280], P(('dp', 'ctx')), may hold values from -0.625 to 0.625
- proj_bias: bfloat16 [1280], P(('dp', 'ctx')), may hold values from -1.75 to 1.75
- ln2_gain: bfloat16 [1280], P(('dp', 'ctx')), may hold values from 0.25 to 1.75
- ln2_bias: bfloat16 [1280], P(('dp', 'ctx')), may hold values from -1.75 to 1.75
- w_fc: bfloat16 [1280, 5120], P(('dp', 'ctx')), may hold values from -0.15625 to 0.15625
- fc_bias: bfloat16 [5120], P(('dp', 'ctx')), may hold values from -1.75 to 1.75
- w_out: bfloat16 [5120, 1280], P(('dp', 'ctx')), may hold values from -0.078125 to 0.078125
- out_bias: bfloat16 [1280], P(('dp', 'ctx')), may hold values from -1.75 to 1.75
Outputs:
- layer_out: bfloat16 [32, 1024, 1280], P('dp', 'ctx')
- input_grad: float32 [32, 1024, 1280], P('dp', 'ctx')
- ln1_gain_grad: float32 [1280], P(('dp', 'ctx'))
- ln1_bias_grad: float32 [1280], P(('dp', 'ctx'))
- w_qkv_grad: float32 [1280, 3840], P(('dp', 'ctx'))
- q_bias_grad: float32 [1280], P(('dp', 'ctx'))
- v_bias_grad: float32 [1280], P(('dp', 'ctx'))
- w_proj_grad: float32 [1280, 1280], P(('dp', 'ctx'))
- proj_bias_grad: float32 [1280], P(('dp', 'ctx'))
- ln2_gain_grad: float32 [1280], P(('dp', 'ctx'))
- ln2_bias_grad: float32 [1280], P(('dp', 'ctx'))
- w_fc_grad: float32 [1280, 5120], P(('dp', 'ctx'))
- fc_bias_grad: float32 [5120], P(('dp', 'ctx'))
- w_out_grad: float32 [5120, 1280], P(('dp', 'ctx'))
- out_bias_grad: float32 [1280], P(('dp', 'ctx'))
Inputs may be any that keep to these rules, and one draw needn't show every extreme that they name: `lengths`: in each aligned block of 2 entries (the sequences of one data group) one entry, at a place drawn from the seed, equals 1024.
All inputs are finite; a program needn't handle non-finite values.
Results may differ from a plain program's by a relative error of at most 0.039.
Values may be sent and summed in bfloat16 or wider, within the bound.
No kernel may reach another device: no remote copies, remote signals or barrier semaphores. Data moves between devices by JAX's collectives and lax.ppermute only.
A program may use at most 320 MiB of HBM per device.

v0:
```python
import math

import jax
import jax.numpy as jnp
from jax import lax
from jax.sharding import PartitionSpec as P

HEADS = 20


NORM_EPS = 1e-05
MASKED = -1000000000.0


def layer_norm(token_rows, gain, shift):
    centre = jnp.mean(token_rows, axis=-1, keepdims=True)
    centred = token_rows - centre
    spread = jnp.mean(centred * centred, axis=-1, keepdims=True)
    return centred * lax.rsqrt(spread + NORM_EPS) * gain + shift


def norm_back(token_rows, gain, shift, grad_rows):
    result, pullback = jax.vjp(layer_norm, token_rows, gain, shift)
    return pullback(grad_rows)


def gelu_back(pre_act, grad_rows):

    def smooth_gate(value_in):
        return jax.nn.gelu(value_in, approximate=True)

    result, pullback = jax.vjp(smooth_gate, pre_act)
    return pullback(grad_rows)[0]


def project_rows(left, weight):
    return jnp.einsum("sck,kn->scn", left, weight, preferred_element_type=jnp.float32)


def weight_grad(left, grad_rows):
    return jnp.einsum("sck,scn->kn", left, grad_rows, preferred_element_type=jnp.float32)


def back_apply(grad_rows, weight):
    return jnp.einsum("scn,kn->sck", grad_rows, weight, preferred_element_type=jnp.float32)


def mask_of(query_pos, key_pos, lengths):
    causal = key_pos[None, :] <= query_pos[:, None]
    inside = key_pos[None, :] < lengths[:, None]
    return causal[None, None] & inside[:, None, None, :]


def key_mask(query_pos, lengths, start_pos, key_count):
    key_pos = start_pos + jnp.arange(key_count, dtype=jnp.int32)
    return mask_of(query_pos, key_pos, lengths)


def split_piece(kv_piece, head_count):
    seq_count, key_count, double_width = kv_piece.shape
    model_width = double_width // 2
    head_dim = model_width // head_count
    key_heads = kv_piece[:, :, :model_width].reshape(seq_count, key_count, head_count, head_dim)
    value_heads = kv_piece[:, :, model_width:].reshape(seq_count, key_count, head_count, head_dim)
    return (key_heads, value_heads)


def attend(fold_state, kv_piece, start_pos, query_heads, query_pos, lengths, score_scale):
    run_max, run_sum, run_acc = fold_state
    key_heads, value_heads = split_piece(kv_piece, run_max.shape[1])
    scores = (
        jnp.einsum("sqhd,skhd->shqk", query_heads, key_heads, preferred_element_type=jnp.float32)
        * score_scale
    )
    scores = jnp.where(key_mask(query_pos, lengths, start_pos, kv_piece.shape[1]), scores, MASKED)
    new_max = jnp.maximum(run_max, jnp.max(scores, axis=-1))
    decay = jnp.exp(run_max - new_max)
    weights = jnp.exp(scores - new_max[..., None])
    run_sum = run_sum * decay + jnp.sum(weights, axis=-1)
    run_acc = run_acc * decay[..., None] + jnp.einsum(
        "shqk,skhd->shqd",
        weights.astype(jnp.bfloat16),
        value_heads,
        preferred_element_type=jnp.float32,
    )
    return (new_max, run_sum, run_acc)


def back_scores(
    query_heads, grad_heads, log_total, row_delta, key_heads, value_heads, allowed, score_scale
):
    scores = (
        jnp.einsum("sqhd,skhd->shqk", query_heads, key_heads, preferred_element_type=jnp.float32)
        * score_scale
    )
    probs = jnp.where(allowed, jnp.exp(scores - log_total[..., None]), 0.0)
    grad_probs = jnp.einsum(
        "sqhd,skhd->shqk", grad_heads, value_heads, preferred_element_type=jnp.float32
    )
    grad_scores = (probs * (grad_probs - row_delta[..., None])).astype(jnp.bfloat16)
    return (probs, grad_scores)


def attend_back(
    fold_state,
    kv_piece,
    start_pos,
    query_heads,
    grad_heads,
    log_total,
    row_delta,
    query_pos,
    lengths,
    score_scale,
):
    grad_query, grad_kv = fold_state
    key_heads, value_heads = split_piece(kv_piece, log_total.shape[1])
    seq_count, key_count, double_width = kv_piece.shape
    allowed = key_mask(query_pos, lengths, start_pos, key_count)
    probs, grad_scores = back_scores(
        query_heads, grad_heads, log_total, row_delta, key_heads, value_heads, allowed, score_scale
    )
    grad_query = (
        grad_query
        + jnp.einsum("shqk,skhd->sqhd", grad_scores, key_heads, preferred_element_type=jnp.float32)
        * score_scale
    )
    grad_key = (
        jnp.einsum("shqk,sqhd->skhd", grad_scores, query_heads, preferred_element_type=jnp.float32)
        * score_scale
    )
    grad_value = jnp.einsum(
        "shqk,sqhd->skhd",
        probs.astype(jnp.bfloat16),
        grad_heads,
        preferred_element_type=jnp.float32,
    )
    grad_block = jnp.concatenate(
        [
            grad_key.reshape(seq_count, key_count, double_width // 2),
            grad_value.reshape(seq_count, key_count, double_width // 2),
        ],
        axis=-1,
    )
    grad_kv = lax.dynamic_update_slice_in_dim(grad_kv, grad_block, start_pos, 1)
    return (grad_query, grad_kv)


def fold_kept(fold_step, initial, whole_kv, piece_count, span_len):

    def one_piece(loop_index, fold_state):
        start_pos = (loop_index * span_len).astype(jnp.int32)
        kv_piece = lax.dynamic_slice_in_dim(whole_kv, start_pos, span_len, 1)
        return fold_step(fold_state, kv_piece, start_pos)

    return lax.fori_loop(0, piece_count, one_piece, initial)


def per_device(
    tokens,
    lengths,
    cotangent,
    ln1_gain,
    ln1_bias,
    w_qkv,
    q_bias,
    v_bias,
    w_proj,
    proj_bias,
    ln2_gain,
    ln2_bias,
    w_fc,
    fc_bias,
    w_out,
    out_bias,
):
    seq_count, span_len, model_width = tokens.shape
    head_count = HEADS
    head_dim = model_width // head_count
    score_scale = 1.0 / math.sqrt(head_dim)
    ctx_ranks = lax.axis_size("ctx")
    ctx_rank = lax.axis_index("ctx")
    first_pos = ctx_rank * span_len
    query_pos = first_pos + jnp.arange(span_len, dtype=jnp.int32)
    longest = jnp.max(lengths)
    last_needed = jnp.minimum(first_pos + span_len, longest)
    attn_set = (
        lax.all_gather(ln1_gain, ("dp", "ctx"), axis=0, tiled=True),
        lax.all_gather(ln1_bias, ("dp", "ctx"), axis=0, tiled=True),
        lax.all_gather(w_qkv, ("dp", "ctx"), axis=0, tiled=True),
        lax.all_gather(q_bias, ("dp", "ctx"), axis=0, tiled=True),
        lax.all_gather(v_bias, ("dp", "ctx"), axis=0, tiled=True),
        lax.all_gather(w_proj, ("dp", "ctx"), axis=0, tiled=True),
        lax.all_gather(proj_bias, ("dp", "ctx"), axis=0, tiled=True),
    )
    gain_one, shift_one, qkv_weight, query_bias, value_bias, proj_weight, proj_shift = attn_set
    token_rows = tokens.astype(jnp.float32)
    normed_one = layer_norm(token_rows, gain_one, shift_one).astype(jnp.bfloat16)
    qkv = project_rows(normed_one, qkv_weight)
    query_rows = (qkv[..., :model_width] + query_bias).astype(jnp.bfloat16)
    key_rows = qkv[..., model_width : 2 * model_width].astype(jnp.bfloat16)
    value_rows = (qkv[..., 2 * model_width :] + value_bias).astype(jnp.bfloat16)
    kv_local = jnp.concatenate([key_rows, value_rows], axis=-1)
    query_heads = query_rows.reshape(seq_count, span_len, head_count, head_dim)

    def forward_piece(fold_state, kv_piece, start_pos):

        def forward_work(state_in):
            return attend(
                state_in, kv_piece, start_pos, query_heads, query_pos, lengths, score_scale
            )

        def forward_skip(state_in):
            return state_in

        return lax.cond(start_pos < last_needed, forward_work, forward_skip, fold_state)

    initial = (
        jnp.full((seq_count, head_count, span_len), -1e30, jnp.float32),
        jnp.zeros((seq_count, head_count, span_len), jnp.float32),
        jnp.zeros((seq_count, head_count, span_len, head_dim), jnp.float32),
    )
    whole_kv = lax.all_gather(kv_local, "ctx", axis=1, tiled=True)
    run_max, run_sum, run_acc = fold_kept(forward_piece, initial, whole_kv, ctx_rank + 1, span_len)
    attention_heads = run_acc / run_sum[..., None]
    attention_rows = attention_heads.transpose(0, 2, 1, 3).reshape(seq_count, span_len, model_width)
    attended = attention_rows.astype(jnp.bfloat16)
    residual = token_rows + project_rows(attended, proj_weight) + proj_shift
    mlp_set = (
        lax.all_gather(ln2_gain, ("dp", "ctx"), axis=0, tiled=True),
        lax.all_gather(ln2_bias, ("dp", "ctx"), axis=0, tiled=True),
        lax.all_gather(w_fc, ("dp", "ctx"), axis=0, tiled=True),
        lax.all_gather(fc_bias, ("dp", "ctx"), axis=0, tiled=True),
        lax.all_gather(w_out, ("dp", "ctx"), axis=0, tiled=True),
        lax.all_gather(out_bias, ("dp", "ctx"), axis=0, tiled=True),
    )
    gain_two, shift_two, fc_weight, fc_shift, out_weight, out_shift = mlp_set
    normed_two = layer_norm(residual, gain_two, shift_two).astype(jnp.bfloat16)
    pre_act = project_rows(normed_two, fc_weight) + fc_shift
    active = jax.nn.gelu(pre_act, approximate=True).astype(jnp.bfloat16)
    layer_out = (residual + project_rows(active, out_weight) + out_shift).astype(jnp.bfloat16)
    valid_rows = (query_pos[None, :] < lengths[:, None]).astype(jnp.float32)[..., None]
    grad_final = cotangent.astype(jnp.float32) * valid_rows
    grad_low = grad_final.astype(jnp.bfloat16)
    mlp_again = (
        lax.all_gather(ln2_gain, ("dp", "ctx"), axis=0, tiled=True),
        lax.all_gather(ln2_bias, ("dp", "ctx"), axis=0, tiled=True),
        lax.all_gather(w_fc, ("dp", "ctx"), axis=0, tiled=True),
        lax.all_gather(fc_bias, ("dp", "ctx"), axis=0, tiled=True),
        lax.all_gather(w_out, ("dp", "ctx"), axis=0, tiled=True),
        lax.all_gather(out_bias, ("dp", "ctx"), axis=0, tiled=True),
    )
    gain_two, shift_two, fc_weight, fc_shift, out_weight, out_shift = mlp_again
    out_weight_grad = weight_grad(active, grad_low)
    out_shift_grad = jnp.sum(grad_final, axis=(0, 1))
    grad_active = back_apply(grad_low, out_weight)
    grad_pre = gelu_back(pre_act, grad_active).astype(jnp.bfloat16)
    fc_weight_grad = weight_grad(normed_two, grad_pre)
    fc_shift_grad = jnp.sum(grad_pre.astype(jnp.float32), axis=(0, 1))
    grad_norm_two = back_apply(grad_pre, fc_weight)
    grad_res_norm, gain_two_grad, shift_two_grad = norm_back(
        residual, gain_two, shift_two, grad_norm_two
    )
    mlp_grads = (
        lax.psum_scatter(
            gain_two_grad.astype(jnp.float32), ("dp", "ctx"), scatter_dimension=0, tiled=True
        ),
        lax.psum_scatter(
            shift_two_grad.astype(jnp.float32), ("dp", "ctx"), scatter_dimension=0, tiled=True
        ),
        lax.psum_scatter(fc_weight_grad, ("dp", "ctx"), scatter_dimension=0, tiled=True),
        lax.psum_scatter(fc_shift_grad, ("dp", "ctx"), scatter_dimension=0, tiled=True),
        lax.psum_scatter(out_weight_grad, ("dp", "ctx"), scatter_dimension=0, tiled=True),
        lax.psum_scatter(out_shift_grad, ("dp", "ctx"), scatter_dimension=0, tiled=True),
    )
    grad_residual = (grad_final + grad_res_norm).astype(jnp.bfloat16)
    attn_again = (
        lax.all_gather(ln1_gain, ("dp", "ctx"), axis=0, tiled=True),
        lax.all_gather(ln1_bias, ("dp", "ctx"), axis=0, tiled=True),
        lax.all_gather(w_qkv, ("dp", "ctx"), axis=0, tiled=True),
        lax.all_gather(q_bias, ("dp", "ctx"), axis=0, tiled=True),
        lax.all_gather(v_bias, ("dp", "ctx"), axis=0, tiled=True),
        lax.all_gather(w_proj, ("dp", "ctx"), axis=0, tiled=True),
        lax.all_gather(proj_bias, ("dp", "ctx"), axis=0, tiled=True),
    )
    gain_one, shift_one, qkv_weight, query_bias, value_bias, proj_weight, proj_shift = attn_again
    proj_weight_grad = weight_grad(attended, grad_residual)
    proj_shift_grad = jnp.sum(grad_residual.astype(jnp.float32), axis=(0, 1))
    grad_attended = back_apply(grad_residual, proj_weight).astype(jnp.bfloat16)
    grad_heads = grad_attended.reshape(seq_count, span_len, head_count, head_dim)
    log_total = run_max + jnp.log(run_sum)
    row_delta = jnp.sum(
        grad_heads.astype(jnp.float32).transpose(0, 2, 1, 3) * attention_heads, axis=-1
    )

    def backward_piece(fold_state, kv_piece, start_pos):

        def backward_work(state_in):
            return attend_back(
                state_in,
                kv_piece,
                start_pos,
                query_heads,
                grad_heads,
                log_total,
                row_delta,
                query_pos,
                lengths,
                score_scale,
            )

        def backward_skip(state_in):
            return state_in

        return lax.cond(start_pos < last_needed, backward_work, backward_skip, fold_state)

    grad_query_zero = jnp.zeros((seq_count, span_len, head_count, head_dim), jnp.float32)
    initial_back = (
        grad_query_zero,
        jnp.zeros((seq_count, span_len * ctx_ranks, 2 * model_width), jnp.float32),
    )
    back_state = fold_kept(backward_piece, initial_back, whole_kv, ctx_rank + 1, span_len)
    grad_query_heads = back_state[0]
    grad_kv = lax.psum_scatter(
        back_state[1].astype(jnp.bfloat16), "ctx", scatter_dimension=1, tiled=True
    )
    grad_query = grad_query_heads.reshape(seq_count, span_len, model_width).astype(jnp.bfloat16)
    grad_qkv = jnp.concatenate([grad_query, grad_kv], axis=-1)
    qkv_weight_grad = weight_grad(normed_one, grad_qkv)
    query_bias_grad = jnp.sum(grad_query.astype(jnp.float32), axis=(0, 1))
    value_bias_grad = jnp.sum(grad_qkv[..., 2 * model_width :].astype(jnp.float32), axis=(0, 1))
    grad_norm_one = back_apply(grad_qkv, qkv_weight)
    grad_rows_norm, gain_one_grad, shift_one_grad = norm_back(
        token_rows, gain_one, shift_one, grad_norm_one
    )
    input_grad = grad_residual.astype(jnp.float32) + grad_rows_norm
    attn_grads = (
        lax.psum_scatter(
            gain_one_grad.astype(jnp.float32), ("dp", "ctx"), scatter_dimension=0, tiled=True
        ),
        lax.psum_scatter(
            shift_one_grad.astype(jnp.float32), ("dp", "ctx"), scatter_dimension=0, tiled=True
        ),
        lax.psum_scatter(qkv_weight_grad, ("dp", "ctx"), scatter_dimension=0, tiled=True),
        lax.psum_scatter(query_bias_grad, ("dp", "ctx"), scatter_dimension=0, tiled=True),
        lax.psum_scatter(value_bias_grad, ("dp", "ctx"), scatter_dimension=0, tiled=True),
        lax.psum_scatter(proj_weight_grad, ("dp", "ctx"), scatter_dimension=0, tiled=True),
        lax.psum_scatter(proj_shift_grad, ("dp", "ctx"), scatter_dimension=0, tiled=True),
    )
    return (
        layer_out,
        input_grad,
        attn_grads[0],
        attn_grads[1],
        attn_grads[2],
        attn_grads[3],
        attn_grads[4],
        attn_grads[5],
        attn_grads[6],
        mlp_grads[0],
        mlp_grads[1],
        mlp_grads[2],
        mlp_grads[3],
        mlp_grads[4],
        mlp_grads[5],
    )


def solution(mesh):
    in_specs = (
        P("dp", "ctx", None),
        P("dp"),
        P("dp", "ctx", None),
        P(("dp", "ctx")),
        P(("dp", "ctx")),
        P(("dp", "ctx"), None),
        P(("dp", "ctx")),
        P(("dp", "ctx")),
        P(("dp", "ctx"), None),
        P(("dp", "ctx")),
        P(("dp", "ctx")),
        P(("dp", "ctx")),
        P(("dp", "ctx"), None),
        P(("dp", "ctx")),
        P(("dp", "ctx"), None),
        P(("dp", "ctx")),
    )
    out_specs = (
        P("dp", "ctx", None),
        P("dp", "ctx", None),
        P(("dp", "ctx")),
        P(("dp", "ctx")),
        P(("dp", "ctx"), None),
        P(("dp", "ctx")),
        P(("dp", "ctx")),
        P(("dp", "ctx"), None),
        P(("dp", "ctx")),
        P(("dp", "ctx")),
        P(("dp", "ctx")),
        P(("dp", "ctx"), None),
        P(("dp", "ctx")),
        P(("dp", "ctx"), None),
        P(("dp", "ctx")),
    )
    return jax.shard_map(
        per_device, mesh=mesh, in_specs=in_specs, out_specs=out_specs, check_vma=False
    )
```

profile of v0, /device:TPU:0, one launch (start us, length us, event | category | flops | bytes accessed | tf_op | source)
XLA Modules:
  0.0 2770.0 jit_solution(14820264691774418423)
XLA Ops:
  17.1 68.9 %all-reduce.23 = (bf16[1280]{0:T(1024)(128)(2,1)S(1)}, bf16[1280]{0:T(1024)(128)(2,1)S(1)}, bf16[1280]{0:T(1024)(128)(2,1)S(1)}, bf16[1280]{0:T(1024)(128)(2,1)S...) all-reduce(bf16[1280]{0:T(1024)(128)(2,1)S(1)} %dynamic-update-slic, ...), channel_id=1, replica_groups=mesh['dp'=16,'ctx'=8] {'dp','ctx'}, use_global_device_ids=true, to_apply=%add.1 | all-reduce | flops 15360 | bytes 61440
  87.6 249.9 %all-gather.13.cloned.1.call-done = bf16[128,10,3840]{2,1,0:T(8,128)(2,1)} async-done(((bf16[1,10,3840]{2,1,0:T(8,128)(2,1)}), bf16[128,10,3840]{2,1,0:T(8,128)(2,1)}) %all-gather.13.cloned.1.call-update) | async-done | bytes 9830416 | tf_op jit(solution)/shard_map/all_gather | solution.py:190
  337.5 15.7 reshape.328
  353.2 6.7 fusion.71
  363.6 285.6 %all-gather.15.cloned.1.call-done = bf16[128,10,1280]{2,1,0:T(8,128)(2,1)} async-done(((bf16[1,10,1280]{2,1,0:T(8,128)(2,1)}), bf16[128,10,1280]{2,1,0:T(8,128)(2,1)}) %all-gather.15.cloned.1.call-update) | async-done | bytes 3276816 | tf_op jit(solution)/shard_map/all_gather | solution.py:193
  649.1 7.1 reshape.329
  656.5 329.6 %all-gather.17.cloned.1.call-done = bf16[128,10,5120]{2,1,0:T(8,128)(2,1)} async-done(((bf16[1,10,5120]{2,1,0:T(8,128)(2,1)}), bf16[128,10,5120]{2,1,0:T(8,128)(2,1)}) %all-gather.17.cloned.1.call-update) | async-done | bytes 13107216 | tf_op jit(solution)/shard_map/all_gather | solution.py:232
  986.2 24.7 reshape.330
  1010.8 105.3 %all-gather.9.cloned.1.call-done = bf16[2,1024,2560]{2,1,0:T(8,128)(2,1)} async-done(((bf16[2,128,2560]{2,1,0:T(8,128)(2,1)}), bf16[2,1024,2560]{2,1,0:T(8,128)(2,1)}) %all-gather.9.cloned.1.call-update) | async-done | bytes 10485776 | tf_op jit(solution)/shard_map/all_gather | solution.py:223
  1116.2 13.7 copy.66
  1130.1 4.1 while.28
  1130.1 4.1 conditional.6
  1135.3 3.1 fusion.80
  1138.7 10.2 convolution_add_fusion.1
  1149.0 287.7 %all-gather.11.cloned.1.call-done = bf16[5120,1280]{1,0:T(8,128)(2,1)} async-done(((bf16[40,1280]{1,0:T(8,128)(2,1)}), bf16[5120,1280]{1,0:T(8,128)(2,1)}) %all-gather.11.cloned.1.call-update) | async-done | bytes 13107216 | tf_op jit(solution)/shard_map/all_gather | solution.py:234
  1436.7 9.9 convert_reduce_fusion
  1446.6 8.7 fusion.78
  1460.5 2.2 copy.68
  1464.2 5.2 broadcast_in_dim.70
  1469.4 7.6 while.29
  1469.4 7.6 conditional.7
  1477.0 13.7 copy.70
  1493.2 3.7 convolution_bitcast_fusion.3
  1497.0 10.8 convolution_bitcast_fusion.1
  1507.7 170.8 %reduce-scatter.3.cloned.1.call-done = bf16[2,128,2560]{2,1,0:T(8,128)(2,1)} async-done(((bf16[2,1024,2560]{2,1,0:T(8,128)(2,1)}), bf16[2,128,2560]{2,1,0:T(8,128)(2,1)}) %reduce-scatter.3.cloned.1.call-update) | async-done | bytes 1310736 | tf_op jit(solution)/shard_map/reduce_scatter | solution.py:324
  1678.5 9.5 convolution_bitcast_fusion.2
  1688.6 17.2 convolution_bitcast_fusion
  1706.5 12.3 fusion.46
  1718.8 7.1 fusion.79
  1726.5 66.2 %all-reduce.21 = (f32[1280]{0:T(1024)S(1)}, f32[1280]{0:T(1024)S(1)}, f32[1280]{0:T(1024)S(1)}, f32[1280]{0:T(1024)S(1)}, f32[1280]{0:T(1024)S(1)}, /*index=5*/f...) all-reduce(bf16[1280]{0:T(1024)(128)(2,1)S(1)} %get-tuple-element.4, ...), channel_id=3, replica_groups=mesh['dp'=16,'ctx'=8] {'dp','ctx'}, use_global_device_ids=true, to_apply=%region_22.23.clone | all-reduce | flops 15360 | bytes 112640
  1799.6 256.9 %all-reduce.26.cloned.1.call-done = (f32[1280,3840]{1,0:T(8,128)}, f32[1280,1280]{1,0:T(8,128)}, f32[1280,5120]{1,0:T(8,128)}) async-done(((f32[1280,3840]{1,0:T(8,128)}, f32[1280,1280]{1,0:T(8,128)}, f32[1280,5120]{1,0:T(8,128)}), (f32[1280,3840]{1,0:T(8,128)}, f32[1280,1280]{1,0:T(8,128)}, f32[1280,5120]{1,0:T(8,128)})) %all-reduce.26.cloned.1.call-update) | async-done | bytes 52428816
  2061.6 701.4 %reduce-scatter.5.cloned.1.call-done = f32[40,1280]{1,0:T(8,128)} async-done(((f32[5120,1280]{1,0:T(8,128)}), f32[40,1280]{1,0:T(8,128)}) %reduce-scatter.5.cloned.1.call-update) | async-done | bytes 204816 | tf_op jit(solution)/shard_map/reduce_scatter | solution.py:273
  (146 shorter events, 50.6 us)
Async XLA Ops:
  7.2 80.1 %copy-start = (bf16[2,128,1280]{2,1,0:T(8,128)(2,1)S(1)}, bf16[2,128,1280]{2,1,0:T(8,128)(2,1)}, u32[]{:S(2)}) copy-start(bf16[2,128,1280]{2,1,0:T(8,128)(2,1)} %param.24) | copy-start | bytes 1966084
  7.2 330.3 %all-gather.13.cloned.1.call-start = ((), (), s32[]{:S(2)}) async-start(), calls=%async_computation.6 | async-start | bytes 15851520 | tf_op jit(solution)/shard_map/all_gather | solution.py:190
  7.9 641.2 %all-gather.15.cloned.1.call-start = ((), (), s32[]{:S(2)}) async-start(), calls=%async_computation.7 | async-start | bytes 5283840 | tf_op jit(solution)/shard_map/all_gather | solution.py:193
  8.7 977.5 %all-gather.17.cloned.1.call-start = ((), (), s32[]{:S(2)}) async-start(), calls=%async_computation.8 | async-start | bytes 21135360 | tf_op jit(solution)/shard_map/all_gather | solution.py:232
  9.4 1106.8 %all-gather.9.cloned.1.call-start = ((), (), s32[]{:S(2)}) async-start(), calls=%async_computation.2 | async-start | bytes 11796480 | tf_op jit(solution)/shard_map/all_gather | solution.py:223
  87.6 265.6 %copy-start.13 = (f32[2,128]{1,0:T(2,128)}, f32[2,128]{1,0:T(2,128)S(1)}, u32[]{:S(2)}) copy-start(f32[2,128]{1,0:T(2,128)S(1)} %fusion.58) | copy-start | bytes 3076
  361.3 0.9 copy-start.16
  361.3 1075.4 %all-gather.11.cloned.1.call-start = ((), (), s32[]{:S(2)}) async-start(), calls=%async_computation.3 | async-start | bytes 13209600 | tf_op jit(solution)/shard_map/all_gather | solution.py:234
  361.9 1316.6 %reduce-scatter.3.cloned.1.call-start = ((), (), s32[]{:S(2)}) async-start(), calls=%async_computation.4 | async-start | bytes 11796480 | tf_op jit(solution)/shard_map/reduce_scatter | solution.py:324
  1134.2 1.1 copy-start.1
  1134.4 4.0 copy-start.4
  1446.6 8.7 copy-start.9
  1455.3 1.1 copy-start.12
  1456.4 2.2 copy-start.3
  1457.1 0.8 copy-start.6
  1471.1 1.1 copy-start.11
  1490.8 565.7 %all-reduce.26.cloned.1.call-start = ((), (), s32[]{:S(2)}) async-start(), calls=%async_computation.9 | async-start | bytes 104857600
  1490.8 2.4 copy-start.5
  1491.8 1.4 copy-start.7
  1493.2 3.7 copy-start.10
  1497.0 181.6 %copy-start.2 = (bf16[2,128,1280]{2,1,0:T(8,128)(2,1)S(1)}, bf16[2,128,1280]{2,1,0:T(8,128)(2,1)}, u32[]{:S(2)}) copy-start(bf16[2,128,1280]{2,1,0:T(8,128)(2,1)} %param.24) | copy-start | bytes 1966084
  1688.1 1074.9 %reduce-scatter.5.cloned.1.call-start = ((), (), s32[]{:S(2)}) async-start(), calls=%async_computation.5 | async-start | bytes 26419200 | tf_op jit(solution)/shard_map/reduce_scatter | solution.py:273
  1705.7 0.7 copy-start.15
  1706.5 12.3 copy-start.8
  1718.8 7.1 copy-start.14
Sparse Core Ops, SparseCore 0:
  9.7 327.7 all-gather.12
  339.2 309.8 all-gather.14
  650.8 335.2 all-gather.16
  988.9 127.2 all-gather.8
  1117.7 318.9 all-gather.10
  1490.9 187.5 reduce-scatter.2
  1688.2 368.2 all-reduce.25
  2059.6 703.3 reduce-scatter.4
where the time goes:
time: 2780 us; the launch traced here: 2770 us
  waiting for transfers between devices  2390 us (86%)
  blocking collectives  135 us (5%)
  local copies, waits for them, and re-layouts  109 us (4%)
  matrix products  107 us (4%)
    reduce_scatter x1, waiting for transfers between devices, per_device(): lax.psum_scatter(out_weight_grad, ('dp', 'ctx'), scatter_dimension=0, til...  701 us
    all_gather x1, waiting for transfers between devices, per_device(): lax.all_gather(w_fc, ('dp', 'ctx'), axis=0, tiled=True)  330 us
    all_gather x1, waiting for transfers between devices, per_device(): lax.all_gather(w_out, ('dp', 'ctx'), axis=0, tiled=True)  288 us
    all_gather x1, waiting for transfers between devices, per_device(): lax.all_gather(w_proj, ('dp', 'ctx'), axis=0, tiled=True)  286 us
    unnamed x9, waiting for transfers between devices  260 us
    all_gather x1, waiting for transfers between devices, per_device(): lax.all_gather(w_qkv, ('dp', 'ctx'), axis=0, tiled=True)  250 us
    reduce_scatter x1, waiting for transfers between devices, per_device(): lax.psum_scatter(back_state[1].astype(jnp.bfloat16), 'ctx', scatter_dimen...  171 us
    unnamed x2, blocking collectives  135 us
  transfers between devices with their start and end apart: 8, of which 8 were waited for; matrix products, arithmetic and copies ran while one was open for 6% of the time, Pallas kernels for 0%

commit v1 on v0

v1 whole, which is shorter than its diff:
```python
import functools
import math

import jax
import jax.numpy as jnp
from jax import lax
from jax.experimental import pallas as pl
from jax.experimental.pallas import tpu as pltpu
from jax.sharding import Mesh
from jax.sharding import PartitionSpec as P

HEADS = 20
NORM_EPS = 1e-05
MASKED = -1000000000.0

F32 = jnp.float32
BF16 = jnp.bfloat16

AXES = ("x", "yl", "c", "z", "yh")
SIZES = (4, 2, 2, 4, 2)
DP = ("x", "yl", "c")
CTX = ("z", "yh")
PLACE = ("z", "yh", "yl", "x", "c")

D = 1280
SPAN = 128
SEQ_GRP = 2
ROWS = SEQ_GRP * SPAN
CTX_N = 8
LEN = CTX_N * SPAN
HEAD_DIM = D // HEADS
GROUP_HEADS = 5
GROUP_W = GROUP_HEADS * HEAD_DIM
COLS = 640
BLK = 80
SCALE = 1.0 / math.sqrt(HEAD_DIM)
Q_BLOCK = 256
MB = 1 << 20


def place_of(dp):
    x, yl, c = dp // 4, (dp // 2) % 2, dp % 2
    return (yl * 4 + x) * 2 + c


def dot(left, right):
    return lax.dot_general(
        left, right, (((1,), (0,)), ((), ())), preferred_element_type=F32
    )


def dot_nt(left, right):
    return lax.dot_general(
        left, right, (((1,), (1,)), ((), ())), preferred_element_type=F32
    )


def norm_stats(rows):
    centre = jnp.mean(rows, axis=-1, keepdims=True)
    centred = rows - centre
    spread = jnp.mean(centred * centred, axis=-1, keepdims=True)
    scale = lax.rsqrt(spread + NORM_EPS)
    return centred * scale, scale


def norm_back(normed, scale, gain, grad):
    scaled = gain * grad
    mean_one = jnp.mean(scaled, axis=-1, keepdims=True)
    mean_two = jnp.mean(scaled * normed, axis=-1, keepdims=True)
    return (scaled - mean_one - normed * mean_two) * scale


def stack_rows(ref, *lead):
    return jnp.concatenate([ref[(*lead, place_of(dp))] for dp in range(16)], axis=0)


def params(vmem_mb):
    return pltpu.CompilerParams(vmem_limit_bytes=vmem_mb * MB)


def cost(flops, nbytes, trans=0):
    return pl.CostEstimate(flops=flops, bytes_accessed=nbytes, transcendentals=trans)


def whole(shape):
    return pl.BlockSpec(shape, lambda *i: (0,) * len(shape))


def qkv_kernel(tok_ref, gain_ref, shift_ref, bias_ref, w_ref, n1_ref, out_ref):
    @pl.when(pl.program_id(0) == 0)
    def _():
        normed, _ = norm_stats(tok_ref[...].astype(F32))
        n1_ref[...] = (normed * gain_ref[...] + shift_ref[...]).astype(BF16)

    rows = dot(n1_ref[...], stack_rows(w_ref, 0)) + bias_ref[...]
    turned = rows.T.astype(BF16)
    for group in range(2):
        for seq in range(SEQ_GRP):
            out_ref[seq, group, 0] = turned[
                group * GROUP_W : (group + 1) * GROUP_W, seq * SPAN : (seq + 1) * SPAN
            ]


def qkv_call(tok, gain, shift, bias, w_attn):
    return pl.pallas_call(
        qkv_kernel,
        grid=(6,),
        in_specs=[
            whole((ROWS, D)),
            whole((1, D)),
            whole((1, D)),
            pl.BlockSpec((1, COLS), lambda i: (0, i)),
            pl.BlockSpec((1, 16, BLK, COLS), lambda i: (i, 0, 0, 0)),
        ],
        out_specs=[
            whole((ROWS, D)),
            pl.BlockSpec(
                (SEQ_GRP, 2, 1, GROUP_W, SPAN), lambda i: (0, i % 2, i // 2, 0, 0)
            ),
        ],
        out_shape=[
            jax.ShapeDtypeStruct((ROWS, D), BF16),
            jax.ShapeDtypeStruct((SEQ_GRP, 4, 3, GROUP_W, SPAN), BF16),
        ],
        compiler_params=params(32),
        cost_estimate=cost(2 * ROWS * D * 3 * D, 12 * MB),
        name="qkv",
    )(tok, gain, shift, bias, w_attn)


def lanes(ref, which):
    return jnp.concatenate([ref[p, which] for p in range(CTX_N)], axis=1)


def turn(block):
    return block.astype(F32).T.astype(BF16)


def allowed_of(length, first_query, key_count, query_count):
    key_pos = lax.broadcasted_iota(jnp.int32, (key_count, query_count), 0)
    query_pos = first_query + lax.broadcasted_iota(
        jnp.int32, (key_count, query_count), 1
    )
    return (key_pos <= query_pos) & (key_pos < length)


def attend_kernel(len_ref, qkv_ref, out_ref, lse_ref):
    length = len_ref[0]
    query = lanes(qkv_ref, 0)
    key = turn(lanes(qkv_ref, 1))
    value = lanes(qkv_ref, 2)
    for block in range(LEN // Q_BLOCK):
        first = block * Q_BLOCK
        last = first + Q_BLOCK
        scores = dot(key[:last], query[:, first:last]) * SCALE
        scores = jnp.where(allowed_of(length, first, last, Q_BLOCK), scores, MASKED)
        top = jnp.max(scores, axis=0, keepdims=True)
        weights = jnp.exp(scores - top)
        total = jnp.sum(weights, axis=0, keepdims=True)
        result = dot(value[:, :last], weights.astype(BF16)) / total
        lse_ref[0, :, first:last] = top + jnp.log(total)
        result = result.astype(BF16)
        for part in range(Q_BLOCK // SPAN):
            out_ref[first // SPAN + part] = result[:, part * SPAN : (part + 1) * SPAN]


def attend_call(length, qkv):
    return pl.pallas_call(
        attend_kernel,
        grid=(GROUP_HEADS,),
        in_specs=[
            pl.BlockSpec(memory_space=pltpu.SMEM),
            pl.BlockSpec((CTX_N, 3, HEAD_DIM, SPAN), lambda h: (0, 0, h, 0)),
        ],
        out_specs=[
            pl.BlockSpec((CTX_N, HEAD_DIM, SPAN), lambda h: (0, h, 0)),
            pl.BlockSpec((1, 1, LEN), lambda h: (h, 0, 0)),
        ],
        out_shape=[
            jax.ShapeDtypeStruct((CTX_N, GROUP_W, SPAN), BF16),
            jax.ShapeDtypeStruct((GROUP_HEADS, 1, LEN), F32),
        ],
        compiler_params=params(40),
        cost_estimate=cost(6 * LEN * LEN * 4 * HEAD_DIM, 3 * MB, 3 * LEN * LEN),
        name="attend",
    )(length, qkv)


def attend_back_kernel(len_ref, qkv_ref, grad_ref, lse_ref, out_ref, gk_ref, gv_ref):
    length = len_ref[0]
    query = lanes(qkv_ref, 0)
    key_t = lanes(qkv_ref, 1)
    key = turn(key_t)
    value = turn(lanes(qkv_ref, 2))
    grad = jnp.concatenate([grad_ref[p] for p in range(CTX_N)], axis=1)
    gk_ref[...] = jnp.zeros_like(gk_ref)
    gv_ref[...] = jnp.zeros_like(gv_ref)
    for block in range(LEN // Q_BLOCK):
        first = block * Q_BLOCK
        last = first + Q_BLOCK
        query_b = query[:, first:last]
        grad_b = grad[:, first:last]
        scores = dot(key[:last], query_b) * SCALE
        probs = jnp.where(
            allowed_of(length, first, last, Q_BLOCK),
            jnp.exp(scores - lse_ref[0, :, first:last]),
            0.0,
        )
        grad_probs = dot(value[:last], grad_b)
        delta = jnp.sum(probs * grad_probs, axis=0, keepdims=True)
        grad_scores = (probs * (grad_probs - delta)).astype(BF16)
        grad_query = (dot(key_t[:, :last], grad_scores) * SCALE).astype(BF16)
        for part in range(Q_BLOCK // SPAN):
            out_ref[first // SPAN + part, 0] = grad_query[
                :, part * SPAN : (part + 1) * SPAN
            ]
        gk_ref[:, :last] += dot_nt(query_b, grad_scores)
        gv_ref[:, :last] += dot_nt(grad_b, probs.astype(BF16))
    for part in range(CTX_N):
        cut = slice(part * SPAN, (part + 1) * SPAN)
        out_ref[part, 1] = (gk_ref[:, cut] * SCALE).astype(BF16)
        out_ref[part, 2] = gv_ref[:, cut].astype(BF16)


def attend_back_call(length, qkv, grad, lse):
    return pl.pallas_call(
        attend_back_kernel,
        grid=(GROUP_HEADS,),
        in_specs=[
            pl.BlockSpec(memory_space=pltpu.SMEM),
            pl.BlockSpec((CTX_N, 3, HEAD_DIM, SPAN), lambda h: (0, 0, h, 0)),
            pl.BlockSpec((CTX_N, HEAD_DIM, SPAN), lambda h: (0, h, 0)),
            pl.BlockSpec((1, 1, LEN), lambda h: (h, 0, 0)),
        ],
        out_specs=pl.BlockSpec((CTX_N, 3, HEAD_DIM, SPAN), lambda h: (0, 0, h, 0)),
        out_shape=jax.ShapeDtypeStruct((CTX_N, 3, GROUP_W, SPAN), BF16),
        scratch_shapes=[pltpu.VMEM((HEAD_DIM, LEN), F32)] * 2,
        compiler_params=params(48),
        cost_estimate=cost(15 * LEN * LEN * 4 * HEAD_DIM, 5 * MB, 3 * LEN * LEN),
        name="attend_back",
    )(length, qkv, grad, lse)


def mlp_kernel(
    info_ref,
    tok_ref,
    cot_ref,
    att_ref,
    vec_ref,
    fc_bias_ref,
    wp_ref,
    wf_ref,
    wo_ref,
    out_ref,
    g_res_ref,
    g_att_ref,
    d_vec_ref,
    d_fc_bias_ref,
    d_wp_ref,
    d_wf_ref,
    d_wo_ref,
    res_ref,
    n2_ref,
    n2t_ref,
    g_out_ref,
    acc_ref,
    gn_ref,
):
    step = pl.program_id(0)
    proj_shift, gain, shift, out_shift = (vec_ref[k : k + 1] for k in range(4))

    @pl.when(step == 0)
    def _():
        att = jnp.concatenate([turn(att_ref[s]) for s in range(SEQ_GRP)], axis=0)
        for half in range(2):
            cut = slice(half * COLS, (half + 1) * COLS)
            res_ref[:, cut] = (
                tok_ref[:, cut].astype(F32)
                + dot(att, stack_rows(wp_ref, half))
                + proj_shift[:, cut]
            )
        residual = res_ref[...]
        normed, _ = norm_stats(residual)
        normed = normed * gain + shift
        n2_ref[...] = normed.astype(BF16)
        n2t_ref[...] = normed.T.astype(BF16)
        for seq in range(SEQ_GRP):
            cut = slice(seq * SPAN, (seq + 1) * SPAN)
            pos = info_ref[SEQ_GRP] + lax.broadcasted_iota(jnp.int32, (SPAN, D), 0)
            g_out_ref[cut] = jnp.where(
                pos < info_ref[seq], cot_ref[cut], jnp.zeros((SPAN, D), BF16)
            )
        acc_ref[...] = residual + out_shift
        gn_ref[...] = jnp.zeros_like(gn_ref)

    w_fc = stack_rows(wf_ref, 0)
    pre = dot(n2_ref[...], w_fc) + fc_bias_ref[...]
    root = math.sqrt(2.0 / math.pi)
    square = pre * pre
    bend = jnp.tanh(root * pre * (1.0 + 0.044715 * square))
    gate = 0.5 * (1.0 + bend)
    slope = gate + 0.5 * pre * (1.0 - bend * bend) * root * (
        1.0 + 3.0 * 0.044715 * square
    )
    act_f = pre * gate
    act = act_f.astype(BF16)
    act_t = act_f.T.astype(BF16)
    g_act = None
    for half in range(2):
        cut = slice(half * COLS, (half + 1) * COLS)
        w_out = jnp.concatenate(
            [wo_ref[z, half, 0, 0, c] for c in range(2) for z in range(4)], axis=0
        )
        acc_ref[:, cut] += dot(act, w_out)
        part = dot_nt(g_out_ref[:, cut], w_out)
        g_act = part if g_act is None else g_act + part
        d_w = dot(act_t, g_out_ref[:, cut]).astype(BF16)
        for c in range(2):
            for z in range(4):
                row = (c * 4 + z) * BLK
                d_wo_ref[c, z, half, 0, 0] = d_w[row : row + BLK]
    g_pre_f = g_act * slope
    g_pre = g_pre_f.astype(BF16)
    d_fc_bias_ref[...] = jnp.sum(g_pre.astype(F32), axis=0, keepdims=True)
    gn_ref[...] += dot_nt(g_pre, w_fc)
    d_w = dot(n2t_ref[...], g_pre).astype(BF16)
    for dp in range(16):
        d_wf_ref[dp % 2, 0, place_of(dp) // 2] = d_w[dp * BLK : (dp + 1) * BLK]

    @pl.when(step == pl.num_programs(0) - 1)
    def _():
        out_ref[...] = acc_ref[...].astype(BF16)
        normed, scale = norm_stats(res_ref[...])
        g_norm = gn_ref[...]
        g_out = g_out_ref[...].astype(F32)
        g_res = (g_out + norm_back(normed, scale, gain, g_norm)).astype(BF16)
        g_res_ref[...] = g_res
        d_vec_ref[0:1] = jnp.sum(g_res.astype(F32), axis=0, keepdims=True)
        d_vec_ref[1:2] = jnp.sum(g_norm * normed, axis=0, keepdims=True)
        d_vec_ref[2:3] = jnp.sum(g_norm, axis=0, keepdims=True)
        d_vec_ref[3:4] = jnp.sum(g_out, axis=0, keepdims=True)
        g_att = None
        for half in range(2):
            cut = slice(half * COLS, (half + 1) * COLS)
            part = dot_nt(g_res[:, cut], stack_rows(wp_ref, half))
            g_att = part if g_att is None else g_att + part
            d_w = None
            for seq in range(SEQ_GRP):
                part = dot(
                    att_ref[seq], g_res_ref[seq * SPAN : (seq + 1) * SPAN, cut]
                )
                d_w = part if d_w is None else d_w + part
            d_w = d_w.astype(BF16)
            for dp in range(16):
                d_wp_ref[dp % 2, half, place_of(dp) // 2] = d_w[
                    dp * BLK : (dp + 1) * BLK
                ]
        for seq in range(SEQ_GRP):
            g_att_ref[seq] = g_att[seq * SPAN : (seq + 1) * SPAN].T.astype(BF16)


def mlp_call(info, tok, cot, att, vecs, fc_bias, w_attn, w_mlp):
    w_mlp_parts = w_mlp.reshape(4, 2, 2, 4, 2, 2 * BLK, COLS)
    return pl.pallas_call(
        mlp_kernel,
        grid=(8,),
        in_specs=[
            pl.BlockSpec(memory_space=pltpu.SMEM),
            whole((ROWS, D)),
            whole((ROWS, D)),
            whole((SEQ_GRP, D, SPAN)),
            whole((4, D)),
            pl.BlockSpec((1, COLS), lambda j: (0, j)),
            pl.BlockSpec((2, 16, BLK, COLS), lambda j: (3, 0, 0, 0)),
            pl.BlockSpec((1, 16, BLK, COLS), lambda j: (j, 0, 0, 0)),
            pl.BlockSpec(
                (4, 2, 1, 1, 2, BLK, COLS), lambda j: (0, 0, j % 2, j // 2, 0, 1, 0)
            ),
        ],
        out_specs=[
            whole((ROWS, D)),
            whole((ROWS, D)),
            whole((SEQ_GRP, D, SPAN)),
            whole((4, D)),
            pl.BlockSpec((1, COLS), lambda j: (0, j)),
            whole((2, 2, 8, BLK, COLS)),
            pl.BlockSpec((2, 1, 8, BLK, COLS), lambda j: (0, j, 0, 0, 0)),
            pl.BlockSpec(
                (2, 4, 2, 1, 1, BLK, COLS), lambda j: (0, 0, 0, j % 2, j // 2, 0, 0)
            ),
        ],
        out_shape=[
            jax.ShapeDtypeStruct((ROWS, D), BF16),
            jax.ShapeDtypeStruct((ROWS, D), BF16),
            jax.ShapeDtypeStruct((SEQ_GRP, D, SPAN), BF16),
            jax.ShapeDtypeStruct((4, D), F32),
            jax.ShapeDtypeStruct((1, 4 * D), F32),
            jax.ShapeDtypeStruct((2, 2, 8, BLK, COLS), BF16),
            jax.ShapeDtypeStruct((2, 8, 8, BLK, COLS), BF16),
            jax.ShapeDtypeStruct((2, 4, 2, 2, 4, BLK, COLS), BF16),
        ],
        scratch_shapes=[
            pltpu.VMEM((ROWS, D), F32),
            pltpu.VMEM((ROWS, D), BF16),
            pltpu.VMEM((D, ROWS), BF16),
            pltpu.VMEM((ROWS, D), BF16),
            pltpu.VMEM((ROWS, D), F32),
            pltpu.VMEM((ROWS, D), F32),
        ],
        compiler_params=params(56),
        cost_estimate=cost(2 * ROWS * D * (24 * D + 3 * D), 62 * MB, 2 * ROWS * 4 * D),
        name="mlp",
    )(info, tok, cot, att, vecs, fc_bias, w_attn, w_mlp, w_mlp_parts)


def qkv_back_kernel(
    tok_ref,
    n1_ref,
    gain_ref,
    g_res_ref,
    g_ref,
    w_ref,
    in_grad_ref,
    d_bias_ref,
    d_norm_ref,
    d_w_ref,
    n1t_ref,
    gn_ref,
):
    step = pl.program_id(0)

    @pl.when(step == 0)
    def _():
        n1t_ref[...] = turn(n1_ref[...])
        gn_ref[...] = jnp.zeros_like(gn_ref)

    turned = jnp.concatenate(
        [
            jnp.concatenate([g_ref[s, group, 0] for s in range(SEQ_GRP)], axis=1)
            for group in range(2)
        ],
        axis=0,
    )
    rows_f = turned.astype(F32).T
    rows = rows_f.astype(BF16)
    d_bias_ref[...] = jnp.sum(rows_f, axis=0, keepdims=True)
    gn_ref[...] += dot_nt(rows, stack_rows(w_ref, 0))
    d_w = dot(n1t_ref[...], rows).astype(BF16)
    for dp in range(16):
        d_w_ref[dp % 2, 0, place_of(dp) // 2] = d_w[dp * BLK : (dp + 1) * BLK]

    @pl.when(step == pl.num_programs(0) - 1)
    def _():
        normed, scale = norm_stats(tok_ref[...].astype(F32))
        g_norm = gn_ref[...]
        in_grad_ref[...] = g_res_ref[...].astype(F32) + norm_back(
            normed, scale, gain_ref[...], g_norm
        )
        d_norm_ref[0:1] = jnp.sum(g_norm * normed, axis=0, keepdims=True)
        d_norm_ref[1:2] = jnp.sum(g_norm, axis=0, keepdims=True)


def qkv_back_call(tok, n1, gain, g_res, g_qkv, w_attn):
    return pl.pallas_call(
        qkv_back_kernel,
        grid=(6,),
        in_specs=[
            whole((ROWS, D)),
            whole((ROWS, D)),
            whole((1, D)),
            whole((ROWS, D)),
            pl.BlockSpec(
                (SEQ_GRP, 2, 1, GROUP_W, SPAN), lambda i: (0, i % 2, i // 2, 0, 0)
            ),
            pl.BlockSpec((1, 16, BLK, COLS), lambda i: (i, 0, 0, 0)),
        ],
        out_specs=[
            whole((ROWS, D)),
            pl.BlockSpec((1, COLS), lambda i: (0, i)),
            whole((2, D)),
            pl.BlockSpec((2, 1, 8, BLK, COLS), lambda i: (0, i, 0, 0, 0)),
        ],
        out_shape=[
            jax.ShapeDtypeStruct((ROWS, D), F32),
            jax.ShapeDtypeStruct((1, 3 * D), F32),
            jax.ShapeDtypeStruct((2, D), F32),
            jax.ShapeDtypeStruct((2, 6, 8, BLK, COLS), BF16),
        ],
        scratch_shapes=[
            pltpu.VMEM((D, ROWS), BF16),
            pltpu.VMEM((ROWS, D), F32),
        ],
        compiler_params=params(48),
        cost_estimate=cost(4 * ROWS * D * 3 * D, 24 * MB),
        name="qkv_back",
    )(tok, n1, gain, g_res, g_qkv, w_attn)


def ring_perm(axis):
    pairs = []
    for core in range(2):
        for pos in range(4):
            to = (pos + (1 if core == 0 else -1)) % 4
            if axis == "x":
                index = lambda p: p * 2 + core
            elif axis == "z":
                index = lambda p: core * 4 + p
            else:
                index = lambda p: ((p % 2) * 2 + core) * 2 + p // 2
            pairs.append((index(pos), index(to)))
    return {"x": ("x", "c"), "z": ("c", "z"), "y": ("yl", "c", "yh")}[axis], pairs


def swap_cores(array):
    return lax.ppermute(array, "c", [(0, 1), (1, 0)])


def reduce_scatter(grads, orders):
    core = lax.axis_index("c")
    way = 1 - 2 * core
    place = {
        "x": lax.axis_index("x"),
        "y": 2 * lax.axis_index("yh") + lax.axis_index("yl"),
        "z": lax.axis_index("z"),
    }
    dims = {"z": 0, "y": 1, "x": 2}
    theirs = [lax.dynamic_index_in_dim(g, 1 - core, 0, False) for g in grads]
    mine = [lax.dynamic_index_in_dim(g, core, 0, False) for g in grads]
    terms = [[m, swap_cores(t)] for m, t in zip(mine, theirs)]

    def local(colour, axis, block):
        total = None
        for term in terms[colour]:
            part = lax.dynamic_slice_in_dim(term, block, 1, dims[axis]).astype(F32)
            total = part if total is None else total + part
        return total

    for phase in range(3):
        axes = [order[phase] for order in orders]
        sent = [
            local(k, a, (place[a] - way) % 4).astype(BF16) for k, a in enumerate(axes)
        ]
        for step in range(3):
            for k, a in enumerate(axes):
                names, pairs = ring_perm(a)
                sent[k] = lax.ppermute(sent[k], names, pairs)
            for k, a in enumerate(axes):
                total = sent[k].astype(F32) + local(k, a, (place[a] - way * (2 + step)) % 4)
                sent[k] = total if phase == 2 and step == 2 else total.astype(BF16)
        terms = [[s] for s in sent]
    return [s.reshape(s.shape[-2:]) for s in sent]


def per_device(
    tokens,
    lengths,
    cotangent,
    ln1_gain,
    ln1_bias,
    w_qkv,
    q_bias,
    v_bias,
    w_proj,
    proj_bias,
    ln2_gain,
    ln2_bias,
    w_fc,
    fc_bias,
    w_out,
    out_bias,
):
    ctx_rank = lax.axis_index(CTX)
    tok = tokens.reshape(ROWS, D)
    cot = cotangent.reshape(ROWS, D)

    w_cols = jnp.stack([jnp.concatenate([w_qkv, w_proj], axis=1), w_fc], axis=0)
    w_cols = w_cols.reshape(2, 10, CTX_N, COLS).transpose(2, 0, 1, 3)
    w_cols = lax.all_to_all(w_cols, CTX, 0, 0, tiled=True)
    w_cols = w_cols.transpose(1, 0, 2, 3).reshape(2, BLK, COLS)
    w_rows = w_out.reshape(40, 2, COLS).transpose(1, 0, 2)
    w_rows = lax.all_to_all(w_rows, "yh", 0, 0, tiled=True).reshape(BLK, COLS)

    small = jnp.concatenate(
        [ln1_gain, ln1_bias, q_bias, v_bias, proj_bias, ln2_gain, ln2_bias, out_bias, fc_bias]
    )
    small = jnp.pad(small[None], ((0, 7), (0, COLS - 120)))
    attn_part = jnp.concatenate([w_cols[0], small], axis=0)
    mlp_part = jnp.concatenate([w_cols[1], w_rows], axis=0)
    w_attn = lax.all_gather(attn_part, PLACE, axis=0, tiled=False)
    mlp_part, w_attn = lax.optimization_barrier((mlp_part, w_attn))
    w_mlp = lax.all_gather(mlp_part, PLACE, axis=0, tiled=False)
    vecs = w_attn[:, BLK, :120].reshape(4, 2, 2, 4, 2, 120)
    vecs = vecs.transpose(3, 2, 4, 0, 1, 5).reshape(128, 120).astype(F32)
    fc_shift = vecs[:, 80:].reshape(1, 4 * D)
    vecs = vecs[:, :80].reshape(128, 8, 10).transpose(1, 0, 2).reshape(8, D)
    w_attn = w_attn.reshape(CTX_N, 16, BLK + 8, COLS)
    w_mlp = w_mlp.reshape(CTX_N, 16, 2 * BLK, COLS)

    qkv_bias = jnp.concatenate([vecs[2:3], jnp.zeros((1, D), F32), vecs[3:4]], axis=1)
    n1, qkv = qkv_call(tok, vecs[0:1], vecs[1:2], qkv_bias, w_attn)

    def exchange(array):
        return lax.all_to_all(array, CTX, 0, 0, tiled=True)

    length = lax.dynamic_slice_in_dim(lengths, ctx_rank // 4, 1)
    qkv = exchange(qkv.reshape(CTX_N, 3, GROUP_W, SPAN))
    att, lse = attend_call(length, qkv)
    att = exchange(att).reshape(SEQ_GRP, D, SPAN)

    info = jnp.concatenate([lengths, (ctx_rank * SPAN).astype(jnp.int32)[None]])
    layer_out, g_res, g_att, d_vecs, d_fc_bias, d_wp, d_wf, d_wo = mlp_call(
        info, tok, cot, att, vecs[4:8], fc_shift, w_attn, w_mlp
    )
    mlp_sums = reduce_scatter(
        [d_wf.reshape(2, 4, 4, 4, BLK, COLS), d_wo.reshape(2, 4, 4, 4, BLK, COLS)],
        ["xyz", "yzx"],
    )

    g_att = exchange(g_att.reshape(CTX_N, GROUP_W, SPAN))
    g_qkv = attend_back_call(length, qkv, g_att, lse)
    g_qkv = exchange(g_qkv).reshape(SEQ_GRP, 4, 3, GROUP_W, SPAN)
    input_grad, d_qkv_bias, d_norm, d_wqkv = qkv_back_call(
        tok, n1, vecs[0:1], g_res, g_qkv, w_attn
    )

    d_small = jnp.concatenate(
        [d_norm, d_qkv_bias[:, :D], d_qkv_bias[:, 2 * D :], d_vecs], axis=0
    )
    d_small = d_small.reshape(8, 128, 10).transpose(1, 0, 2).reshape(128, 80)
    d_small = jnp.concatenate([d_small, d_fc_bias.reshape(128, 40)], axis=1)
    d_small = d_small.reshape(4, 2, 2, 4, 2, 120).transpose(2, 3, 4, 1, 0, 5)
    d_small = jnp.pad(
        d_small.reshape(2, CTX_N, 8, 1, 120).astype(BF16),
        ((0, 0), (0, 0), (0, 0), (0, 7), (0, COLS - 120)),
    )
    d_attn = jnp.concatenate([d_wqkv, d_wp], axis=1)
    d_attn = jnp.concatenate([d_attn, d_small], axis=3)
    d_attn = d_attn.reshape(2, 4, 4, 4, BLK + 8, COLS)
    attn_sums = reduce_scatter(
        [d_attn[..., 0:32, :], d_attn[..., 32:64, :], d_attn[..., 64:88, :]],
        ["xyz", "yzx", "zxy"],
    )
    attn_sum = jnp.concatenate(attn_sums, axis=0)

    back = jnp.stack([attn_sum[:BLK], mlp_sums[0]], axis=0).astype(BF16)
    back = back.reshape(2, CTX_N, 10, COLS).transpose(1, 0, 2, 3)
    back = lax.all_to_all(back, CTX, 0, 0, tiled=True)
    back = back.transpose(1, 2, 0, 3).reshape(2, 10, CTX_N * COLS).astype(F32)
    d_w_out = mlp_sums[1].astype(BF16).reshape(2, 40, COLS)
    d_w_out = lax.all_to_all(d_w_out, "yh", 0, 0, tiled=True)
    d_w_out = d_w_out.transpose(1, 0, 2).reshape(40, D).astype(F32)
    small_sum = attn_sum[BLK, :120]
    names = ["g1", "b1", "q", "v", "proj", "g2", "b2", "out"]
    vec = {n: small_sum[10 * k : 10 * (k + 1)] for k, n in enumerate(names)}

    return (
        layer_out.reshape(tokens.shape),
        input_grad.reshape(tokens.shape),
        vec["g1"],
        vec["b1"],
        back[0, :, : 3 * D],
        vec["q"],
        vec["v"],
        back[0, :, 3 * D :],
        vec["proj"],
        vec["g2"],
        vec["b2"],
        back[1],
        small_sum[80:120],
        d_w_out,
        vec["out"],
    )


def solution(mesh):
    fine = Mesh(mesh.devices.reshape(SIZES), AXES)
    rows = P(DP, CTX, None)
    mat = P(AXES, None)
    vec = P(AXES)
    in_specs = (
        rows,
        P(DP),
        rows,
        vec,
        vec,
        mat,
        vec,
        vec,
        mat,
        vec,
        vec,
        vec,
        mat,
        vec,
        mat,
        vec,
    )
    out_specs = (
        rows,
        rows,
        vec,
        vec,
        mat,
        vec,
        vec,
        mat,
        vec,
        vec,
        vec,
        mat,
        vec,
        mat,
        vec,
    )
    return jax.shard_map(
        per_device, mesh=fine, in_specs=in_specs, out_specs=out_specs, check_vma=False
    )
```

time: 2780 us -> 637 us (0.23)
  waiting for transfers between devices: 2390 us -> 353 us
  blocking collectives: 135 us -> 19.8 us
  matrix products: 107 us -> 0 us
  Pallas kernels: 0 us -> 88.5 us
  local copies, waits for them, and re-layouts: 109 us -> 53.6 us
  other arithmetic: 12.4 us -> 57.3 us
  starting transfers between devices: 0.89 us -> 42.8 us
    all_gather x5 -> x2, waiting for transfers between devices: 1260 us -> 106 us  [the longest x1 63.3 us: per_device(): w_attn = lax.all_gather(attn_part, PLACE, axis=0, tiled=False)]
    reduce_scatter x2 -> x0, waiting for transfers between devices: 872 us -> none  [the longest x1 701 us: per_device(): lax.psum_scatter(out_weight_grad, ('dp', 'ctx'), scatter_dimension=0, til...]
    unnamed x9 -> x2, waiting for transfers between devices: 260 us -> 0.03 us
    ppermute x0 -> x50, waiting for transfers between devices: none -> 156 us  [the longest x45 156 us: reduce_scatter(): sent[k] = lax.ppermute(sent[k], names, pairs)]
    unnamed x2 -> x0, blocking collectives: 135 us -> none
    dot_general x19 -> x0, matrix products: 107 us -> none  [the longest x4 41.2 us: weight_grad(): jnp.einsum('sck,scn->kn', left, grad_rows, preferred_element_type=jnp.flo...]
    all_to_all x0 -> x7, waiting for transfers between devices: none -> 90.5 us  [the longest x3 64.1 us: exchange(): return lax.all_to_all(array, CTX, 0, 0, tiled=True)]
    pallas_call x0 -> x5, Pallas kernels: none -> 88.5 us  [the longest x1 42.4 us: mlp_call(): pl.pallas_call(mlp_kernel, grid=(8,), in_specs=[pl.BlockSpec(memory_space...]
  transfers between devices with their start and end apart: 8 -> 59, of which waited for: 8 -> 41; matrix products, arithmetic and copies ran while one was open for 6% -> 12% of each run, Pallas kernels for 0% -> 3%
where the time goes in v1:
time: 637 us; the launch traced here: 630 us
  waiting for transfers between devices  353 us (55%)
  Pallas kernels  88.5 us (14%)
  other arithmetic  57.3 us (9%)
  local copies, waits for them, and re-layouts  53.6 us (8%)
  starting transfers between devices  42.8 us (7%)
  blocking collectives  19.8 us (3%)
  between operations  15.7 us (2%)
    ppermute x45, waiting for transfers between devices, reduce_scatter(): sent[k] = lax.ppermute(sent[k], names, pairs)  156 us
    all_to_all x3, waiting for transfers between devices, exchange(): return lax.all_to_all(array, CTX, 0, 0, tiled=True)  64.1 us
    all_gather x1, waiting for transfers between devices, per_device(): w_attn = lax.all_gather(attn_part, PLACE, axis=0, tiled=False)  63.3 us
    all_gather x1, waiting for transfers between devices, per_device(): w_mlp = lax.all_gather(mlp_part, PLACE, axis=0, tiled=False)  42.4 us
    pallas_call x1, Pallas kernels, mlp_call(): pl.pallas_call(mlp_kernel, grid=(8,), in_specs=[pl.BlockSpec(memory_space...  42.4 us
    convert_element_type x40, other arithmetic, reduce_scatter(): sent[k] = total if phase == 2 and step == 2 else total.astype(BF16)  33.7 us
    all_to_all x1, blocking collectives, exchange(): return lax.all_to_all(array, CTX, 0, 0, tiled=True)  19.8 us
    unnamed x58, local copies, waits for them, and re-layouts  19.1 us
  transfers between devices with their start and end apart: 59, of which 41 were waited for; matrix products, arithmetic and copies ran while one was open for 12% of the time, Pallas kernels for 3%

profile of v1, /device:TPU:0, one launch (start us, length us, event | category | flops | bytes accessed | tf_op | source)
XLA Modules:
  0.0 630.4 jit_solution(1131666270263767061)
XLA Ops:
  10.2 8.0 %all-to-all-start = ((bf16[8,2,10,640]{3,1,2,0:T(2,128)(2,1)}), bf16[8,2,10,640]{3,1,2,0:T(2,128)(2,1)S(1)}, u32[]{:S(2)}, u32[]{:S(2)}) async-start(bf16[8,2,10,640]{3,1,2,0:T(2,128)(2,1)} %copy.157), calls=%async_computation | async-start | bytes 409600 | tf_op jit(solution)/shard_map/all_to_all | solution.py:578
  18.5 8.3 %all-to-all-done = bf16[8,2,10,640]{3,1,2,0:T(2,128)(2,1)S(1)} async-done(((bf16[8,2,10,640]{3,1,2,0:T(2,128)(2,1)}), bf16[8,2,10,640]{3,1,2,0:T(2,128)(2,1)S(1)}, u32[]{:S(2)}, u32[]{:S(2)}) %all-to-all-start) | async-done | bytes 204832 | tf_op jit(solution)/shard_map/all_to_all | solution.py:578
  32.5 5.7 all-to-all-done.1
  38.9 63.3 %all-gather.5.cloned.1.call-done = bf16[11264,640]{1,0:T(8,128)(2,1)} async-done(((bf16[88,640]{1,0:T(8,128)(2,1)}), bf16[11264,640]{1,0:T(8,128)(2,1)}) %all-gather.5.cloned.1.call-update) | async-done | bytes 14417936 | tf_op jit(solution)/shard_map/all_gather | solution.py:589
  104.5 5.1 copy-done
  109.6 6.3 %qkv.1 = (bf16[256,1280]{1,0:T(8,128)(2,1)S(1)}, bf16[2,4,3,320,128]{4,3,2,1,0:T(8,128)(2,1)S(1)}) custom-call(bf16[256,1280]{1,0:T(8,128)(2,1)S(1)} %bitcast.214, f32[1,1280]{1,0:T(1,128)S(1)} %slice.148.gain_ref, f32[1,1280]{1,0:T(1,128)S(1)} %slice.150.shift_ref, f32[1,3840]{1,0:T(1,128)S(1)} %fusion.41.bias_ref, bf16[8,16,88,640]{3,2,1,0:T(8,128)(2,1)S(1)} %bitcast.210), custom_call_target="tpu_custom_call" | custom-call | flops 2516582400 | bytes 12582912 | tf_op jit(solution)/shard_map/qkv/pallas_call | solution.py:105
  117.3 6.6 %all-to-all-start.2 = ((bf16[8,3,320,128]{3,2,1,0:T(8,128)(2,1)}), bf16[8,3,320,128]{3,2,1,0:T(8,128)(2,1)S(1)}, u32[]{:S(2)}, u32[]{:S(2)}) async-start(bf16[8,3,320,128]{3,2,1,0:T(8,128)(2,1)} %bitcast.211), calls=%async_computation.2 | async-start | bytes 3932160 | tf_op jit(solution)/shard_map/all_to_all | solution.py:603
  124.4 27.3 %all-to-all-done.2.qkv_ref = bf16[8,3,320,128]{3,2,1,0:T(8,128)(2,1)S(1)} async-done(((bf16[8,3,320,128]{3,2,1,0:T(8,128)(2,1)}), bf16[8,3,320,128]{3,2,1,0:T(8,128)(2,1)S(1)}, u32[]{:S(2)}, u32[]{:S(2)}) %all-to-all-start.2) | async-done | bytes 1966112 | tf_op jit(solution)/shard_map/all_to_all | solution.py:603
  151.7 11.5 %attend.1 = (bf16[8,320,128]{2,1,0:T(8,128)(2,1)}, f32[5,1,1024]{2,1,0:T(1,128)S(1)}) custom-call(s32[1]{0:T(128)} %dynamic_slice.266.len_ref, bf16[8,3,320,128]{3,2,1,0:T(8,128)(2,1)S(1)} %all-to-all-done.2.qkv_ref), custom_call_target="tpu_custom_call" | custom-call | flops 1610612736 | bytes 3145728 | tf_op jit(solution)/shard_map/attend/pallas_call | solution.py:168
  170.2 10.6 %all-to-all-done.3 = bf16[8,320,128]{2,1,0:T(8,128)(2,1)} async-done(((bf16[8,320,128]{2,1,0:T(8,128)(2,1)}), bf16[8,320,128]{2,1,0:T(8,128)(2,1)}, u32[]{:S(2)}, u32[]{:S(2)}) %all-to-all-start.3) | async-done | bytes 655392 | tf_op jit(solution)/shard_map/all_to_all | solution.py:603
  180.7 42.4 %all-gather.7.cloned.1.call-done = bf16[20480,640]{1,0:T(8,128)(2,1)} async-done(((bf16[160,640]{1,0:T(8,128)(2,1)}), bf16[20480,640]{1,0:T(8,128)(2,1)}) %all-gather.7.cloned.1.call-update) | async-done | bytes 26214416 | tf_op jit(solution)/shard_map/all_gather | solution.py:591
  223.2 42.4 %mlp.1 = (bf16[256,1280]{1,0:T(8,128)(2,1)}, bf16[256,1280]{1,0:T(8,128)(2,1)}, bf16[2,1280,128]{2,1,0:T(8,128)(2,1)}, f32[4,1280]{1,0:T(4,128)}, f32[1,5120]{1,...) custom-call(s32[3]{0:T(128)} %pad_add_fusion.info_ref, ...), custom_call_target="tpu_custom_call" | custom-call | flops 22649241600 | bytes 65011712 | tf_op jit(solution)/shard_map/mlp/pallas_call | solution.py:364
  265.6 19.8 %all_to_all.40.grad_ref = bf16[8,320,128]{2,1,0:T(8,128)(2,1)S(1)} all-to-all(bf16[8,320,128]{2,1,0:T(8,128)(2,1)} %bitcast.236), channel_id=1, replica_groups=mesh['x'=4,'yl'=2,'c'=2,'z'=4,'yh'=2] {'z','yh'}, dimensions={0} | all-to-all | bytes 1310720 | tf_op jit(solution)/shard_map/all_to_all | solution.py:603
  285.4 14.5 %attend_back.1 = bf16[8,3,320,128]{3,2,1,0:T(8,128)(2,1)S(1)} custom-call(s32[1]{0:T(128)} %dynamic_slice.266.len_ref, bf16[8,3,320,128]{3,2,1,0:T(8,128)(2,1)S(1)} %all-to-all-done.2.qkv_ref, bf16[8,320,128]{2,1,0:T(8,128)(2,1)S(1)} %all_to_all.40.grad_ref, f32[5,1,1024]{2,1,0:T(1,128)S(1)} %get-tuple-element.41.lse_ref), custom_call_target="tpu_custom_call" | custom-call | flops 4026531840 | bytes 5242880 | tf_op jit(solution)/shard_map/attend_back/pallas_call | solution.py:226
  305.3 26.3 %all-to-all-done.5 = bf16[8,3,320,128]{3,2,1,0:T(8,128)(2,1)S(1)} async-done(((bf16[8,3,320,128]{3,2,1,0:T(8,128)(2,1)}), bf16[8,3,320,128]{3,2,1,0:T(8,128)(2,1)S(1)}, u32[]{:S(2)}, u32[]{:S(2)}) %all-to-all-start.5) | async-done | bytes 1966112 | tf_op jit(solution)/shard_map/all_to_all | solution.py:603
  332.6 13.8 %qkv_back.1 = (f32[256,1280]{1,0:T(8,128)}, f32[1,3840]{1,0:T(1,128)S(1)}, f32[2,1280]{1,0:T(2,128)S(1)}, bf16[2,6,8,80,640]{4,3,2,1,0:T(8,128)(2,1)}) custom-call(bf16[256,1280]{1,0:T(8,128)(2,1)S(1)} %bitcast.215, bf16[256,1280]{1,0:T(8,128)(2,1)S(1)} %get-tuple-element.38.n1_ref, f32[1,1280]{1,0:T(1,128)S(1)} %slice.148.gain_ref, ...), custom_call_target="tpu_custom_call" | custom-call | flops 5033164800 | bytes 25165824 | tf_op jit(solution)/shard_map/qkv_back/pallas_call | solution.py:464
  347.6 9.4 %fusion.1 = bf16[2,8,8,88,640]{4,3,2,1,0:T(8,128)(2,1)S(1)} fusion(bf16[2,8,8,1,120]{4,3,2,1,0:T(2,128)(2,1)S(1)} %copy.168, bf16[2,2,8,80,640]{4,3,2,1,0:T(8,128)(2,1)} %get-tuple-element.44, bf16[2,6,8,80,640]{4,3,2,1,0:T(8,128)(2,1)} %get-tuple-element.43), kind=kLoop, calls=%fused_computation.2 | loop fusion | flops 57671680 | bytes 27555840 | tf_op jit(solution)/shard_map/concatenate | solution.py:637
  364.9 6.2 copy_bitcast_fusion
  374.9 9.7 %fusion.43 = (bf16[2,4,4,4,32,640]{5,4,3,2,1,0:T(8,128)(2,1)}, bf16[2,4,4,4,32,640]{5,4,3,2,1,0:T(8,128)(2,1)}) fusion(bf16[2,4,4,4,88,640]{5,4,3,2,1,0:T(8,128)(2,1)} %bitcast.217), kind=kLoop, calls=%fused_computation.144 | loop fusion | bytes 20971520 | tf_op jit(solution)/shard_map/slice | solution.py:640
  397.8 10.1 %collective-permute-done.2 = bf16[1,4,4,24,640]{4,3,2,1,0:T(8,128)(2,1)} collective-permute-done((bf16[1,4,4,24,640]{4,3,2,1,0:T(8,128)(2,1)S(1)}, bf16[1,4,4,24,640]{4,3,2,1,0:T(8,128)(2,1)}, u32[]{:S(2)}, u32[]{:S(2)}) %collective-permute-start.2) | collective-permute-done | bytes 491552 | tf_op jit(solution)/shard_map/ppermute | solution.py:546
  409.6 10.1 %collective-permute-done.3 = bf16[1,4,4,24,640]{4,3,2,1,0:T(8,128)(2,1)} collective-permute-done((bf16[1,4,4,24,640]{4,3,2,1,0:T(8,128)(2,1)S(1)}, bf16[1,4,4,24,640]{4,3,2,1,0:T(8,128)(2,1)}, u32[]{:S(2)}, u32[]{:S(2)}) %collective-permute-start.3) | collective-permute-done | bytes 491552 | tf_op jit(solution)/shard_map/ppermute | solution.py:546
  421.4 5.9 collective-permute-done.4
  435.8 6.7 %collective-permute-done.6 = bf16[1,4,1,24,640]{4,3,2,1,0:T(8,128)(2,1)S(1)} collective-permute-done((bf16[1,4,1,24,640]{4,3,2,1,0:T(8,128)(2,1)S(1)}, bf16[1,4,1,24,640]{4,3,2,1,0:T(8,128)(2,1)S(1)}, u32[]{:S(2)}, u32[]{:S(2)}) %collective-permute-start.6) | collective-permute-done | bytes 122912 | tf_op jit(solution)/shard_map/ppermute | solution.py:546
  469.4 5.6 collective-permute-done.13
  495.5 6.4 %collective-permute-done.24 = bf16[1,1,4,32,640]{4,3,2,0,1:T(8,128)(2,1)S(1)} collective-permute-done((bf16[1,1,4,32,640]{4,3,2,0,1:T(8,128)(2,1)S(1)}, bf16[1,1,4,32,640]{4,3,2,0,1:T(8,128)(2,1)S(1)}, u32[]{:S(2)}, u32[]{:S(2)}) %collective-permute-start.24) | collective-permute-done | bytes 163872 | tf_op jit(solution)/shard_map/ppermute | solution.py:546
  502.0 5.3 collective-permute-done.15
  508.8 5.1 collective-permute-done.16
  522.0 20.9 %collective-permute-done.27 = bf16[1,1,1,32,640]{4,3,2,0,1:T(8,128)(2,1)S(1)} collective-permute-done((bf16[1,1,1,32,640]{4,3,2,0,1:T(8,128)(2,1)S(1)}, bf16[1,1,1,32,640]{4,3,2,0,1:T(8,128)(2,1)S(1)}, u32[]{:S(2)}, u32[]{:S(2)}) %collective-permute-start.27) | collective-permute-done | bytes 40992 | tf_op jit(solution)/shard_map/ppermute | solution.py:546
  553.7 6.5 %collective-permute-done.44 = bf16[1,1,4,80,640]{4,3,2,0,1:T(8,128)(2,1)S(1)} collective-permute-done((bf16[1,1,4,80,640]{4,3,2,0,1:T(8,128)(2,1)S(1)}, bf16[1,1,4,80,640]{4,3,2,0,1:T(8,128)(2,1)S(1)}, u32[]{:S(2)}, u32[]{:S(2)}) %collective-permute-start.44) | collective-permute-done | bytes 409632 | tf_op jit(solution)/shard_map/ppermute | solution.py:546
  563.1 6.4 %collective-permute-done.45 = bf16[1,1,4,80,640]{4,3,2,0,1:T(8,128)(2,1)S(1)} collective-permute-done((bf16[1,1,4,80,640]{4,3,2,0,1:T(8,128)(2,1)S(1)}, bf16[1,1,4,80,640]{4,3,2,0,1:T(8,128)(2,1)S(1)}, u32[]{:S(2)}, u32[]{:S(2)}) %collective-permute-start.45) | collective-permute-done | bytes 409632 | tf_op jit(solution)/shard_map/ppermute | solution.py:546
  573.1 6.7 %collective-permute-done.46 = bf16[1,1,4,80,640]{4,3,2,0,1:T(8,128)(2,1)} collective-permute-done((bf16[1,1,4,80,640]{4,3,2,0,1:T(8,128)(2,1)}, bf16[1,1,4,80,640]{4,3,2,0,1:T(8,128)(2,1)}, u32[]{:S(2)}, u32[]{:S(2)}) %collective-permute-start.46) | collective-permute-done | bytes 409632 | tf_op jit(solution)/shard_map/ppermute | solution.py:546
  612.8 7.7 %all-to-all-done.6 = bf16[8,2,10,640]{3,1,2,0:T(2,128)(2,1)S(1)} async-done(((bf16[8,2,10,640]{3,1,2,0:T(2,128)(2,1)}), bf16[8,2,10,640]{3,1,2,0:T(2,128)(2,1)S(1)}, u32[]{:S(2)}, u32[]{:S(2)}) %all-to-all-start.6) | async-done | bytes 204832 | tf_op jit(solution)/shard_map/all_to_all | solution.py:647
  (283 shorter events, 174.2 us)
Async XLA Ops:
  10.2 16.5 %all-to-all-start = ((bf16[8,2,10,640]{3,1,2,0:T(2,128)(2,1)}), bf16[8,2,10,640]{3,1,2,0:T(2,128)(2,1)S(1)}, u32[]{:S(2)}, u32[]{:S(2)}) async-start(bf16[8,2,10,640]{3,1,2,0:T(2,128)(2,1)} %copy.157), calls=%async_computation | async-start | bytes 409600 | tf_op jit(solution)/shard_map/all_to_all | solution.py:578
  18.2 84.0 %all-gather.5.cloned.1.call-start = ((), (), s32[]{:S(2)}) async-start(), calls=%async_computation.8 | async-start | bytes 14530560 | tf_op jit(solution)/shard_map/all_gather | solution.py:589
  32.4 190.7 %all-gather.7.cloned.1.call-start = ((), (), s32[]{:S(2)}) async-start(), calls=%async_computation.9 | async-start | bytes 26419200 | tf_op jit(solution)/shard_map/all_gather | solution.py:591
  117.3 34.4 %all-to-all-start.2 = ((bf16[8,3,320,128]{3,2,1,0:T(8,128)(2,1)}), bf16[8,3,320,128]{3,2,1,0:T(8,128)(2,1)S(1)}, u32[]{:S(2)}, u32[]{:S(2)}) async-start(bf16[8,3,320,128]{3,2,1,0:T(8,128)(2,1)} %bitcast.211), calls=%async_computation.2 | async-start | bytes 3932160 | tf_op jit(solution)/shard_map/all_to_all | solution.py:603
  163.2 17.6 %all-to-all-start.3 = ((bf16[8,320,128]{2,1,0:T(8,128)(2,1)}), bf16[8,320,128]{2,1,0:T(8,128)(2,1)}, u32[]{:S(2)}, u32[]{:S(2)}) async-start(bf16[8,320,128]{2,1,0:T(8,128)(2,1)} %get-tuple-element.35), calls=%async_computation.3 | async-start | bytes 1310720 | tf_op jit(solution)/shard_map/all_to_all | solution.py:603
  301.1 30.4 %all-to-all-start.5 = ((bf16[8,3,320,128]{3,2,1,0:T(8,128)(2,1)}), bf16[8,3,320,128]{3,2,1,0:T(8,128)(2,1)S(1)}, u32[]{:S(2)}, u32[]{:S(2)}) async-start(bf16[8,3,320,128]{3,2,1,0:T(8,128)(2,1)} %copy-done.2), calls=%async_computation.5 | async-start | bytes 3932160 | tf_op jit(solution)/shard_map/all_to_all | solution.py:603
  364.8 19.8 %collective-permute-start = (bf16[4,4,4,24,640]{4,3,2,1,0:T(8,128)(2,1)S(1)}, bf16[4,4,4,24,640]{4,3,2,1,0:T(8,128)(2,1)}, u32[]{:S(2)}, u32[]{:S(2)}) collective-permute-start(bf16[4,4,4,24,640]{4,3,2,1,0:T(8,128)(2,1)S(1)} %dynamic-slice_bitcast_fusion.2), channel_id=1, source_target_pairs={{0,8},{8,0},{1,9},{9,1},{2,10},{10,2},{3,11},{11,3},{4,12},{12,4},... | collective-permute-start | bytes 5898248 | tf_op jit(solution)/shard_map/ppermute | solution.py:515
  371.1 81.9 %collective-permute-start.40 = (bf16[4,4,4,80,640]{4,3,2,0,1:T(8,128)(2,1)}, bf16[4,4,4,80,640]{4,3,2,0,1:T(8,128)(2,1)}, u32[]{:S(2)}, u32[]{:S(2)}) collective-permute-start(bf16[4,4,4,80,640]{4,3,2,0,1:T(8,128)(2,1)} %copy_bitcast_fusion), channel_id=1, source_target_pairs={{0,8},{8,0},{1,9},{9,1},{2,10},{10,2},{3,11},{11,3},{4,12},{12,4},... | collective-permute-start | bytes 19660808 | tf_op jit(solution)/shard_map/ppermute | solution.py:515
  374.9 88.4 %collective-permute-start.30 = (bf16[4,4,4,80,640]{4,3,2,1,0:T(8,128)(2,1)}, bf16[4,4,4,80,640]{4,3,2,1,0:T(8,128)(2,1)}, u32[]{:S(2)}, u32[]{:S(2)}) collective-permute-start(bf16[4,4,4,80,640]{4,3,2,1,0:T(8,128)(2,1)} %dynamic-slice_bitcast_fusion), channel_id=1, source_target_pairs={{0,8},{8,0},{1,9},{9,1},{2,10},{10,2},{3,11},{11,3},{4,12},{12,4},... | collective-permute-start | bytes 19660808 | tf_op jit(solution)/shard_map/ppermute | solution.py:515
  386.0 10.2 %collective-permute-start.1 = (bf16[1,4,4,24,640]{4,3,2,1,0:T(8,128)(2,1)S(1)}, bf16[1,4,4,24,640]{4,3,2,1,0:T(8,128)(2,1)}, u32[]{:S(2)}, u32[]{:S(2)}) collective-permute-start(bf16[1,4,4,24,640]{4,3,2,1,0:T(8,128)(2,1)S(1)} %fusion.36), channel_id=1, source_target_pairs={{0,2},{2,4},{4,6},{6,0},{8,14},{10,8},{12,10},{14,12},{1,3},{3,5},... | collective-permute-start | bytes 1474568 | tf_op jit(solution)/shard_map/ppermute | solution.py:546
  389.8 37.6 %collective-permute-start.10 = (bf16[4,4,4,32,640]{4,3,2,1,0:T(8,128)(2,1)}, bf16[4,4,4,32,640]{4,3,2,1,0:T(8,128)(2,1)}, u32[]{:S(2)}, u32[]{:S(2)}) collective-permute-start(bf16[4,4,4,32,640]{4,3,2,1,0:T(8,128)(2,1)} %dynamic-slice_bitcast_fusion.1), channel_id=1, source_target_pairs={{0,8},{8,0},{1,9},{9,1},{2,10},{10,2},{3,11},{11,3},{4,12},{12,4},... | collective-permute-start | bytes 7864328 | tf_op jit(solution)/shard_map/ppermute | solution.py:515
  391.0 42.6 %collective-permute-start.20 = (bf16[4,4,4,32,640]{4,3,2,0,1:T(8,128)(2,1)S(1)}, bf16[4,4,4,32,640]{4,3,2,0,1:T(8,128)(2,1)}, u32[]{:S(2)}, u32[]{:S(2)}) collective-permute-start(bf16[4,4,4,32,640]{4,3,2,0,1:T(8,128)(2,1)S(1)} %copy_bitcast_fusion.1), channel_id=1, source_target_pairs={{0,8},{8,0},{1,9},{9,1},{2,10},{10,2},{3,11},{11,3},{4,12},{12,4},... | collective-permute-start | bytes 7864328 | tf_op jit(solution)/shard_map/ppermute | solution.py:515
  428.9 14.3 %collective-permute-start.11 = (bf16[4,4,1,32,640]{4,3,1,0,2:T(8,128)(2,1)S(1)}, bf16[4,4,1,32,640]{4,3,1,0,2:T(8,128)(2,1)S(1)}, u32[]{:S(2)}, u32[]{:S(2)}) collective-permute-start(bf16[4,4,1,32,640]{4,3,1,0,2:T(8,128)(2,1)S(1)} %fusion.29), channel_id=1, source_target_pairs={{0,32},{32,64},{64,96},{96,0},{8,104},{40,8},{72,40},{104,72},{1,3... | collective-permute-start | bytes 1966088 | tf_op jit(solution)/shard_map/ppermute | solution.py:546
  435.1 12.7 %collective-permute-start.21 = (bf16[4,1,4,32,640]{4,3,2,0,1:T(8,128)(2,1)S(1)}, bf16[4,1,4,32,640]{4,3,2,0,1:T(8,128)(2,1)S(1)}, u32[]{:S(2)}, u32[]{:S(2)}) collective-permute-start(bf16[4,1,4,32,640]{4,3,2,0,1:T(8,128)(2,1)S(1)} %fusion.22), channel_id=1, source_target_pairs={{0,16},{16,1},{1,17},{17,0},{8,25},{24,8},{9,24},{25,9},{2,18},{18... | collective-permute-start | bytes 1966088 | tf_op jit(solution)/shard_map/ppermute | solution.py:546
  444.8 16.9 %collective-permute-start.12 = (bf16[4,4,1,32,640]{4,3,1,0,2:T(8,128)(2,1)S(1)}, bf16[4,4,1,32,640]{4,3,1,0,2:T(8,128)(2,1)S(1)}, u32[]{:S(2)}, u32[]{:S(2)}) collective-permute-start(bf16[4,4,1,32,640]{4,3,1,0,2:T(8,128)(2,1)S(1)} %fusion.28), channel_id=1, source_target_pairs={{0,32},{32,64},{64,96},{96,0},{8,104},{40,8},{72,40},{104,72},{1,3... | collective-permute-start | bytes 1966088 | tf_op jit(solution)/shard_map/ppermute | solution.py:546
  449.4 18.4 %collective-permute-start.22 = (bf16[4,1,4,32,640]{4,3,2,0,1:T(8,128)(2,1)S(1)}, bf16[4,1,4,32,640]{4,3,2,0,1:T(8,128)(2,1)S(1)}, u32[]{:S(2)}, u32[]{:S(2)}) collective-permute-start(bf16[4,1,4,32,640]{4,3,2,0,1:T(8,128)(2,1)S(1)} %fusion.21), channel_id=1, source_target_pairs={{0,16},{16,1},{1,17},{17,0},{8,25},{24,8},{9,24},{25,9},{2,18},{18... | collective-permute-start | bytes 1966088 | tf_op jit(solution)/shard_map/ppermute | solution.py:546
  455.4 23.8 %collective-permute-start.41 = (bf16[4,1,4,80,640]{4,3,2,0,1:T(8,128)(2,1)S(1)}, bf16[4,1,4,80,640]{4,3,2,0,1:T(8,128)(2,1)S(1)}, u32[]{:S(2)}, u32[]{:S(2)}) collective-permute-start(bf16[4,1,4,80,640]{4,3,2,0,1:T(8,128)(2,1)S(1)} %fusion.8), channel_id=1, source_target_pairs={{0,16},{16,1},{1,17},{17,0},{8,25},{24,8},{9,24},{25,9},{2,18},{18... | collective-permute-start | bytes 4915208 | tf_op jit(solution)/shard_map/ppermute | solution.py:546
  463.2 11.9 %collective-permute-start.13 = (bf16[4,4,1,32,640]{4,3,1,0,2:T(8,128)(2,1)S(1)}, bf16[4,4,1,32,640]{4,3,1,0,2:T(8,128)(2,1)S(1)}, u32[]{:S(2)}, u32[]{:S(2)}) collective-permute-start(bf16[4,4,1,32,640]{4,3,1,0,2:T(8,128)(2,1)S(1)} %fusion.26), channel_id=1, source_target_pairs={{0,32},{32,64},{64,96},{96,0},{8,104},{40,8},{72,40},{104,72},{1,3... | collective-permute-start | bytes 1966088 | tf_op jit(solution)/shard_map/ppermute | solution.py:546
  465.6 27.0 %collective-permute-start.31 = (bf16[4,4,1,80,640]{4,3,2,1,0:T(8,128)(2,1)S(1)}, bf16[4,4,1,80,640]{4,3,2,1,0:T(8,128)(2,1)S(1)}, u32[]{:S(2)}, u32[]{:S(2)}) collective-permute-start(bf16[4,4,1,80,640]{4,3,2,1,0:T(8,128)(2,1)S(1)} %fusion.15), channel_id=1, source_target_pairs={{0,32},{32,64},{64,96},{96,0},{8,104},{40,8},{72,40},{104,72},{1,3... | collective-permute-start | bytes 4915208 | tf_op jit(solution)/shard_map/ppermute | solution.py:546
  469.3 16.9 %collective-permute-start.23 = (bf16[4,1,4,32,640]{4,3,2,0,1:T(8,128)(2,1)S(1)}, bf16[4,1,4,32,640]{4,3,2,0,1:T(8,128)(2,1)S(1)}, u32[]{:S(2)}, u32[]{:S(2)}) collective-permute-start(bf16[4,1,4,32,640]{4,3,2,0,1:T(8,128)(2,1)S(1)} %fusion.19), channel_id=1, source_target_pairs={{0,16},{16,1},{1,17},{17,0},{8,25},{24,8},{9,24},{25,9},{2,18},{18... | collective-permute-start | bytes 1966088 | tf_op jit(solution)/shard_map/ppermute | solution.py:546
  476.6 18.7 %collective-permute-start.14 = (bf16[4,1,1,32,640]{4,3,2,1,0:T(8,128)(2,1)S(1)}, bf16[4,1,1,32,640]{4,3,2,1,0:T(8,128)(2,1)S(1)}, u32[]{:S(2)}, u32[]{:S(2)}) collective-permute-start(bf16[4,1,1,32,640]{4,3,2,1,0:T(8,128)(2,1)S(1)} %constant_dynamic-slice_fusion.8), channel_id=1, source_target_pairs={{0,16},{16,1},{1,17},{17,0},{8,25},{24,8},{9,24},{25,9},{2,18},{18... | collective-permute-start | bytes 491528 | tf_op jit(solution)/shard_map/ppermute | solution.py:546
  481.7 32.2 %collective-permute-start.42 = (bf16[4,1,4,80,640]{4,3,2,0,1:T(8,128)(2,1)S(1)}, bf16[4,1,4,80,640]{4,3,2,0,1:T(8,128)(2,1)S(1)}, u32[]{:S(2)}, u32[]{:S(2)}) collective-permute-start(bf16[4,1,4,80,640]{4,3,2,0,1:T(8,128)(2,1)S(1)} %fusion.7), channel_id=1, source_target_pairs={{0,16},{16,1},{1,17},{17,0},{8,25},{24,8},{9,24},{25,9},{2,18},{18... | collective-permute-start | bytes 4915208 | tf_op jit(solution)/shard_map/ppermute | solution.py:546
  495.1 22.4 %collective-permute-start.32 = (bf16[4,4,1,80,640]{4,3,2,1,0:T(8,128)(2,1)S(1)}, bf16[4,4,1,80,640]{4,3,2,1,0:T(8,128)(2,1)S(1)}, u32[]{:S(2)}, u32[]{:S(2)}) collective-permute-start(bf16[4,4,1,80,640]{4,3,2,1,0:T(8,128)(2,1)S(1)} %fusion.14), channel_id=1, source_target_pairs={{0,32},{32,64},{64,96},{96,0},{8,104},{40,8},{72,40},{104,72},{1,3... | collective-permute-start | bytes 4915208 | tf_op jit(solution)/shard_map/ppermute | solution.py:546
  495.4 11.8 %collective-permute-start.15 = (bf16[4,1,1,32,640]{4,3,2,1,0:T(8,128)(2,1)S(1)}, bf16[4,1,1,32,640]{4,3,2,1,0:T(8,128)(2,1)S(1)}, u32[]{:S(2)}, u32[]{:S(2)}) collective-permute-start(bf16[4,1,1,32,640]{4,3,2,1,0:T(8,128)(2,1)S(1)} %add_convert_fusion.11), channel_id=1, source_target_pairs={{0,16},{16,1},{1,17},{17,0},{8,25},{24,8},{9,24},{25,9},{2,18},{18... | collective-permute-start | bytes 491528 | tf_op jit(solution)/shard_map/ppermute | solution.py:546
  508.5 11.6 %collective-permute-start.26 = (bf16[1,1,4,32,640]{4,3,2,0,1:T(8,128)(2,1)S(1)}, bf16[1,1,4,32,640]{4,3,2,0,1:T(8,128)(2,1)S(1)}, u32[]{:S(2)}, u32[]{:S(2)}) collective-permute-start(bf16[1,1,4,32,640]{4,3,2,0,1:T(8,128)(2,1)S(1)} %add_convert_fusion.7), channel_id=1, source_target_pairs={{0,2},{2,4},{4,6},{6,0},{8,14},{10,8},{12,10},{14,12},{1,3},{3,5},... | collective-permute-start | bytes 491528 | tf_op jit(solution)/shard_map/ppermute | solution.py:546
  516.5 31.8 %collective-permute-start.43 = (bf16[4,1,4,80,640]{4,3,2,0,1:T(8,128)(2,1)S(1)}, bf16[4,1,4,80,640]{4,3,2,0,1:T(8,128)(2,1)S(1)}, u32[]{:S(2)}, u32[]{:S(2)}) collective-permute-start(bf16[4,1,4,80,640]{4,3,2,0,1:T(8,128)(2,1)S(1)} %fusion.5), channel_id=1, source_target_pairs={{0,16},{16,1},{1,17},{17,0},{8,25},{24,8},{9,24},{25,9},{2,18},{18... | collective-permute-start | bytes 4915208 | tf_op jit(solution)/shard_map/ppermute | solution.py:546
  520.1 30.9 %collective-permute-start.33 = (bf16[4,4,1,80,640]{4,3,2,1,0:T(8,128)(2,1)S(1)}, bf16[4,4,1,80,640]{4,3,2,1,0:T(8,128)(2,1)S(1)}, u32[]{:S(2)}, u32[]{:S(2)}) collective-permute-start(bf16[4,4,1,80,640]{4,3,2,1,0:T(8,128)(2,1)S(1)} %fusion.12), channel_id=1, source_target_pairs={{0,32},{32,64},{64,96},{96,0},{8,104},{40,8},{72,40},{104,72},{1,3... | collective-permute-start | bytes 4915208 | tf_op jit(solution)/shard_map/ppermute | solution.py:546
  520.2 22.7 %collective-permute-start.27 = (bf16[1,1,1,32,640]{4,3,2,0,1:T(8,128)(2,1)S(1)}, bf16[1,1,1,32,640]{4,3,2,0,1:T(8,128)(2,1)S(1)}, u32[]{:S(2)}, u32[]{:S(2)}) collective-permute-start(bf16[1,1,1,32,640]{4,3,2,0,1:T(8,128)(2,1)S(1)} %constant_dynamic-slice_fusion.3), channel_id=1, source_target_pairs={{0,32},{32,64},{64,96},{96,0},{8,104},{40,8},{72,40},{104,72},{1,3... | collective-permute-start | bytes 122888 | tf_op jit(solution)/shard_map/ppermute | solution.py:546
  521.9 21.1 %collective-permute-start.18 = (bf16[1,1,1,32,640]{4,3,2,1,0:T(8,128)(2,1)S(1)}, bf16[1,1,1,32,640]{4,3,2,1,0:T(8,128)(2,1)S(1)}, u32[]{:S(2)}, u32[]{:S(2)}) collective-permute-start(bf16[1,1,1,32,640]{4,3,2,1,0:T(8,128)(2,1)S(1)} %add_convert_fusion.26), channel_id=1, source_target_pairs={{0,2},{2,4},{4,6},{6,0},{8,14},{10,8},{12,10},{14,12},{1,3},{3,5},... | collective-permute-start | bytes 122888 | tf_op jit(solution)/shard_map/ppermute | solution.py:546
  543.0 17.3 %collective-permute-start.19 = (bf16[1,1,1,32,640]{4,3,2,1,0:T(8,128)(2,1)S(1)}, bf16[1,1,1,32,640]{4,3,2,1,0:T(8,128)(2,1)S(1)}, u32[]{:S(2)}, u32[]{:S(2)}) collective-permute-start(bf16[1,1,1,32,640]{4,3,2,1,0:T(8,128)(2,1)S(1)} %add_convert_fusion.25), channel_id=1, source_target_pairs={{0,2},{2,4},{4,6},{6,0},{8,14},{10,8},{12,10},{14,12},{1,3},{3,5},... | collective-permute-start | bytes 122888 | tf_op jit(solution)/shard_map/ppermute | solution.py:546
  548.2 22.1 %collective-permute-start.29 = (bf16[1,1,1,32,640]{4,3,2,0,1:T(8,128)(2,1)S(1)}, bf16[1,1,1,32,640]{4,3,2,0,1:T(8,128)(2,1)S(1)}, u32[]{:S(2)}, u32[]{:S(2)}) collective-permute-start(bf16[1,1,1,32,640]{4,3,2,0,1:T(8,128)(2,1)S(1)} %add_convert_fusion.22), channel_id=1, source_target_pairs={{0,32},{32,64},{64,96},{96,0},{8,104},{40,8},{72,40},{104,72},{1,3... | collective-permute-start | bytes 122888 | tf_op jit(solution)/shard_map/ppermute | solution.py:546
  608.7 11.8 %all-to-all-start.6 = ((bf16[8,2,10,640]{3,1,2,0:T(2,128)(2,1)}), bf16[8,2,10,640]{3,1,2,0:T(2,128)(2,1)S(1)}, u32[]{:S(2)}, u32[]{:S(2)}) async-start(bf16[8,2,10,640]{3,1,2,0:T(2,128)(2,1)} %copy.184), calls=%async_computation.6 | async-start | bytes 409600 | tf_op jit(solution)/shard_map/all_to_all | solution.py:647
  (53 other events, 562.7 us)
Sparse Core Ops, SparseCore 0:
  28.5 73.6 all-gather.4
  105.8 117.3 all-gather.6

commit v2 on v1

v2 whole, which is shorter than its diff:
```python
import functools
import math

import jax
import jax.numpy as jnp
from jax import lax
from jax.experimental import pallas as pl
from jax.experimental.pallas import tpu as pltpu
from jax.sharding import Mesh
from jax.sharding import PartitionSpec as P

HEADS = 20
NORM_EPS = 1e-05
MASKED = -1000000000.0

F32 = jnp.float32
BF16 = jnp.bfloat16

AXES = ("x", "yl", "c", "z", "yh")
SIZES = (4, 2, 2, 4, 2)
DP = ("x", "yl", "c")
CTX = ("z", "yh")
PLACE = ("z", "yh", "yl", "x", "c")

D = 1280
SPAN = 128
SEQ_GRP = 2
ROWS = SEQ_GRP * SPAN
CTX_N = 8
LEN = CTX_N * SPAN
HEAD_DIM = D // HEADS
GROUP_HEADS = 5
GROUP_W = GROUP_HEADS * HEAD_DIM
COLS = 640
BLK = 80
SCALE = 1.0 / math.sqrt(HEAD_DIM)
Q_BLOCK = 256
HEADS_W = 3 * GROUP_W
PIECE = 32
MB = 1 << 20


def place_of(dp):
    x, yl, c = dp // 4, (dp // 2) % 2, dp % 2
    return (yl * 4 + x) * 2 + c


def dot(left, right):
    return lax.dot_general(
        left, right, (((1,), (0,)), ((), ())), preferred_element_type=F32
    )


def dot_nt(left, right):
    return lax.dot_general(
        left, right, (((1,), (1,)), ((), ())), preferred_element_type=F32
    )


def norm_stats(rows):
    centre = jnp.mean(rows, axis=-1, keepdims=True)
    centred = rows - centre
    spread = jnp.mean(centred * centred, axis=-1, keepdims=True)
    scale = lax.rsqrt(spread + NORM_EPS)
    return centred * scale, scale


def norm_back(normed, scale, gain, grad):
    scaled = gain * grad
    mean_one = jnp.mean(scaled, axis=-1, keepdims=True)
    mean_two = jnp.mean(scaled * normed, axis=-1, keepdims=True)
    return (scaled - mean_one - normed * mean_two) * scale


def stack_rows(ref, *lead):
    return jnp.concatenate([ref[(*lead, place_of(dp))] for dp in range(16)], axis=0)


def params(vmem_mb):
    return pltpu.CompilerParams(vmem_limit_bytes=vmem_mb * MB)


def cost(flops, nbytes, trans=0):
    return pl.CostEstimate(flops=flops, bytes_accessed=nbytes, transcendentals=trans)


def whole(shape):
    return pl.BlockSpec(shape, lambda *i: (0,) * len(shape))


def turn(block):
    return block.astype(F32).T.astype(BF16)


def allowed_of(length, first_query, key_count, query_count):
    key_pos = lax.broadcasted_iota(jnp.int32, (key_count, query_count), 0)
    query_pos = first_query + lax.broadcasted_iota(
        jnp.int32, (key_count, query_count), 1
    )
    return (key_pos <= query_pos) & (key_pos < length)


def attend_kernel(
    len_ref, tok_ref, norm_ref, bias_ref, w_ref, qkv_ref, out_ref, lse_ref
):
    head = pl.program_id(0)

    @pl.when(head == 0)
    def _():
        weight = w_ref[...].reshape(D, HEADS_W)
        for block in range(LEN // Q_BLOCK):
            cut = slice(block * Q_BLOCK, (block + 1) * Q_BLOCK)
            normed, _ = norm_stats(tok_ref[cut].astype(F32))
            normed = (normed * norm_ref[0:1] + norm_ref[1:2]).astype(BF16)
            turned = (dot(normed, weight) + bias_ref[...]).T.astype(BF16)
            for row in range(3 * GROUP_HEADS):
                qkv_ref[row // GROUP_HEADS, row % GROUP_HEADS, :, cut] = turned[
                    row * HEAD_DIM : (row + 1) * HEAD_DIM
                ]

    length = len_ref[0]
    query = qkv_ref[0, head]
    key = turn(qkv_ref[1, head])
    value = qkv_ref[2, head]
    for block in range(LEN // Q_BLOCK):
        first = block * Q_BLOCK
        last = first + Q_BLOCK
        scores = dot(key[:last], query[:, first:last]) * SCALE
        scores = jnp.where(allowed_of(length, first, last, Q_BLOCK), scores, MASKED)
        top = jnp.max(scores, axis=0, keepdims=True)
        weights = jnp.exp(scores - top)
        total = jnp.sum(weights, axis=0, keepdims=True)
        result = dot(value[:, :last], weights.astype(BF16)) / total
        lse_ref[0, :, first:last] = top + jnp.log(total)
        result = result.astype(BF16)
        for part in range(Q_BLOCK // SPAN):
            out_ref[first // SPAN + part] = result[:, part * SPAN : (part + 1) * SPAN]


def attend_call(length, tok, norm, bias, w_qkv):
    return pl.pallas_call(
        attend_kernel,
        grid=(GROUP_HEADS,),
        in_specs=[
            pl.BlockSpec(memory_space=pltpu.SMEM),
            whole((LEN, D)),
            whole((2, D)),
            whole((1, HEADS_W)),
            whole((16, BLK, HEADS_W)),
        ],
        out_specs=[
            whole((3, GROUP_HEADS, HEAD_DIM, LEN)),
            pl.BlockSpec((CTX_N, HEAD_DIM, SPAN), lambda h: (0, h, 0)),
            pl.BlockSpec((1, 1, LEN), lambda h: (h, 0, 0)),
        ],
        out_shape=[
            jax.ShapeDtypeStruct((3, GROUP_HEADS, HEAD_DIM, LEN), BF16),
            jax.ShapeDtypeStruct((CTX_N, GROUP_W, SPAN), BF16),
            jax.ShapeDtypeStruct((GROUP_HEADS, 1, LEN), F32),
        ],
        compiler_params=params(56),
        cost_estimate=cost(
            6 * LEN * LEN * 4 * HEAD_DIM + 2 * LEN * D * HEADS_W, 8 * MB, 3 * LEN * LEN
        ),
        name="attend",
    )(length, tok, norm, bias, w_qkv)


def attend_back_kernel(
    len_ref,
    tok_ref,
    norm_ref,
    w_ref,
    qkv_ref,
    grad_ref,
    lse_ref,
    d_w_ref,
    d_bias_ref,
    g_norm_ref,
    g_ref,
    gk_ref,
    gv_ref,
    n1t_ref,
):
    head = pl.program_id(0)

    @pl.when(head == 0)
    def _():
        for block in range(LEN // Q_BLOCK):
            cut = slice(block * Q_BLOCK, (block + 1) * Q_BLOCK)
            normed, _ = norm_stats(tok_ref[cut].astype(F32))
            normed = normed * norm_ref[0:1] + norm_ref[1:2]
            n1t_ref[:, cut] = normed.T.astype(BF16)

    length = len_ref[0]
    query = qkv_ref[0, head]
    key_t = qkv_ref[1, head]
    key = turn(key_t)
    value = turn(qkv_ref[2, head])
    grad = jnp.concatenate([grad_ref[p] for p in range(CTX_N)], axis=1)
    gk_ref[...] = jnp.zeros_like(gk_ref)
    gv_ref[...] = jnp.zeros_like(gv_ref)
    for block in range(LEN // Q_BLOCK):
        first = block * Q_BLOCK
        last = first + Q_BLOCK
        query_b = query[:, first:last]
        grad_b = grad[:, first:last]
        scores = dot(key[:last], query_b) * SCALE
        probs = jnp.where(
            allowed_of(length, first, last, Q_BLOCK),
            jnp.exp(scores - lse_ref[0, :, first:last]),
            0.0,
        )
        grad_probs = dot(value[:last], grad_b)
        delta = jnp.sum(probs * grad_probs, axis=0, keepdims=True)
        grad_scores = (probs * (grad_probs - delta)).astype(BF16)
        g_ref[0, head, :, first:last] = (
            dot(key_t[:, :last], grad_scores) * SCALE
        ).astype(BF16)
        gk_ref[:, :last] += dot_nt(query_b, grad_scores)
        gv_ref[:, :last] += dot_nt(grad_b, probs.astype(BF16))
    g_ref[1, head] = (gk_ref[...] * SCALE).astype(BF16)
    g_ref[2, head] = gv_ref[...].astype(BF16)

    @pl.when(head == GROUP_HEADS - 1)
    def _():
        grads = g_ref[...].reshape(HEADS_W, LEN)
        d_bias_ref[...] = dot_nt(jnp.ones((8, LEN), BF16), grads)
        for part in range(4):
            rows = 4 * BLK
            d_w = dot_nt(n1t_ref[part * rows : (part + 1) * rows], grads)
            d_w_ref[part * 4 : (part + 1) * 4] = d_w.astype(BF16).reshape(
                4, BLK, HEADS_W
            )
        weight = w_ref[...].reshape(D, HEADS_W)
        for block in range(LEN // Q_BLOCK):
            cut = slice(block * Q_BLOCK, (block + 1) * Q_BLOCK)
            g_norm = dot_nt(turn(grads[:, cut]), weight).astype(BF16)
            for part in range(Q_BLOCK // SPAN):
                g_norm_ref[block * (Q_BLOCK // SPAN) + part] = g_norm[
                    part * SPAN : (part + 1) * SPAN
                ]


def attend_back_call(length, tok, norm, w_qkv, qkv, grad, lse):
    return pl.pallas_call(
        attend_back_kernel,
        grid=(GROUP_HEADS,),
        in_specs=[
            pl.BlockSpec(memory_space=pltpu.SMEM),
            whole((LEN, D)),
            whole((2, D)),
            whole((16, BLK, HEADS_W)),
            whole((3, GROUP_HEADS, HEAD_DIM, LEN)),
            pl.BlockSpec((CTX_N, HEAD_DIM, SPAN), lambda h: (0, h, 0)),
            pl.BlockSpec((1, 1, LEN), lambda h: (h, 0, 0)),
        ],
        out_specs=[
            whole((16, BLK, HEADS_W)),
            whole((8, HEADS_W)),
            whole((CTX_N, SPAN, D)),
        ],
        out_shape=[
            jax.ShapeDtypeStruct((16, BLK, HEADS_W), BF16),
            jax.ShapeDtypeStruct((8, HEADS_W), F32),
            jax.ShapeDtypeStruct((CTX_N, SPAN, D), BF16),
        ],
        scratch_shapes=[
            pltpu.VMEM((3, GROUP_HEADS, HEAD_DIM, LEN), BF16),
            pltpu.VMEM((HEAD_DIM, LEN), F32),
            pltpu.VMEM((HEAD_DIM, LEN), F32),
            pltpu.VMEM((D, LEN), BF16),
        ],
        compiler_params=params(56),
        cost_estimate=cost(
            15 * LEN * LEN * 4 * HEAD_DIM + 4 * LEN * D * HEADS_W,
            16 * MB,
            3 * LEN * LEN,
        ),
        name="attend_back",
    )(length, tok, norm, w_qkv, qkv, grad, lse)


def norm_back_kernel(
    tok_ref, gain_ref, g_res_ref, part_ref, in_grad_ref, d_norm_ref
):
    for seq in range(SEQ_GRP):
        cut = slice(seq * SPAN, (seq + 1) * SPAN)
        normed, scale = norm_stats(tok_ref[cut].astype(F32))
        g_norm = part_ref[4 * seq].astype(F32)
        for group in range(1, 4):
            g_norm = g_norm + part_ref[4 * seq + group].astype(F32)
        in_grad_ref[cut] = g_res_ref[cut].astype(F32) + norm_back(
            normed, scale, gain_ref[...], g_norm
        )
        d_gain = jnp.sum(g_norm * normed, axis=0, keepdims=True)
        d_shift = jnp.sum(g_norm, axis=0, keepdims=True)
        if seq == 0:
            d_norm_ref[0:1] = d_gain
            d_norm_ref[1:2] = d_shift
        else:
            d_norm_ref[0:1] += d_gain
            d_norm_ref[1:2] += d_shift


def norm_back_call(tok, gain, g_res, parts):
    return pl.pallas_call(
        norm_back_kernel,
        out_shape=[
            jax.ShapeDtypeStruct((ROWS, D), F32),
            jax.ShapeDtypeStruct((2, D), F32),
        ],
        compiler_params=params(32),
        cost_estimate=cost(40 * ROWS * D, 6 * MB),
        name="norm_back",
    )(tok, gain, g_res, parts)


def mlp_kernel(
    info_ref,
    tok_ref,
    cot_ref,
    att_ref,
    vec_ref,
    fc_bias_ref,
    wp_ref,
    wf_ref,
    wo_ref,
    out_ref,
    g_res_ref,
    g_att_ref,
    d_vec_ref,
    d_fc_bias_ref,
    d_wp_keep_ref,
    d_wp_give_ref,
    d_wf_keep_ref,
    d_wf_give_ref,
    d_wo_keep_ref,
    d_wo_give_ref,
    res_ref,
    n2_ref,
    n2t_ref,
    att_t_ref,
    act_t_ref,
    g_out_ref,
    acc_ref,
    gn_ref,
    wp_all_ref,
):
    step = pl.program_id(0)
    core = info_ref[SEQ_GRP + 1]
    proj_shift, gain, shift, out_shift = (vec_ref[k : k + 1] for k in range(4))

    @pl.when(step == 0)
    def _():
        att = jnp.concatenate([turn(att_ref[s]) for s in range(SEQ_GRP)], axis=0)
        for half in range(2):
            cut = slice(half * COLS, (half + 1) * COLS)
            pack = pack_of(half, (BLK, CTX_N * PIECE), 0, 1)
            for dp in range(16):
                pieces = wp_ref[:, place_of(dp)].reshape(CTX_N * PIECE, COLS)
                wp_all_ref[dp * BLK : (dp + 1) * BLK, cut] = dot(pack, pieces).astype(
                    BF16
                )
        res_ref[...] = (
            tok_ref[...].astype(F32) + dot(att, wp_all_ref[...]) + proj_shift
        )
        residual = res_ref[...]
        normed, _ = norm_stats(residual)
        normed = normed * gain + shift
        n2_ref[...] = normed.astype(BF16)
        by_core(n2t_ref, normed.T.astype(BF16))
        for seq in range(SEQ_GRP):
            cut = slice(seq * SPAN, (seq + 1) * SPAN)
            by_core(att_t_ref, att_ref[seq], cut)
            pos = info_ref[SEQ_GRP] + lax.broadcasted_iota(jnp.int32, (SPAN, D), 0)
            g_out_ref[cut] = jnp.where(
                pos < info_ref[seq], cot_ref[cut], jnp.zeros((SPAN, D), BF16)
            )
        acc_ref[...] = residual + out_shift
        gn_ref[...] = jnp.zeros_like(gn_ref)

    w_fc = stack_rows(wf_ref, 0)
    pre = dot(n2_ref[...], w_fc) + fc_bias_ref[...]
    root = math.sqrt(2.0 / math.pi)
    square = pre * pre
    bend = jnp.tanh(root * pre * (1.0 + 0.044715 * square))
    gate = 0.5 * (1.0 + bend)
    slope = gate + 0.5 * pre * (1.0 - bend * bend) * root * (
        1.0 + 3.0 * 0.044715 * square
    )
    act_f = pre * gate
    act = act_f.astype(BF16)
    act_t = act_f.T.astype(BF16)
    for c in range(2):
        act_t_ref[c] = act_t[c * 320 : (c + 1) * 320]
    g_act = None
    for half in range(2):
        cut = slice(half * COLS, (half + 1) * COLS)
        w_out = jnp.concatenate(
            [
                wo_ref[z, yh, 0, 0, c, half * 40 : (half + 1) * 40]
                for c in range(2)
                for z in range(4)
                for yh in range(2)
            ],
            axis=0,
        )
        acc_ref[:, cut] += dot(act, w_out)
        part = dot_nt(g_out_ref[:, cut], w_out)
        g_act = part if g_act is None else g_act + part
        for side, ref in ((core, d_wo_keep_ref), (1 - core, d_wo_give_ref)):
            d_w = dot(act_t_ref[side], g_out_ref[:, cut]).astype(BF16)
            for z in range(4):
                for yh in range(2):
                    row = (z * 2 + yh) * 40
                    ref[z, yh, 0, 0, half] = d_w[row : row + 40]
    g_pre = (g_act * slope).astype(BF16)
    d_fc_bias_ref[...] = jnp.sum(g_pre.astype(F32), axis=0, keepdims=True)
    gn_ref[...] += dot_nt(g_pre, w_fc)
    for side, ref in ((core, d_wf_keep_ref), (1 - core, d_wf_give_ref)):
        d_w = dot(n2t_ref[side].reshape(D // 2, ROWS), g_pre).astype(BF16)
        ref[0] = d_w.reshape(8, BLK, COLS)

    @pl.when(step == pl.num_programs(0) - 1)
    def _():
        out_ref[...] = acc_ref[...].astype(BF16)
        normed, scale = norm_stats(res_ref[...])
        g_norm = gn_ref[...]
        g_out = g_out_ref[...].astype(F32)
        g_res = (g_out + norm_back(normed, scale, gain, g_norm)).astype(BF16)
        g_res_ref[...] = g_res
        d_vec_ref[0:1] = jnp.sum(g_res.astype(F32), axis=0, keepdims=True)
        d_vec_ref[1:2] = jnp.sum(g_norm * normed, axis=0, keepdims=True)
        d_vec_ref[2:3] = jnp.sum(g_norm, axis=0, keepdims=True)
        d_vec_ref[3:4] = jnp.sum(g_out, axis=0, keepdims=True)
        g_att = dot_nt(g_res, wp_all_ref[...])
        for side, ref in ((core, d_wp_keep_ref), (1 - core, d_wp_give_ref)):
            d_w = dot(att_t_ref[side].reshape(D // 2, ROWS), g_res).astype(BF16)
            for chip in range(8):
                piece = None
                for half in range(2):
                    unpack = pack_of(half, (CTX_N * PIECE, BLK), 1, 0)
                    part = dot(
                        unpack,
                        d_w[
                            chip * BLK : (chip + 1) * BLK,
                            half * COLS : (half + 1) * COLS,
                        ],
                    )
                    piece = part if piece is None else piece + part
                ref[:, chip] = piece.astype(BF16).reshape(CTX_N, PIECE, COLS)
        for seq in range(SEQ_GRP):
            g_att_ref[seq] = g_att[seq * SPAN : (seq + 1) * SPAN].T.astype(BF16)


def pack_of(half, shape, row_dim, piece_dim):
    row = lax.broadcasted_iota(jnp.int32, shape, row_dim)
    place = lax.broadcasted_iota(jnp.int32, shape, piece_dim)
    offset = place - 22 * (row // 10) - 10 * half
    return (offset == row).astype(F32).astype(BF16)


def by_core(ref, turned, cut=slice(None)):
    for dp in range(16):
        ref[dp % 2, place_of(dp) // 2, :, cut] = turned[dp * BLK : (dp + 1) * BLK]


def mlp_call(info, tok, cot, att, vecs, fc_bias, weights):
    wp_block = whole((8, 8, PIECE, COLS))
    wf_block = pl.BlockSpec((1, 8, BLK, COLS), lambda j: (j, 0, 0, 0))
    wo_block = pl.BlockSpec(
        (4, 2, 1, 1, 2, 40, COLS), lambda j: (0, 0, j % 2, j // 2, 0, 0, 0)
    )
    small = jax.ShapeDtypeStruct((8, 8, PIECE, COLS), BF16)
    wide = jax.ShapeDtypeStruct((8, 8, BLK, COLS), BF16)
    tall = jax.ShapeDtypeStruct((4, 2, 2, 4, 2, 40, COLS), BF16)
    by_ctx = weights.reshape(CTX_N, 16, 2 * BLK + PIECE, COLS)
    by_chip = weights.reshape(4, 2, 2, 4, 2, 2 * BLK + PIECE, COLS)
    return pl.pallas_call(
        mlp_kernel,
        grid=(8,),
        in_specs=[
            pl.BlockSpec(memory_space=pltpu.SMEM),
            whole((ROWS, D)),
            whole((ROWS, D)),
            whole((SEQ_GRP, D, SPAN)),
            whole((4, D)),
            pl.BlockSpec((1, COLS), lambda j: (0, j)),
            pl.BlockSpec((CTX_N, 16, PIECE, COLS), lambda j: (0, 0, 5, 0)),
            pl.BlockSpec((1, 16, BLK, COLS), lambda j: (j, 0, 0, 0)),
            pl.BlockSpec(
                (4, 2, 1, 1, 2, BLK, COLS), lambda j: (0, 0, j % 2, j // 2, 0, 1, 0)
            ),
        ],
        out_specs=[
            whole((ROWS, D)),
            whole((ROWS, D)),
            whole((SEQ_GRP, D, SPAN)),
            whole((4, D)),
            pl.BlockSpec((1, COLS), lambda j: (0, j)),
            wp_block,
            wp_block,
            wf_block,
            wf_block,
            wo_block,
            wo_block,
        ],
        out_shape=[
            jax.ShapeDtypeStruct((ROWS, D), BF16),
            jax.ShapeDtypeStruct((ROWS, D), BF16),
            jax.ShapeDtypeStruct((SEQ_GRP, D, SPAN), BF16),
            jax.ShapeDtypeStruct((4, D), F32),
            jax.ShapeDtypeStruct((1, 4 * D), F32),
            small,
            small,
            wide,
            wide,
            tall,
            tall,
        ],
        scratch_shapes=[
            pltpu.VMEM((ROWS, D), F32),
            pltpu.VMEM((ROWS, D), BF16),
            pltpu.VMEM((2, 8, BLK, ROWS), BF16),
            pltpu.VMEM((2, 8, BLK, ROWS), BF16),
            pltpu.VMEM((2, 320, ROWS), BF16),
            pltpu.VMEM((ROWS, D), BF16),
            pltpu.VMEM((ROWS, D), F32),
            pltpu.VMEM((ROWS, D), F32),
            pltpu.VMEM((D, D), BF16),
        ],
        compiler_params=params(58),
        cost_estimate=cost(2 * ROWS * D * (24 * D + 3 * D), 62 * MB, 2 * ROWS * 4 * D),
        name="mlp",
    )(info, tok, cot, att, vecs, fc_bias, by_ctx, by_ctx, by_chip)


def ring_perm(axis):
    pairs = []
    for core in range(2):
        for pos in range(4):
            to = (pos + (1 if core == 0 else -1)) % 4
            if axis == "x":
                index = lambda p: p * 2 + core
            elif axis == "z":
                index = lambda p: core * 4 + p
            else:
                index = lambda p: ((p % 2) * 2 + core) * 2 + p // 2
            pairs.append((index(pos), index(to)))
    return {"x": ("x", "c"), "z": ("c", "z"), "y": ("yl", "c", "yh")}[axis], pairs


def swap_cores(array):
    return lax.ppermute(array, "c", [(0, 1), (1, 0)])


def shift_perm(axis, by):
    if axis != "y":
        return axis, [(p, (p + by) % 4) for p in range(4)]
    index = lambda p: (p % 2) * 2 + p // 2
    return ("yl", "yh"), [(index(p), index((p + by) % 4)) for p in range(4)]


class Sums:
    dims = {"z": 0, "y": 1, "x": 2}

    def __init__(self, colours):
        self.pieces = [pieces for pieces, _ in colours]
        self.orders = [order for _, order in colours]
        self.way = 1 - 2 * lax.axis_index("c")
        self.place = {
            "x": lax.axis_index("x"),
            "y": 2 * lax.axis_index("yh") + lax.axis_index("yl"),
            "z": lax.axis_index("z"),
        }
        self.phase = 0
        self.step = 0
        self.flight = None

    def local(self, colour, axis, block):
        parts = []
        for terms, first, last in self.pieces[colour]:
            total = None
            for term in terms:
                part = lax.dynamic_slice_in_dim(
                    term[..., first:last, :], block, 1, self.dims[axis]
                ).astype(F32)
                total = part if total is None else total + part
            parts.append(total)
        return parts[0] if len(parts) == 1 else jnp.concatenate(parts, axis=-2)

    def axes(self):
        return [order[self.phase] for order in self.orders]

    def start(self):
        if self.phase == 2:
            self.flight = [
                [
                    lax.ppermute(
                        self.local(k, a, (self.place[a] + by) % 4).astype(BF16),
                        *shift_perm(a, by),
                    )
                    for by in (1, 2, 3)
                ]
                for k, a in enumerate(self.axes())
            ]
            return
        if self.step == 0:
            self.sent = [
                self.local(k, a, (self.place[a] - self.way) % 4).astype(BF16)
                for k, a in enumerate(self.axes())
            ]
        self.flight = [
            lax.ppermute(self.sent[k], *ring_perm(a)) for k, a in enumerate(self.axes())
        ]

    def land(self):
        if self.phase == 2:
            return [
                (
                    self.local(k, a, self.place[a])
                    + sum(part.astype(F32) for part in self.flight[k])
                ).reshape(self.flight[k][0].shape[-2:])
                for k, a in enumerate(self.axes())
            ]
        self.sent = [
            (
                self.flight[k].astype(F32)
                + self.local(k, a, (self.place[a] - self.way * (2 + self.step)) % 4)
            ).astype(BF16)
            for k, a in enumerate(self.axes())
        ]
        self.step += 1
        if self.step == 3:
            self.pieces = [[([s], 0, s.shape[-2])] for s in self.sent]
            self.step, self.phase = 0, self.phase + 1
        return None

    def run(self):
        sums = None
        while sums is None:
            self.start()
            sums = self.land()
        return sums


def tie(first, second):
    return lax.optimization_barrier((first, second))


def per_device(
    tokens,
    lengths,
    cotangent,
    ln1_gain,
    ln1_bias,
    w_qkv,
    q_bias,
    v_bias,
    w_proj,
    proj_bias,
    ln2_gain,
    ln2_bias,
    w_fc,
    fc_bias,
    w_out,
    out_bias,
):
    ctx_rank = lax.axis_index(CTX)
    core = lax.axis_index("c")
    seq_rank = ctx_rank // 4
    head_group = ctx_rank % 4
    tok = tokens.reshape(ROWS, D)
    cot = cotangent.reshape(ROWS, D)

    def exchange(array):
        return lax.all_to_all(array, CTX, 0, 0, tiled=True)

    groups = w_qkv.reshape(10, 3, 4, GROUP_W).transpose(2, 0, 1, 3)
    groups = groups.reshape(4, 10, HEADS_W)
    vec_one = jnp.concatenate([ln1_gain, ln1_bias, q_bias, v_bias])
    vec_one = jnp.pad(vec_one[None, None], ((0, 0), (0, 0), (0, HEADS_W - 40)))
    groups = jnp.concatenate([groups, jnp.broadcast_to(vec_one, (4, 1, HEADS_W))], axis=1)
    groups = jnp.concatenate([groups, groups], axis=0)
    w_cols = w_fc.reshape(10, CTX_N, COLS).transpose(1, 0, 2)
    w_cols = jnp.pad(w_cols, ((0, 0), (0, 0), (0, HEADS_W - COLS)))
    shards = exchange(jnp.concatenate([groups, w_cols], axis=1))

    vec_two = jnp.concatenate([proj_bias, ln2_gain, ln2_bias, out_bias, fc_bias])
    vec_two = jnp.pad(vec_two[None], ((0, PIECE - 21), (0, COLS - 80)))
    part = jnp.concatenate(
        [
            shards[:, 11:, :COLS].reshape(BLK, COLS),
            w_out.reshape(40, 2, COLS).transpose(1, 0, 2).reshape(BLK, COLS),
            w_proj.reshape(10, 2, COLS).transpose(1, 0, 2).reshape(20, COLS),
            vec_two,
        ],
        axis=0,
    )
    part, shards = tie(part, shards)
    weights = lax.all_gather(part, PLACE, axis=0, tiled=False)

    w_group = jnp.concatenate(
        [shards[:, :10].reshape(BLK, HEADS_W), shards[:, 10]], axis=0
    )
    w_group = jnp.broadcast_to(w_group[None], (16, BLK + 8, HEADS_W))
    w_group = lax.all_to_all(w_group, DP, 0, 0, tiled=True)
    sequence = jnp.broadcast_to(tokens[:, None], (SEQ_GRP, 4, SPAN, D))
    w_group, sequence = tie(w_group, sequence)
    sequence = exchange(sequence.reshape(CTX_N, SPAN, D)).reshape(LEN, D)

    vecs = w_group[:, BLK:, :40].reshape(128, 4, 10).transpose(1, 0, 2)
    vecs = vecs.reshape(4, D).astype(F32)
    own = lax.dynamic_slice_in_dim(vecs[2:], head_group * GROUP_W, GROUP_W, 1)
    bias = jnp.concatenate([own[0:1], jnp.zeros((1, GROUP_W), F32), own[1:2]], axis=1)
    length = lax.dynamic_slice_in_dim(lengths, seq_rank, 1)
    qkv, att, lse = attend_call(length, sequence, vecs[:2], bias, w_group)
    att = exchange(att).reshape(SEQ_GRP, D, SPAN)

    more = weights[:, 2 * BLK + 20, :80].reshape(4, 2, 2, 4, 2, 80)
    more = more.transpose(3, 2, 4, 0, 1, 5).reshape(128, 80).astype(F32)
    fc_shift = more[:, 40:].reshape(1, 4 * D)
    more = more[:, :40].reshape(128, 4, 10).transpose(1, 0, 2).reshape(4, D)
    info = jnp.concatenate([lengths, jnp.stack([ctx_rank * SPAN, core]).astype(jnp.int32)])
    layer_out, g_res, g_att, d_vecs, d_fc_bias, *d_mats = mlp_call(
        info, tok, cot, att, more, fc_shift, weights
    )
    wp_keep, wp_give, wf_keep, wf_give, wo_keep, wo_give = d_mats

    given = [swap_cores(wf_give), swap_cores(wo_give), swap_cores(wp_give)]
    g_att = exchange(g_att.reshape(CTX_N, GROUP_W, SPAN))
    given, g_att = tie(given, g_att)
    sums = Sums(
        [
            ([([keep.reshape(4, 4, 4, -1, COLS), give.reshape(4, 4, 4, -1, COLS)], 0, rows)], order)
            for keep, give, rows, order in (
                (wf_keep, given[0], BLK, "xyz"),
                (wo_keep, given[1], BLK, "yzx"),
                (wp_keep, given[2], PIECE, "zxy"),
            )
        ]
    )
    sums.start()
    d_group, d_bias, g_norm = attend_back_call(
        length, sequence, vecs[:2], w_group, qkv, g_att, lse
    )
    sums.flight, g_norm = tie(sums.flight, g_norm)
    sums.land()
    sums.start()
    g_norm = exchange(g_norm)
    sums.flight, g_norm = tie(sums.flight, g_norm)
    sums.land()
    sums.start()
    input_grad, d_norm = norm_back_call(tok, vecs[:1], g_res, g_norm)

    d_heads = jnp.zeros((2, D), F32)
    d_heads = lax.dynamic_update_slice(
        d_heads,
        jnp.concatenate([d_bias[:1, :GROUP_W], d_bias[:1, 2 * GROUP_W :]], axis=0),
        (0, head_group * GROUP_W),
    )
    d_small = jnp.concatenate([d_norm, d_heads, d_vecs], axis=0)
    d_small = d_small.reshape(8, 128, 10).transpose(1, 0, 2).reshape(128, 80)
    d_small = jnp.concatenate([d_small, d_fc_bias.reshape(128, 40)], axis=1)
    d_small = jnp.pad(
        d_small.reshape(16, 8, 120).astype(BF16), ((0, 0), (0, 0), (0, HEADS_W - 120))
    )
    d_group = jnp.concatenate([d_group, d_small], axis=1)
    d_group = lax.all_to_all(d_group, DP, 0, 0, tiled=True)
    sums.flight, d_group = tie(sums.flight, d_group)
    sums.land()
    d_group = jnp.sum(d_group.astype(F32), axis=0).astype(BF16)
    d_group = jnp.concatenate(
        [d_group[:BLK].reshape(CTX_N, 10, HEADS_W), d_group[BLK:, None]], axis=1
    )
    d_group = exchange(d_group).astype(F32)
    d_qkv = (d_group[:4, :10] + d_group[4:, :10]).reshape(4, 10, 3, GROUP_W)
    d_qkv = d_qkv.transpose(1, 2, 0, 3).reshape(10, 3 * D)
    small = jnp.sum(d_group[:, 10, :120], axis=0)

    wf_sum, wo_sum, wp_sum = sums.run()
    d_fc = exchange(wf_sum.astype(BF16).reshape(CTX_N, 10, COLS))
    d_fc = d_fc.transpose(1, 0, 2).reshape(10, CTX_N * COLS).astype(F32)
    d_out = wo_sum.reshape(2, 40, COLS).transpose(1, 0, 2).reshape(40, D)
    d_proj = wp_sum[:20].reshape(2, 10, COLS).transpose(1, 0, 2).reshape(10, D)
    names = ["g1", "b1", "q", "v", "proj", "g2", "b2", "out"]
    vec = {n: small[10 * k : 10 * (k + 1)] for k, n in enumerate(names)}

    return (
        layer_out.reshape(tokens.shape),
        input_grad.reshape(tokens.shape),
        vec["g1"],
        vec["b1"],
        d_qkv,
        vec["q"],
        vec["v"],
        d_proj,
        vec["proj"],
        vec["g2"],
        vec["b2"],
        d_fc,
        small[80:120],
        d_out,
        vec["out"],
    )


def solution(mesh):
    fine = Mesh(mesh.devices.reshape(SIZES), AXES)
    rows = P(DP, CTX, None)
    mat = P(AXES, None)
    vec = P(AXES)
    in_specs = (
        rows,
        P(DP),
        rows,
        vec,
        vec,
        mat,
        vec,
        vec,
        mat,
        vec,
        vec,
        vec,
        mat,
        vec,
        mat,
        vec,
    )
    out_specs = (
        rows,
        rows,
        vec,
        vec,
        mat,
        vec,
        vec,
        mat,
        vec,
        vec,
        vec,
        mat,
        vec,
        mat,
        vec,
    )
    return jax.shard_map(
        per_device, mesh=fine, in_specs=in_specs, out_specs=out_specs, check_vma=False
    )
```

time: 637 us -> 518 us (0.81)
  waiting for transfers between devices: 353 us -> 180 us
  starting transfers between devices: 42.8 us -> 86.1 us
  local copies, waits for them, and re-layouts: 53.6 us -> 27.6 us
  blocking collectives: 19.8 us -> 45.8 us
  Pallas kernels: 88.5 us -> 95.8 us
    all_gather x2 -> x1, waiting for transfers between devices: 106 us -> 0.01 us  [per_device(): weights = lax.all_gather(part, PLACE, axis=0, tiled=False)]
    ppermute x45 -> x27, waiting for transfers between devices: 156 us -> 78.3 us  [the longest x18 77.6 us: start(): lax.ppermute(self.sent[k], *ring_perm(a))]
    ppermute x45 -> x27, starting transfers between devices: 7.8 us -> 46.6 us  [the longest x18 33.5 us: start(): lax.ppermute(self.sent[k], *ring_perm(a))]
    all_to_all x3 -> x7, waiting for transfers between devices: 64.1 us -> 96.1 us  [exchange(): return lax.all_to_all(array, CTX, 0, 0, tiled=True)]
    all_to_all x4 -> x1, waiting for transfers between devices: 26.4 us -> 0.01 us  [per_device(): d_group = lax.all_to_all(d_group, DP, 0, 0, tiled=True)]
    all_to_all x1, blocking collectives: 19.8 us -> 45.8 us  [per_device(): w_group = lax.all_to_all(w_group, DP, 0, 0, tiled=True)]
    all_to_all x3 -> x7, starting transfers between devices: 15.1 us -> 35 us  [exchange(): return lax.all_to_all(array, CTX, 0, 0, tiled=True)]
    pallas_call x2 -> x1, Pallas kernels: 20.1 us -> 2.38 us  [norm_back_call(): pl.pallas_call(norm_back_kernel, out_shape=[jax.ShapeDtypeStruct((ROWS, D...]
  transfers between devices with their start and end apart: 59 -> 39, of which waited for: 41 -> 15; matrix products, arithmetic and copies ran while one was open for 12% -> 13% of each run, Pallas kernels for 3% -> 9%
where the time goes in v2:
time: 518 us; the launch traced here: 509 us
  waiting for transfers between devices  180 us (35%)
  Pallas kernels  95.8 us (18%)
  starting transfers between devices  86.1 us (17%)
  other arithmetic  58.2 us (11%)
  blocking collectives  45.8 us (9%)
  local copies, waits for them, and re-layouts  27.6 us (5%)
  between operations  15.3 us (3%)
    all_to_all x7, waiting for transfers between devices, exchange(): return lax.all_to_all(array, CTX, 0, 0, tiled=True)  96.1 us
    ppermute x18, waiting for transfers between devices, start(): lax.ppermute(self.sent[k], *ring_perm(a))  77.6 us
    pallas_call x1, Pallas kernels, mlp_call(): pl.pallas_call(mlp_kernel, grid=(8,), in_specs=[pl.BlockSpec(memory_space...  46.6 us
    all_to_all x1, blocking collectives, per_device(): w_group = lax.all_to_all(w_group, DP, 0, 0, tiled=True)  45.8 us
    convert_element_type x18, other arithmetic, land(): self.sent = [(self.flight[k].astype(F32) + self.local(k, a, (self.place[a...  39 us
    all_to_all x7, starting transfers between devices, exchange(): return lax.all_to_all(array, CTX, 0, 0, tiled=True)  35 us
    ppermute x18, starting transfers between devices, start(): lax.ppermute(self.sent[k], *ring_perm(a))  33.5 us
    pallas_call x1, Pallas kernels, attend_back_call(): pl.pallas_call(attend_back_kernel, grid=(GROUP_HEADS,), in_specs=[pl.Bloc...  28.4 us
  transfers between devices with their start and end apart: 39, of which 15 were waited for; matrix products, arithmetic and copies ran while one was open for 13% of the time, Pallas kernels for 9%

profile of v2, /device:TPU:0, one launch (start us, length us, event | category | flops | bytes accessed | tf_op | source)
XLA Modules:
  0.0 509.3 jit_solution(14755389671331236234)
XLA Ops:
  11.4 8.0 %all-to-all-start = ((bf16[8,21,960]{2,1,0:T(8,128)(2,1)}), bf16[8,21,960]{2,1,0:T(8,128)(2,1)S(1)}, u32[]{:S(2)}, u32[]{:S(2)}) async-start(bf16[8,21,960]{2,1,0:T(8,128)(2,1)} %copy.73), calls=%async_computation | async-start | bytes 786432 | tf_op jit(solution)/shard_map/all_to_all | solution.py:678
  19.7 9.9 %all-to-all-done = bf16[8,21,960]{2,1,0:T(8,128)(2,1)S(1)} async-done(((bf16[8,21,960]{2,1,0:T(8,128)(2,1)}), bf16[8,21,960]{2,1,0:T(8,128)(2,1)S(1)}, u32[]{:S(2)}, u32[]{:S(2)}) %all-to-all-start) | async-done | bytes 322592 | tf_op jit(solution)/shard_map/all_to_all | solution.py:678
  31.2 45.8 %all_to_all.45.w_ref = bf16[16,88,960]{2,1,0:T(8,128)(2,1)S(1)} all-to-all(bf16[16,88,960]{2,1,0:T(8,128)(2,1)S(1)} %broadcast_in_dim.38), channel_id=1, replica_groups=mesh['x'=4,'yl'=2,'c'=2,'z'=4,'yh'=2] {'x','yl','c'}, dimensions={0} | all-to-all | bytes 5406720 | tf_op jit(solution)/shard_map/all_to_all | solution.py:708
  78.9 4.5 all-to-all-start.2
  86.0 54.3 %all-to-all-done.2 = bf16[8,128,1280]{2,1,0:T(8,128)(2,1)} async-done(((bf16[8,128,1280]{2,1,0:T(8,128)(2,1)}), bf16[8,128,1280]{2,1,0:T(8,128)(2,1)}, u32[]{:S(2)}, u32[]{:S(2)}) %all-to-all-start.2) | async-done | bytes 2621472 | tf_op jit(solution)/shard_map/all_to_all | solution.py:678
  140.3 18.5 %attend.1 = (bf16[3,5,64,1024]{3,2,1,0:T(8,128)(2,1)}, bf16[8,320,128]{2,1,0:T(8,128)(2,1)}, f32[5,1,1024]{2,1,0:T(1,128)}) custom-call(s32[1]{0:T(128)} %dynamic_slice.150.len_ref, bf16[1024,1280]{1,0:T(8,128)(2,1)} %bitcast.13.tok_ref, f32[2,1280]{1,0:T(2,128)} %slice.103.norm_ref, f32[1,960]{1,0:T(1,128)} %pad_maximum_fusion.4.bias_ref, ...), custom_call_target="tpu_custom_call" | custom-call | flops 4127195136 | bytes 8388608 | tf_op jit(solution)/shard_map/attend/pallas_call | solution.py:141
  158.9 3.5 all-to-all-start.3
  165.9 10.8 %all-to-all-done.3 = bf16[8,320,128]{2,1,0:T(8,128)(2,1)S(1)} async-done(((bf16[8,320,128]{2,1,0:T(8,128)(2,1)}), bf16[8,320,128]{2,1,0:T(8,128)(2,1)S(1)}, u32[]{:S(2)}, u32[]{:S(2)}) %all-to-all-start.3) | async-done | bytes 655392 | tf_op jit(solution)/shard_map/all_to_all | solution.py:678
  177.5 46.6 %mlp.1 = (bf16[256,1280]{1,0:T(8,128)(2,1)}, bf16[256,1280]{1,0:T(8,128)(2,1)}, bf16[2,1280,128]{2,1,0:T(8,128)(2,1)}, f32[4,1280]{1,0:T(4,128)}, f32[1,5120]{1,...) custom-call(s32[4]{0:T(128)} %pad_add_fusion.info_ref, ...), custom_call_target="tpu_custom_call" | custom-call | flops 22649241600 | bytes 65011712 | tf_op jit(solution)/shard_map/mlp/pallas_call | solution.py:480
  224.8 3.5 all-to-all-start.4
  228.4 13.7 %all-to-all-done.4.grad_ref = bf16[8,320,128]{2,1,0:T(8,128)(2,1)S(1)} async-done(((bf16[8,320,128]{2,1,0:T(8,128)(2,1)}), bf16[8,320,128]{2,1,0:T(8,128)(2,1)S(1)}, u32[]{:S(2)}, u32[]{:S(2)}) %all-to-all-start.4) | async-done | bytes 655392 | tf_op jit(solution)/shard_map/all_to_all | solution.py:678
  242.2 6.0 %collective-permute-done.1 = bf16[4,2,2,4,2,40,640]{6,5,4,3,2,1,0:T(8,128)(2,1)} collective-permute-done((bf16[4,2,2,4,2,40,640]{6,5,4,3,2,1,0:T(8,128)(2,1)}, bf16[4,2,2,4,2,40,640]{6,5,4,3,2,1,0:T(8,128)(2,1)}, u32[]{:S(2)}, u32[]{:S(2)}) %collective-permute-start.1) | collective-permute-done | bytes 6553632 | tf_op jit(solution)/shard_map/ppermute | solution.py:555
  248.2 3.5 add_convert_fusion.7
  251.7 3.5 add_convert_fusion.6
  259.9 8.9 %collective-permute-start.5 = (bf16[1,4,4,32,640]{4,3,2,1,0:T(8,128)(2,1)S(1)}, bf16[1,4,4,32,640]{4,3,2,1,0:T(8,128)(2,1)S(1)}, u32[]{:S(2)}, u32[]{:S(2)}) collective-permute-start(bf16[1,4,4,32,640]{4,3,2,1,0:T(8,128)(2,1)S(1)} %add_convert_fusion.11), channel_id=1, source_target_pairs={{0,2},{2,4},{4,6},{6,0},{8,14},{10,8},{12,10},{14,12},{1,3},{3,5},... | collective-permute-start | bytes 1966088 | tf_op jit(solution)/shard_map/ppermute | solution.py:615
  268.8 28.4 %attend_back.1 = (bf16[16,80,960]{2,1,0:T(8,128)(2,1)}, f32[8,960]{1,0:T(8,128)}, bf16[8,128,1280]{2,1,0:T(8,128)(2,1)}) custom-call(s32[1]{0:T(128)} %dynamic_slice.150.len_ref, bf16[1024,1280]{1,0:T(8,128)(2,1)} %bitcast.13.tok_ref, f32[2,1280]{1,0:T(2,128)} %slice.103.norm_ref, bf16[16,88,960]{2,1,0:T(8,128)(2,1)} %copy-done.3, ...), custom_call_target="tpu_custom_call" | custom-call | flops 9059696640 | bytes 16777216 | tf_op jit(solution)/shard_map/attend_back/pallas_call | solution.py:246
  298.0 5.4 %all-to-all-start.5 = ((bf16[8,128,1280]{2,1,0:T(8,128)(2,1)}), bf16[8,128,1280]{2,1,0:T(8,128)(2,1)S(1)}, u32[]{:S(2)}, u32[]{:S(2)}) async-start(bf16[8,128,1280]{2,1,0:T(8,128)(2,1)} %get-tuple-element.78), calls=%async_computation.5 | async-start | bytes 5242880 | tf_op jit(solution)/shard_map/all_to_all | solution.py:678
  303.4 4.3 add_convert_fusion.4
  307.6 4.2 add_convert_fusion.5
  321.0 20.8 %collective-permute-done.8 = bf16[1,4,4,32,640]{4,3,2,1,0:T(8,128)(2,1)} collective-permute-done((bf16[1,4,4,32,640]{4,3,2,1,0:T(8,128)(2,1)}, bf16[1,4,4,32,640]{4,3,2,1,0:T(8,128)(2,1)}, u32[]{:S(2)}, u32[]{:S(2)}) %collective-permute-start.8) | collective-permute-done | bytes 655392 | tf_op jit(solution)/shard_map/ppermute | solution.py:615
  341.8 10.5 %collective-permute-done.7 = bf16[4,1,4,80,640]{4,3,2,1,0:T(8,128)(2,1)} collective-permute-done((bf16[4,1,4,80,640]{4,3,2,1,0:T(8,128)(2,1)}, bf16[4,1,4,80,640]{4,3,2,1,0:T(8,128)(2,1)}, u32[]{:S(2)}, u32[]{:S(2)}) %collective-permute-start.7) | collective-permute-done | bytes 1638432 | tf_op jit(solution)/shard_map/ppermute | solution.py:615
  356.8 3.8 pad_maximum_fusion
  360.6 3.7 all-to-all-start.6
  364.4 4.3 add_convert_fusion.2
  370.4 4.2 add_convert_fusion.3
  380.2 10.5 %collective-permute-done.11 = bf16[1,4,4,32,640]{4,3,2,1,0:T(8,128)(2,1)S(1)} collective-permute-done((bf16[1,4,4,32,640]{4,3,2,1,0:T(8,128)(2,1)}, bf16[1,4,4,32,640]{4,3,2,1,0:T(8,128)(2,1)S(1)}, u32[]{:S(2)}, u32[]{:S(2)}) %collective-permute-start.11) | collective-permute-done | bytes 655392 | tf_op jit(solution)/shard_map/ppermute | solution.py:615
  390.7 23.1 %collective-permute-done.10 = bf16[4,1,4,80,640]{4,3,2,1,0:T(8,128)(2,1)} collective-permute-done((bf16[4,1,4,80,640]{4,3,2,1,0:T(8,128)(2,1)}, bf16[4,1,4,80,640]{4,3,2,1,0:T(8,128)(2,1)}, u32[]{:S(2)}, u32[]{:S(2)}) %collective-permute-start.10) | collective-permute-done | bytes 1638432 | tf_op jit(solution)/shard_map/ppermute | solution.py:615
  418.7 5.1 %all-to-all-start.7 = ((bf16[8,11,960]{2,1,0:T(8,128)(2,1)}), bf16[8,11,960]{2,1,0:T(8,128)(2,1)S(1)}, u32[]{:S(2)}, u32[]{:S(2)}) async-start(bf16[8,11,960]{2,1,0:T(8,128)(2,1)} %pad_maximum_fusion.1), calls=%async_computation.7 | async-start | bytes 524288 | tf_op jit(solution)/shard_map/all_to_all | solution.py:678
  448.0 3.8 collective-permute-done.13
  471.1 4.6 collective-permute-done.20
  488.0 4.8 all-to-all-start.8
  493.7 7.4 %all-to-all-done.8 = bf16[8,10,640]{2,1,0:T(8,128)(2,1)S(1)} async-done(((bf16[8,10,640]{2,1,0:T(8,128)(2,1)}), bf16[8,10,640]{2,1,0:T(8,128)(2,1)S(1)}, u32[]{:S(2)}, u32[]{:S(2)}) %all-to-all-start.8) | async-done | bytes 102432 | tf_op jit(solution)/shard_map/all_to_all | solution.py:678
  (206 shorter events, 103.9 us)
Async XLA Ops:
  11.4 18.2 %all-to-all-start = ((bf16[8,21,960]{2,1,0:T(8,128)(2,1)}), bf16[8,21,960]{2,1,0:T(8,128)(2,1)S(1)}, u32[]{:S(2)}, u32[]{:S(2)}) async-start(bf16[8,21,960]{2,1,0:T(8,128)(2,1)} %copy.73), calls=%async_computation | async-start | bytes 786432 | tf_op jit(solution)/shard_map/all_to_all | solution.py:678
  19.4 143.6 %all-gather.3.cloned.1.call-start = ((), (), s32[]{:S(2)}) async-start(), calls=%async_computation.9 | async-start | bytes 31703040 | tf_op jit(solution)/shard_map/all_gather | solution.py:702
  78.9 61.5 %all-to-all-start.2 = ((bf16[8,128,1280]{2,1,0:T(8,128)(2,1)}), bf16[8,128,1280]{2,1,0:T(8,128)(2,1)}, u32[]{:S(2)}, u32[]{:S(2)}) async-start(bf16[8,128,1280]{2,1,0:T(8,128)(2,1)} %bitcast.12), calls=%async_computation.2 | async-start | bytes 5242880 | tf_op jit(solution)/shard_map/all_to_all | solution.py:678
  158.9 17.8 %all-to-all-start.3 = ((bf16[8,320,128]{2,1,0:T(8,128)(2,1)}), bf16[8,320,128]{2,1,0:T(8,128)(2,1)S(1)}, u32[]{:S(2)}, u32[]{:S(2)}) async-start(bf16[8,320,128]{2,1,0:T(8,128)(2,1)} %get-tuple-element.57), calls=%async_computation.3 | async-start | bytes 1310720 | tf_op jit(solution)/shard_map/all_to_all | solution.py:678
  224.1 18.1 %collective-permute-start = (bf16[8,8,80,640]{3,2,1,0:T(8,128)(2,1)}, bf16[8,8,80,640]{3,2,1,0:T(8,128)(2,1)}, u32[]{:S(2)}, u32[]{:S(2)}) collective-permute-start(bf16[8,8,80,640]{3,2,1,0:T(8,128)(2,1)} %get-tuple-element.62), channel_id=1, source_target_pairs={{0,8},{8,0},{1,9},{9,1},{2,10},{10,2},{3,11},{11,3},{4,12},{12,4},... | collective-permute-start | bytes 19660808 | tf_op jit(solution)/shard_map/ppermute | solution.py:555
  224.3 23.9 %collective-permute-start.1 = (bf16[4,2,2,4,2,40,640]{6,5,4,3,2,1,0:T(8,128)(2,1)}, bf16[4,2,2,4,2,40,640]{6,5,4,3,2,1,0:T(8,128)(2,1)}, u32[]{:S(2)}, u32[]{:S(2)}) collective-permute-start(bf16[4,2,2,4,2,40,640]{6,5,4,3,2,1,0:T(8,128)(2,1)} %get-tuple-element.63), channel_id=1, source_target_pairs={{0,8},{8,0},{1,9},{9,1},{2,10},{10,2},{3,11},{11,3},{4,12},{12,4},... | collective-permute-start | bytes 19660808 | tf_op jit(solution)/shard_map/ppermute | solution.py:555
  224.7 17.5 %collective-permute-start.2 = (bf16[8,8,32,640]{3,2,1,0:T(8,128)(2,1)}, bf16[8,8,32,640]{3,2,1,0:T(8,128)(2,1)S(1)}, u32[]{:S(2)}, u32[]{:S(2)}) collective-permute-start(bf16[8,8,32,640]{3,2,1,0:T(8,128)(2,1)} %get-tuple-element.64), channel_id=1, source_target_pairs={{0,8},{8,0},{1,9},{9,1},{2,10},{10,2},{3,11},{11,3},{4,12},{12,4},... | collective-permute-start | bytes 7864328 | tf_op jit(solution)/shard_map/ppermute | solution.py:555
  224.8 17.3 %all-to-all-start.4 = ((bf16[8,320,128]{2,1,0:T(8,128)(2,1)}), bf16[8,320,128]{2,1,0:T(8,128)(2,1)S(1)}, u32[]{:S(2)}, u32[]{:S(2)}) async-start(bf16[8,320,128]{2,1,0:T(8,128)(2,1)} %bitcast.105), calls=%async_computation.4 | async-start | bytes 1310720 | tf_op jit(solution)/shard_map/all_to_all | solution.py:678
  251.7 46.3 %collective-permute-start.3 = (bf16[4,4,1,80,640]{4,3,2,1,0:T(8,128)(2,1)}, bf16[4,4,1,80,640]{4,3,2,1,0:T(8,128)(2,1)}, u32[]{:S(2)}, u32[]{:S(2)}) collective-permute-start(bf16[4,4,1,80,640]{4,3,2,1,0:T(8,128)(2,1)} %add_convert_fusion.7), channel_id=1, source_target_pairs={{0,32},{32,64},{64,96},{96,0},{8,104},{40,8},{72,40},{104,72},{1,3... | collective-permute-start | bytes 4915208 | tf_op jit(solution)/shard_map/ppermute | solution.py:615
  255.2 42.8 %collective-permute-start.4 = (bf16[4,1,4,80,640]{4,3,2,1,0:T(8,128)(2,1)}, bf16[4,1,4,80,640]{4,3,2,1,0:T(8,128)(2,1)}, u32[]{:S(2)}, u32[]{:S(2)}) collective-permute-start(bf16[4,1,4,80,640]{4,3,2,1,0:T(8,128)(2,1)} %add_convert_fusion.6), channel_id=1, source_target_pairs={{0,16},{16,1},{1,17},{17,0},{8,25},{24,8},{9,24},{25,9},{2,18},{18... | collective-permute-start | bytes 4915208 | tf_op jit(solution)/shard_map/ppermute | solution.py:615
  259.9 37.3 %collective-permute-start.5 = (bf16[1,4,4,32,640]{4,3,2,1,0:T(8,128)(2,1)S(1)}, bf16[1,4,4,32,640]{4,3,2,1,0:T(8,128)(2,1)S(1)}, u32[]{:S(2)}, u32[]{:S(2)}) collective-permute-start(bf16[1,4,4,32,640]{4,3,2,1,0:T(8,128)(2,1)S(1)} %add_convert_fusion.11), channel_id=1, source_target_pairs={{0,2},{2,4},{4,6},{6,0},{8,14},{10,8},{12,10},{14,12},{1,3},{3,5},... | collective-permute-start | bytes 1966088 | tf_op jit(solution)/shard_map/ppermute | solution.py:615
  298.0 54.3 %all-to-all-start.5 = ((bf16[8,128,1280]{2,1,0:T(8,128)(2,1)}), bf16[8,128,1280]{2,1,0:T(8,128)(2,1)S(1)}, u32[]{:S(2)}, u32[]{:S(2)}) async-start(bf16[8,128,1280]{2,1,0:T(8,128)(2,1)} %get-tuple-element.78), calls=%async_computation.5 | async-start | bytes 5242880 | tf_op jit(solution)/shard_map/all_to_all | solution.py:678
  307.6 44.6 %collective-permute-start.7 = (bf16[4,1,4,80,640]{4,3,2,1,0:T(8,128)(2,1)}, bf16[4,1,4,80,640]{4,3,2,1,0:T(8,128)(2,1)}, u32[]{:S(2)}, u32[]{:S(2)}) collective-permute-start(bf16[4,1,4,80,640]{4,3,2,1,0:T(8,128)(2,1)} %add_convert_fusion.4), channel_id=1, source_target_pairs={{0,16},{16,1},{1,17},{17,0},{8,25},{24,8},{9,24},{25,9},{2,18},{18... | collective-permute-start | bytes 4915208 | tf_op jit(solution)/shard_map/ppermute | solution.py:615
  311.8 40.4 %collective-permute-start.6 = (bf16[4,4,1,80,640]{4,3,2,1,0:T(8,128)(2,1)}, bf16[4,4,1,80,640]{4,3,2,1,0:T(8,128)(2,1)}, u32[]{:S(2)}, u32[]{:S(2)}) collective-permute-start(bf16[4,4,1,80,640]{4,3,2,1,0:T(8,128)(2,1)} %add_convert_fusion.5), channel_id=1, source_target_pairs={{0,32},{32,64},{64,96},{96,0},{8,104},{40,8},{72,40},{104,72},{1,3... | collective-permute-start | bytes 4915208 | tf_op jit(solution)/shard_map/ppermute | solution.py:615
  314.6 27.1 %collective-permute-start.8 = (bf16[1,4,4,32,640]{4,3,2,1,0:T(8,128)(2,1)}, bf16[1,4,4,32,640]{4,3,2,1,0:T(8,128)(2,1)}, u32[]{:S(2)}, u32[]{:S(2)}) collective-permute-start(bf16[1,4,4,32,640]{4,3,2,1,0:T(8,128)(2,1)} %add_convert_fusion.10), channel_id=1, source_target_pairs={{0,2},{2,4},{4,6},{6,0},{8,14},{10,8},{12,10},{14,12},{1,3},{3,5},... | collective-permute-start | bytes 1966088 | tf_op jit(solution)/shard_map/ppermute | solution.py:615
  360.6 56.6 %all-to-all-start.6 = ((bf16[16,88,960]{2,1,0:T(8,128)(2,1)}), bf16[16,88,960]{2,1,0:T(8,128)(2,1)S(1)}, u32[]{:S(2)}, u32[]{:S(2)}) async-start(bf16[16,88,960]{2,1,0:T(8,128)(2,1)} %pad_maximum_fusion), calls=%async_computation.6 | async-start | bytes 5767168 | tf_op jit(solution)/shard_map/all_to_all | solution.py:770
  368.7 45.1 %collective-permute-start.10 = (bf16[4,1,4,80,640]{4,3,2,1,0:T(8,128)(2,1)}, bf16[4,1,4,80,640]{4,3,2,1,0:T(8,128)(2,1)}, u32[]{:S(2)}, u32[]{:S(2)}) collective-permute-start(bf16[4,1,4,80,640]{4,3,2,1,0:T(8,128)(2,1)} %add_convert_fusion.2), channel_id=1, source_target_pairs={{0,16},{16,1},{1,17},{17,0},{8,25},{24,8},{9,24},{25,9},{2,18},{18... | collective-permute-start | bytes 4915208 | tf_op jit(solution)/shard_map/ppermute | solution.py:615
  374.6 42.6 %collective-permute-start.9 = (bf16[4,4,1,80,640]{4,3,2,1,0:T(8,128)(2,1)}, bf16[4,4,1,80,640]{4,3,2,1,0:T(8,128)(2,1)}, u32[]{:S(2)}, u32[]{:S(2)}) collective-permute-start(bf16[4,4,1,80,640]{4,3,2,1,0:T(8,128)(2,1)} %add_convert_fusion.3), channel_id=1, source_target_pairs={{0,32},{32,64},{64,96},{96,0},{8,104},{40,8},{72,40},{104,72},{1,3... | collective-permute-start | bytes 4915208 | tf_op jit(solution)/shard_map/ppermute | solution.py:615
  378.7 12.0 %collective-permute-start.11 = (bf16[1,4,4,32,640]{4,3,2,1,0:T(8,128)(2,1)}, bf16[1,4,4,32,640]{4,3,2,1,0:T(8,128)(2,1)S(1)}, u32[]{:S(2)}, u32[]{:S(2)}) collective-permute-start(bf16[1,4,4,32,640]{4,3,2,1,0:T(8,128)(2,1)} %add_convert_fusion.9), channel_id=1, source_target_pairs={{0,2},{2,4},{4,6},{6,0},{8,14},{10,8},{12,10},{14,12},{1,3},{3,5},... | collective-permute-start | bytes 1966088 | tf_op jit(solution)/shard_map/ppermute | solution.py:615
  418.7 19.2 %all-to-all-start.7 = ((bf16[8,11,960]{2,1,0:T(8,128)(2,1)}), bf16[8,11,960]{2,1,0:T(8,128)(2,1)S(1)}, u32[]{:S(2)}, u32[]{:S(2)}) async-start(bf16[8,11,960]{2,1,0:T(8,128)(2,1)} %pad_maximum_fusion.1), calls=%async_computation.7 | async-start | bytes 524288 | tf_op jit(solution)/shard_map/all_to_all | solution.py:678
  426.5 16.5 %collective-permute-start.12 = (bf16[1,4,1,32,640]{4,3,2,1,0:T(8,128)(2,1)}, bf16[1,4,1,32,640]{4,3,2,1,0:T(8,128)(2,1)}, u32[]{:S(2)}, u32[]{:S(2)}) collective-permute-start(bf16[1,4,1,32,640]{4,3,2,1,0:T(8,128)(2,1)} %constant_dynamic-slice_fusion.10), channel_id=1, source_target_pairs={{0,32},{32,64},{64,96},{96,0},{8,104},{40,8},{72,40},{104,72},{1,3... | collective-permute-start | bytes 491528 | tf_op jit(solution)/shard_map/ppermute | solution.py:615
  432.1 25.7 %collective-permute-start.24 = (bf16[1,1,4,80,640]{4,3,2,1,0:T(8,128)(2,1)}, bf16[1,1,4,80,640]{4,3,2,1,0:T(8,128)(2,1)}, u32[]{:S(2)}, u32[]{:S(2)}) collective-permute-start(bf16[1,1,4,80,640]{4,3,2,1,0:T(8,128)(2,1)} %constant_dynamic-slice_fusion.1), channel_id=1, source_target_pairs={{0,2},{2,4},{4,6},{6,0},{8,14},{10,8},{12,10},{14,12},{1,3},{3,5},... | collective-permute-start | bytes 1228808 | tf_op jit(solution)/shard_map/ppermute | solution.py:615
  437.9 15.8 %collective-permute-start.18 = (bf16[4,1,1,80,640]{4,3,2,1,0:T(8,128)(2,1)}, bf16[4,1,1,80,640]{4,3,2,1,0:T(8,128)(2,1)}, u32[]{:S(2)}, u32[]{:S(2)}) collective-permute-start(bf16[4,1,1,80,640]{4,3,2,1,0:T(8,128)(2,1)} %constant_dynamic-slice_fusion.6), channel_id=1, source_target_pairs={{0,16},{16,1},{1,17},{17,0},{8,25},{24,8},{9,24},{25,9},{2,18},{18... | collective-permute-start | bytes 1228808 | tf_op jit(solution)/shard_map/ppermute | solution.py:615
  454.8 10.6 %collective-permute-start.19 = (bf16[4,1,1,80,640]{4,3,2,1,0:T(8,128)(2,1)S(1)}, bf16[4,1,1,80,640]{4,3,2,1,0:T(8,128)(2,1)S(1)}, u32[]{:S(2)}, u32[]{:S(2)}) collective-permute-start(bf16[4,1,1,80,640]{4,3,2,1,0:T(8,128)(2,1)S(1)} %add_convert_fusion.17), channel_id=1, source_target_pairs={{0,16},{16,1},{1,17},{17,0},{8,25},{24,8},{9,24},{25,9},{2,18},{18... | collective-permute-start | bytes 1228808 | tf_op jit(solution)/shard_map/ppermute | solution.py:615
  458.9 9.2 %collective-permute-start.25 = (bf16[1,1,4,80,640]{4,3,2,1,0:T(8,128)(2,1)S(1)}, bf16[1,1,4,80,640]{4,3,2,1,0:T(8,128)(2,1)S(1)}, u32[]{:S(2)}, u32[]{:S(2)}) collective-permute-start(bf16[1,1,4,80,640]{4,3,2,1,0:T(8,128)(2,1)S(1)} %add_convert_fusion.14), channel_id=1, source_target_pairs={{0,2},{2,4},{4,6},{6,0},{8,14},{10,8},{12,10},{14,12},{1,3},{3,5},... | collective-permute-start | bytes 1228808 | tf_op jit(solution)/shard_map/ppermute | solution.py:615
  466.3 9.5 %collective-permute-start.20 = (bf16[4,1,1,80,640]{4,3,2,1,0:T(8,128)(2,1)}, bf16[4,1,1,80,640]{4,3,2,1,0:T(8,128)(2,1)}, u32[]{:S(2)}, u32[]{:S(2)}) collective-permute-start(bf16[4,1,1,80,640]{4,3,2,1,0:T(8,128)(2,1)} %add_convert_fusion.16), channel_id=1, source_target_pairs={{0,16},{16,1},{1,17},{17,0},{8,25},{24,8},{9,24},{25,9},{2,18},{18... | collective-permute-start | bytes 1228808 | tf_op jit(solution)/shard_map/ppermute | solution.py:615
  469.0 12.7 %collective-permute-start.26 = (bf16[1,1,4,80,640]{4,3,2,1,0:T(8,128)(2,1)}, bf16[1,1,4,80,640]{4,3,2,1,0:T(8,128)(2,1)}, u32[]{:S(2)}, u32[]{:S(2)}) collective-permute-start(bf16[1,1,4,80,640]{4,3,2,1,0:T(8,128)(2,1)} %add_convert_fusion.13), channel_id=1, source_target_pairs={{0,2},{2,4},{4,6},{6,0},{8,14},{10,8},{12,10},{14,12},{1,3},{3,5},... | collective-permute-start | bytes 1228808 | tf_op jit(solution)/shard_map/ppermute | solution.py:615
  476.9 9.2 %collective-permute-start.21 = (bf16[1,1,1,80,640]{4,3,2,1,0:T(8,128)(2,1)S(1)}, bf16[1,1,1,80,640]{4,3,2,1,0:T(8,128)(2,1)S(1)}, u32[]{:S(2)}, u32[]{:S(2)}) collective-permute-start(bf16[1,1,1,80,640]{4,3,2,1,0:T(8,128)(2,1)S(1)} %get-tuple-element.96), channel_id=1, source_target_pairs={{0,2},{2,4},{4,6},{6,0},{1,3},{3,5},{5,7},{7,1},{8,10},{10,12},{12... | collective-permute-start | bytes 307208 | tf_op jit(solution)/shard_map/ppermute | solution.py:600
  478.5 8.8 %collective-permute-start.23 = (bf16[1,1,1,80,640]{4,3,2,1,0:T(8,128)(2,1)S(1)}, bf16[1,1,1,80,640]{4,3,2,1,0:T(8,128)(2,1)S(1)}, u32[]{:S(2)}, u32[]{:S(2)}) collective-permute-start(bf16[1,1,1,80,640]{4,3,2,1,0:T(8,128)(2,1)S(1)} %get-tuple-element.97), channel_id=1, source_target_pairs={{0,6},{2,0},{4,2},{6,4},{1,7},{3,1},{5,3},{7,5},{8,14},{10,8},{12,... | collective-permute-start | bytes 307208 | tf_op jit(solution)/shard_map/ppermute | solution.py:600
  482.9 9.9 %collective-permute-start.27 = (bf16[1,1,1,80,640]{4,3,2,1,0:T(8,128)(2,1)S(1)}, bf16[1,1,1,80,640]{4,3,2,1,0:T(8,128)(2,1)S(1)}, u32[]{:S(2)}, u32[]{:S(2)}) collective-permute-start(bf16[1,1,1,80,640]{4,3,2,1,0:T(8,128)(2,1)S(1)} %get-tuple-element.93), channel_id=1, source_target_pairs={{0,32},{32,64},{64,96},{96,0},{1,33},{33,65},{65,97},{97,1},{2,34}... | collective-permute-start | bytes 307208 | tf_op jit(solution)/shard_map/ppermute | solution.py:600
  484.5 8.3 %collective-permute-start.29 = (bf16[1,1,1,80,640]{4,3,2,1,0:T(8,128)(2,1)S(1)}, bf16[1,1,1,80,640]{4,3,2,1,0:T(8,128)(2,1)S(1)}, u32[]{:S(2)}, u32[]{:S(2)}) collective-permute-start(bf16[1,1,1,80,640]{4,3,2,1,0:T(8,128)(2,1)S(1)} %get-tuple-element.94), channel_id=1, source_target_pairs={{0,96},{32,0},{64,32},{96,64},{1,97},{33,1},{65,33},{97,65},{2,98}... | collective-permute-start | bytes 307208 | tf_op jit(solution)/shard_map/ppermute | solution.py:600
  488.0 13.1 %all-to-all-start.8 = ((bf16[8,10,640]{2,1,0:T(8,128)(2,1)}), bf16[8,10,640]{2,1,0:T(8,128)(2,1)S(1)}, u32[]{:S(2)}, u32[]{:S(2)}) async-start(bf16[8,10,640]{2,1,0:T(8,128)(2,1)} %convert_element_type.404), calls=%async_computation.8 | async-start | bytes 327680 | tf_op jit(solution)/shard_map/all_to_all | solution.py:678
  (25 other events, 293.5 us)
Sparse Core Ops, SparseCore 0:
  30.5 130.8 all-gather.2

commit v3 on v2

v3 whole, which is shorter than its diff:
```python
import functools
import math

import jax
import jax.numpy as jnp
from jax import lax
from jax.experimental import pallas as pl
from jax.experimental.pallas import tpu as pltpu
from jax.sharding import Mesh
from jax.sharding import PartitionSpec as P

HEADS = 20
NORM_EPS = 1e-05
MASKED = -1000000000.0

F32 = jnp.float32
BF16 = jnp.bfloat16

AXES = ("x", "yl", "c", "z", "yh")
SIZES = (4, 2, 2, 4, 2)
DP = ("x", "yl", "c")
CTX = ("z", "yh")
PLACE = ("z", "yh", "yl", "x", "c")

D = 1280
SPAN = 128
SEQ_GRP = 2
ROWS = SEQ_GRP * SPAN
CTX_N = 8
LEN = CTX_N * SPAN
HEAD_DIM = D // HEADS
GROUP_HEADS = 5
GROUP_W = GROUP_HEADS * HEAD_DIM
COLS = 640
BLK = 80
SCALE = 1.0 / math.sqrt(HEAD_DIM)
Q_BLOCK = 256
HEADS_W = 3 * GROUP_W
PIECE = 32
LAST = 24
MB = 1 << 20


def place_of(dp):
    x, yl, c = dp // 4, (dp // 2) % 2, dp % 2
    return (yl * 4 + x) * 2 + c


def dot(left, right):
    return lax.dot_general(
        left, right, (((1,), (0,)), ((), ())), preferred_element_type=F32
    )


def dot_nt(left, right):
    return lax.dot_general(
        left, right, (((1,), (1,)), ((), ())), preferred_element_type=F32
    )


def norm_stats(rows):
    centre = jnp.mean(rows, axis=-1, keepdims=True)
    centred = rows - centre
    spread = jnp.mean(centred * centred, axis=-1, keepdims=True)
    scale = lax.rsqrt(spread + NORM_EPS)
    return centred * scale, scale


def norm_back(normed, scale, gain, grad):
    scaled = gain * grad
    mean_one = jnp.mean(scaled, axis=-1, keepdims=True)
    mean_two = jnp.mean(scaled * normed, axis=-1, keepdims=True)
    return (scaled - mean_one - normed * mean_two) * scale


def stack_rows(ref, *lead):
    return jnp.concatenate([ref[(*lead, place_of(dp))] for dp in range(16)], axis=0)


def params(vmem_mb):
    return pltpu.CompilerParams(vmem_limit_bytes=vmem_mb * MB)


def cost(flops, nbytes, trans=0):
    return pl.CostEstimate(flops=flops, bytes_accessed=nbytes, transcendentals=trans)


def whole(shape):
    return pl.BlockSpec(shape, lambda *i: (0,) * len(shape))


def turn(block):
    return block.astype(F32).T.astype(BF16)


def allowed_of(length, first_query, key_count, query_count):
    key_pos = lax.broadcasted_iota(jnp.int32, (key_count, query_count), 0)
    query_pos = first_query + lax.broadcasted_iota(
        jnp.int32, (key_count, query_count), 1
    )
    return (key_pos <= query_pos) & (key_pos < length)


def attend_kernel(
    len_ref, tok_ref, norm_ref, bias_ref, w_ref, qkv_ref, out_ref, lse_ref
):
    head = pl.program_id(0)

    @pl.when(head == 0)
    def _():
        weight = w_ref[...].reshape(D, HEADS_W)
        for block in range(LEN // Q_BLOCK):
            cut = slice(block * Q_BLOCK, (block + 1) * Q_BLOCK)
            normed, _ = norm_stats(tok_ref[cut].astype(F32))
            normed = (normed * norm_ref[0:1] + norm_ref[1:2]).astype(BF16)
            turned = (dot(normed, weight) + bias_ref[...]).T.astype(BF16)
            for row in range(3 * GROUP_HEADS):
                qkv_ref[row // GROUP_HEADS, row % GROUP_HEADS, :, cut] = turned[
                    row * HEAD_DIM : (row + 1) * HEAD_DIM
                ]

    length = len_ref[0]
    query = qkv_ref[0, head]
    key = turn(qkv_ref[1, head])
    value = qkv_ref[2, head]
    for block in range(LEN // Q_BLOCK):
        first = block * Q_BLOCK
        last = first + Q_BLOCK
        scores = dot(key[:last], query[:, first:last]) * SCALE
        scores = jnp.where(allowed_of(length, first, last, Q_BLOCK), scores, MASKED)
        top = jnp.max(scores, axis=0, keepdims=True)
        weights = jnp.exp(scores - top)
        total = jnp.sum(weights, axis=0, keepdims=True)
        result = dot(value[:, :last], weights.astype(BF16)) / total
        lse_ref[0, :, first:last] = top + jnp.log(total)
        result = result.astype(BF16)
        for part in range(Q_BLOCK // SPAN):
            out_ref[first // SPAN + part] = result[:, part * SPAN : (part + 1) * SPAN]


def attend_call(length, tok, norm, bias, w_qkv):
    return pl.pallas_call(
        attend_kernel,
        grid=(GROUP_HEADS,),
        in_specs=[
            pl.BlockSpec(memory_space=pltpu.SMEM),
            whole((LEN, D)),
            whole((2, D)),
            whole((1, HEADS_W)),
            whole((16, BLK, HEADS_W)),
        ],
        out_specs=[
            whole((3, GROUP_HEADS, HEAD_DIM, LEN)),
            pl.BlockSpec((CTX_N, HEAD_DIM, SPAN), lambda h: (0, h, 0)),
            pl.BlockSpec((1, 1, LEN), lambda h: (h, 0, 0)),
        ],
        out_shape=[
            jax.ShapeDtypeStruct((3, GROUP_HEADS, HEAD_DIM, LEN), BF16),
            jax.ShapeDtypeStruct((CTX_N, GROUP_W, SPAN), BF16),
            jax.ShapeDtypeStruct((GROUP_HEADS, 1, LEN), F32),
        ],
        compiler_params=params(56),
        cost_estimate=cost(
            6 * LEN * LEN * 4 * HEAD_DIM + 2 * LEN * D * HEADS_W, 8 * MB, 3 * LEN * LEN
        ),
        name="attend",
    )(length, tok, norm, bias, w_qkv)


def attend_back_kernel(len_ref, qkv_ref, grad_ref, lse_ref, g_ref, gk_ref, gv_ref):
    length = len_ref[0]
    query = qkv_ref[0, 0]
    key_t = qkv_ref[1, 0]
    key = turn(key_t)
    value = turn(qkv_ref[2, 0])
    grad = jnp.concatenate([grad_ref[p] for p in range(CTX_N)], axis=1)
    gk_ref[...] = jnp.zeros_like(gk_ref)
    gv_ref[...] = jnp.zeros_like(gv_ref)
    for block in range(LEN // Q_BLOCK):
        first = block * Q_BLOCK
        last = first + Q_BLOCK
        query_b = query[:, first:last]
        grad_b = grad[:, first:last]
        scores = dot(key[:last], query_b) * SCALE
        probs = jnp.where(
            allowed_of(length, first, last, Q_BLOCK),
            jnp.exp(scores - lse_ref[0, :, first:last]),
            0.0,
        )
        grad_probs = dot(value[:last], grad_b)
        delta = jnp.sum(probs * grad_probs, axis=0, keepdims=True)
        grad_scores = (probs * (grad_probs - delta)).astype(BF16)
        g_ref[0, 0, :, first:last] = (dot(key_t[:, :last], grad_scores) * SCALE).astype(
            BF16
        )
        gk_ref[:, :last] += dot_nt(query_b, grad_scores)
        gv_ref[:, :last] += dot_nt(grad_b, probs.astype(BF16))
    g_ref[1, 0] = (gk_ref[...] * SCALE).astype(BF16)
    g_ref[2, 0] = gv_ref[...].astype(BF16)


def attend_back_call(length, qkv, grad, lse):
    heads = pl.BlockSpec((3, 1, HEAD_DIM, LEN), lambda h: (0, h, 0, 0))
    return pl.pallas_call(
        attend_back_kernel,
        grid=(GROUP_HEADS,),
        in_specs=[
            pl.BlockSpec(memory_space=pltpu.SMEM),
            heads,
            pl.BlockSpec((CTX_N, HEAD_DIM, SPAN), lambda h: (0, h, 0)),
            pl.BlockSpec((1, 1, LEN), lambda h: (h, 0, 0)),
        ],
        out_specs=heads,
        out_shape=jax.ShapeDtypeStruct((3, GROUP_HEADS, HEAD_DIM, LEN), BF16),
        scratch_shapes=[pltpu.VMEM((HEAD_DIM, LEN), F32)] * 2,
        compiler_params=params(48),
        cost_estimate=cost(15 * LEN * LEN * 4 * HEAD_DIM, 5 * MB, 3 * LEN * LEN),
        name="attend_back",
    )(length, qkv, grad, lse)


def norm_grad_kernel(w_ref, g_ref, out_ref):
    weight = w_ref[...].reshape(D, HEADS_W)
    grads = turn(g_ref[...].reshape(HEADS_W, Q_BLOCK))
    g_norm = dot_nt(grads, weight).astype(BF16)
    for part in range(Q_BLOCK // SPAN):
        out_ref[part] = g_norm[part * SPAN : (part + 1) * SPAN]


def norm_grad_call(w_qkv, g_qkv):
    return pl.pallas_call(
        norm_grad_kernel,
        grid=(LEN // Q_BLOCK,),
        in_specs=[
            whole((16, BLK, HEADS_W)),
            pl.BlockSpec((3, GROUP_HEADS, HEAD_DIM, Q_BLOCK), lambda i: (0, 0, 0, i)),
        ],
        out_specs=pl.BlockSpec((Q_BLOCK // SPAN, SPAN, D), lambda i: (i, 0, 0)),
        out_shape=jax.ShapeDtypeStruct((CTX_N, SPAN, D), BF16),
        compiler_params=params(48),
        cost_estimate=cost(2 * LEN * D * HEADS_W, 8 * MB),
        name="norm_grad",
    )(w_qkv, g_qkv)


def qkv_grad_kernel(
    info_ref, tok_ref, norm_ref, g_ref, keep_ref, give_ref, d_bias_ref, n1t_ref
):
    core = info_ref[SEQ_GRP + 1]
    for block in range(LEN // Q_BLOCK):
        cut = slice(block * Q_BLOCK, (block + 1) * Q_BLOCK)
        normed, _ = norm_stats(tok_ref[cut].astype(F32))
        turned = (normed * norm_ref[0:1] + norm_ref[1:2]).T.astype(BF16)
        for dp in range(16):
            n1t_ref[dp % 2, dp // 2, :, cut] = turned[dp * BLK : (dp + 1) * BLK]
    grads = g_ref[...].reshape(HEADS_W, LEN)
    d_bias_ref[...] = dot_nt(jnp.ones((8, LEN), BF16), grads)
    for side, ref in ((core, keep_ref), (1 - core, give_ref)):
        for half in range(2):
            rows = n1t_ref[side, 4 * half : 4 * half + 4].reshape(4 * BLK, LEN)
            ref[4 * half : 4 * half + 4] = (
                dot_nt(rows, grads).astype(BF16).reshape(4, BLK, HEADS_W)
            )


def qkv_grad_call(info, tok, norm, g_qkv):
    half = jax.ShapeDtypeStruct((8, BLK, HEADS_W), BF16)
    vmem = pl.BlockSpec(memory_space=pltpu.VMEM)
    return pl.pallas_call(
        qkv_grad_kernel,
        in_specs=[pl.BlockSpec(memory_space=pltpu.SMEM), vmem, vmem, vmem],
        out_specs=[vmem, vmem, vmem],
        out_shape=[half, half, jax.ShapeDtypeStruct((8, HEADS_W), F32)],
        scratch_shapes=[pltpu.VMEM((2, 8, BLK, LEN), BF16)],
        compiler_params=params(48),
        cost_estimate=cost(2 * LEN * D * HEADS_W, 8 * MB),
        name="qkv_grad",
    )(info, tok, norm, g_qkv)


def norm_back_kernel(
    tok_ref, gain_ref, g_res_ref, part_ref, in_grad_ref, d_norm_ref
):
    for seq in range(SEQ_GRP):
        cut = slice(seq * SPAN, (seq + 1) * SPAN)
        normed, scale = norm_stats(tok_ref[cut].astype(F32))
        g_norm = part_ref[4 * seq].astype(F32)
        for group in range(1, 4):
            g_norm = g_norm + part_ref[4 * seq + group].astype(F32)
        in_grad_ref[cut] = g_res_ref[cut].astype(F32) + norm_back(
            normed, scale, gain_ref[...], g_norm
        )
        d_gain = jnp.sum(g_norm * normed, axis=0, keepdims=True)
        d_shift = jnp.sum(g_norm, axis=0, keepdims=True)
        if seq == 0:
            d_norm_ref[0:1] = d_gain
            d_norm_ref[1:2] = d_shift
        else:
            d_norm_ref[0:1] += d_gain
            d_norm_ref[1:2] += d_shift


def norm_back_call(tok, gain, g_res, parts):
    return pl.pallas_call(
        norm_back_kernel,
        out_shape=[
            jax.ShapeDtypeStruct((ROWS, D), F32),
            jax.ShapeDtypeStruct((2, D), F32),
        ],
        compiler_params=params(32),
        cost_estimate=cost(40 * ROWS * D, 6 * MB),
        name="norm_back",
    )(tok, gain, g_res, parts)


def mlp_kernel(
    info_ref,
    tok_ref,
    cot_ref,
    att_ref,
    vec_ref,
    fc_bias_ref,
    wp_ref,
    wf_ref,
    wo_ref,
    out_ref,
    g_res_ref,
    g_att_ref,
    d_vec_ref,
    d_fc_bias_ref,
    rows_ref,
    keep_ref,
    give_ref,
    n2_ref,
    g_out_ref,
    res_ref,
    acc_ref,
    gn_ref,
    wp_all_ref,
    turned_ref,
):
    step = pl.program_id(0)
    core = info_ref[SEQ_GRP + 1]
    proj_shift, gain, shift, out_shift = (vec_ref[k : k + 1] for k in range(4))

    def by_core(turned, first):
        for dp in range(16):
            turned_ref[dp % 2, place_of(dp) // 2] = turned[dp * BLK : (dp + 1) * BLK]
        keep_ref[first : first + 8] = turned_ref[core]
        give_ref[first : first + 8] = turned_ref[1 - core]

    @pl.when(step == 0)
    def _():
        att = jnp.concatenate([turn(att_ref[s]) for s in range(SEQ_GRP)], axis=0)
        for half in range(2):
            cut = slice(half * COLS, (half + 1) * COLS)
            pack = pack_of(half, PIECE, (BLK, CTX_N * PIECE), 0, 1)
            for dp in range(16):
                pieces = wp_ref[:, place_of(dp)].reshape(CTX_N * PIECE, COLS)
                wp_all_ref[dp * BLK : (dp + 1) * BLK, cut] = dot(pack, pieces).astype(
                    BF16
                )
        residual = tok_ref[...].astype(F32) + dot(att, wp_all_ref[...]) + proj_shift
        res_ref[...] = residual
        normed, _ = norm_stats(residual)
        normed = normed * gain + shift
        n2_ref[...] = normed.astype(BF16)
        by_core(normed.T.astype(BF16), 32)
        by_core(jnp.concatenate([att_ref[s] for s in range(SEQ_GRP)], axis=1), 40)
        for seq in range(SEQ_GRP):
            cut = slice(seq * SPAN, (seq + 1) * SPAN)
            pos = info_ref[SEQ_GRP] + lax.broadcasted_iota(jnp.int32, (SPAN, D), 0)
            g_out_ref[cut] = jnp.where(
                pos < info_ref[seq], cot_ref[cut], jnp.zeros((SPAN, D), BF16)
            )
        rows_ref[:, 4 * D : 5 * D] = g_out_ref[...]
        acc_ref[...] = residual + out_shift
        gn_ref[...] = jnp.zeros_like(gn_ref)

    w_fc = stack_rows(wf_ref, 0)
    pre = dot(n2_ref[...], w_fc) + fc_bias_ref[...]
    root = math.sqrt(2.0 / math.pi)
    square = pre * pre
    bend = jnp.tanh(root * pre * (1.0 + 0.044715 * square))
    gate = 0.5 * (1.0 + bend)
    slope = gate + 0.5 * pre * (1.0 - bend * bend) * root * (
        1.0 + 3.0 * 0.044715 * square
    )
    act = pre * gate
    act_t = act.T.astype(BF16).reshape(2, 4, BLK, ROWS)
    act = act.astype(BF16)
    turned_ref[:, 0:4] = act_t
    keep_ref[pl.ds(step * 4, 4)] = turned_ref[core, 0:4]
    give_ref[pl.ds(step * 4, 4)] = turned_ref[1 - core, 0:4]
    g_act = None
    for half in range(2):
        cut = slice(half * COLS, (half + 1) * COLS)
        w_out = jnp.concatenate(
            [
                wo_ref[z, yh, 0, 0, c, half * 40 : (half + 1) * 40]
                for c in range(2)
                for z in range(4)
                for yh in range(2)
            ],
            axis=0,
        )
        acc_ref[:, cut] += dot(act, w_out)
        part = dot_nt(g_out_ref[:, cut], w_out)
        g_act = part if g_act is None else g_act + part
    g_pre = (g_act * slope).astype(BF16)
    rows_ref[:, pl.ds(pl.multiple_of(step * COLS, COLS), COLS)] = g_pre
    d_fc_bias_ref[...] = jnp.sum(g_pre.astype(F32), axis=0, keepdims=True)
    gn_ref[...] += dot_nt(g_pre, w_fc)

    @pl.when(step == pl.num_programs(0) - 1)
    def _():
        out_ref[...] = acc_ref[...].astype(BF16)
        normed, scale = norm_stats(res_ref[...])
        g_norm = gn_ref[...]
        g_out = g_out_ref[...].astype(F32)
        g_res = (g_out + norm_back(normed, scale, gain, g_norm)).astype(BF16)
        g_res_ref[...] = g_res
        rows_ref[:, 5 * D :] = g_res
        d_vec_ref[0:1] = jnp.sum(g_res.astype(F32), axis=0, keepdims=True)
        d_vec_ref[1:2] = jnp.sum(g_norm * normed, axis=0, keepdims=True)
        d_vec_ref[2:3] = jnp.sum(g_norm, axis=0, keepdims=True)
        d_vec_ref[3:4] = jnp.sum(g_out, axis=0, keepdims=True)
        g_att = dot_nt(g_res, wp_all_ref[...])
        for seq in range(SEQ_GRP):
            g_att_ref[seq] = g_att[seq * SPAN : (seq + 1) * SPAN].T.astype(BF16)


def pack_of(half, piece, shape, row_dim, piece_dim):
    row = lax.broadcasted_iota(jnp.int32, shape, row_dim)
    place = lax.broadcasted_iota(jnp.int32, shape, piece_dim)
    offset = place - (piece - 10) * (row // 10) - 10 * half
    return (offset == row).astype(F32).astype(BF16)


def mlp_call(info, tok, cot, att, vecs, fc_bias, weights):
    by_ctx = weights.reshape(CTX_N, 16, 2 * BLK + PIECE, COLS)
    by_chip = weights.reshape(4, 2, 2, 4, 2, 2 * BLK + PIECE, COLS)
    rows = jax.ShapeDtypeStruct((ROWS, D), BF16)
    turned = jax.ShapeDtypeStruct((48, BLK, ROWS), BF16)
    return pl.pallas_call(
        mlp_kernel,
        grid=(8,),
        in_specs=[
            pl.BlockSpec(memory_space=pltpu.SMEM),
            whole((ROWS, D)),
            whole((ROWS, D)),
            whole((SEQ_GRP, D, SPAN)),
            whole((4, D)),
            pl.BlockSpec((1, COLS), lambda j: (0, j)),
            pl.BlockSpec((CTX_N, 16, PIECE, COLS), lambda j: (0, 0, 5, 0)),
            pl.BlockSpec((1, 16, BLK, COLS), lambda j: (j, 0, 0, 0)),
            pl.BlockSpec(
                (4, 2, 1, 1, 2, BLK, COLS), lambda j: (0, 0, j % 2, j // 2, 0, 1, 0)
            ),
        ],
        out_specs=[
            whole((ROWS, D)),
            whole((ROWS, D)),
            whole((SEQ_GRP, D, SPAN)),
            whole((4, D)),
            pl.BlockSpec((1, COLS), lambda j: (0, j)),
            whole((ROWS, 6 * D)),
            whole((48, BLK, ROWS)),
            whole((48, BLK, ROWS)),
        ],
        out_shape=[
            rows,
            rows,
            jax.ShapeDtypeStruct((SEQ_GRP, D, SPAN), BF16),
            jax.ShapeDtypeStruct((4, D), F32),
            jax.ShapeDtypeStruct((1, 4 * D), F32),
            jax.ShapeDtypeStruct((ROWS, 6 * D), BF16),
            turned,
            turned,
        ],
        scratch_shapes=[
            pltpu.VMEM((ROWS, D), BF16),
            pltpu.VMEM((ROWS, D), BF16),
            pltpu.VMEM((ROWS, D), F32),
            pltpu.VMEM((ROWS, D), F32),
            pltpu.VMEM((ROWS, D), F32),
            pltpu.VMEM((D, D), BF16),
            pltpu.VMEM((2, 8, BLK, ROWS), BF16),
        ],
        compiler_params=params(58),
        cost_estimate=cost(2 * ROWS * D * (16 * D + 2 * D), 38 * MB, 2 * ROWS * 4 * D),
        name="mlp",
    )(info, tok, cot, att, vecs, fc_bias, by_ctx, by_ctx, by_chip)


def both(ref, other_ref, axis):
    return jnp.concatenate([ref[...], other_ref[...]], axis=axis)


def fc_grad_kernel(n2_ref, n2_other_ref, g_ref, g_other_ref, out_ref):
    left = both(n2_ref, n2_other_ref, 2).reshape(D // 2, 2 * ROWS)
    d_w = dot(left, both(g_ref, g_other_ref, 0)).astype(BF16).reshape(8, BLK, COLS)
    for chip in range(8):
        out_ref[chip % 4, 0, chip // 4] = d_w[chip]


def fc_grad_call(turned, turned_other, rows, rows_other):
    n2_block = pl.BlockSpec((8, BLK, ROWS), lambda j: (4, 0, 0))
    g_block = pl.BlockSpec((ROWS, COLS), lambda j: (0, j))
    return pl.pallas_call(
        fc_grad_kernel,
        grid=(8,),
        in_specs=[n2_block, n2_block, g_block, g_block],
        out_specs=pl.BlockSpec((4, 1, 2, BLK, COLS), lambda j: (0, j, 0, 0, 0)),
        out_shape=jax.ShapeDtypeStruct((4, 8, 2, BLK, COLS), BF16),
        compiler_params=params(40),
        cost_estimate=cost(8 * ROWS * D * D, 12 * MB),
        name="fc_grad",
    )(turned, turned_other, rows, rows_other)


def out_grad_kernel(
    act_ref,
    act_other_ref,
    att_ref,
    att_other_ref,
    g_ref,
    g_other_ref,
    one_ref,
    two_ref,
):
    g_both = both(g_ref, g_other_ref, 0)
    act = both(act_ref, act_other_ref, 2).reshape(4 * BLK, 2 * ROWS)
    d_w = dot(act, g_both[:, :D]).astype(BF16)
    for z in range(4):
        for yh in range(2):
            row = (z * 2 + yh) * 40
            one_ref[yh, 0, z, 0] = d_w[row : row + 40, :COLS]
            two_ref[z, 0, yh, 0, :40] = d_w[row : row + 40, COLS:]
    att = both(att_ref, att_other_ref, 2).reshape(BLK, 2 * ROWS)
    d_w = dot(att, g_both[:, D:]).astype(BF16)
    piece = None
    for half in range(2):
        unpack = pack_of(half, LAST, (CTX_N * LAST, BLK), 1, 0)
        part = dot(unpack, d_w[:, half * COLS : (half + 1) * COLS])
        piece = part if piece is None else piece + part
    piece = piece.astype(BF16)
    for z in range(4):
        for yh in range(2):
            row = (z * 2 + yh) * LAST
            two_ref[z, 0, yh, 0, 40:] = piece[row : row + LAST]


def out_grad_call(turned, turned_other, rows, rows_other):
    act_block = pl.BlockSpec((4, BLK, ROWS), lambda j: (j, 0, 0))
    att_block = pl.BlockSpec((1, BLK, ROWS), lambda j: (40 + (j % 2) * 4 + j // 2, 0, 0))
    g_block = pl.BlockSpec((ROWS, 2 * D), lambda j: (0, 2))
    return pl.pallas_call(
        out_grad_kernel,
        grid=(8,),
        in_specs=[act_block, act_block, att_block, att_block, g_block, g_block],
        out_specs=[
            pl.BlockSpec(
                (2, 1, 4, 1, 40, COLS), lambda j: (0, j % 2, 0, j // 2, 0, 0)
            ),
            pl.BlockSpec(
                (4, 1, 2, 1, 40 + LAST, COLS), lambda j: (0, j // 2, 0, j % 2, 0, 0)
            ),
        ],
        out_shape=[
            jax.ShapeDtypeStruct((2, 2, 4, 4, 40, COLS), BF16),
            jax.ShapeDtypeStruct((4, 4, 2, 2, 40 + LAST, COLS), BF16),
        ],
        compiler_params=params(40),
        cost_estimate=cost(10 * ROWS * D * D, 14 * MB),
        name="out_grad",
    )(turned, turned_other, turned, turned_other, rows, rows_other)


def ring_perm(axis):
    pairs = []
    for core in range(2):
        for pos in range(4):
            to = (pos + (1 if core == 0 else -1)) % 4
            if axis == "x":
                index = lambda p: p * 2 + core
            elif axis == "z":
                index = lambda p: core * 4 + p
            else:
                index = lambda p: ((p % 2) * 2 + core) * 2 + p // 2
            pairs.append((index(pos), index(to)))
    return {"x": ("x", "c"), "z": ("c", "z"), "y": ("yl", "c", "yh")}[axis], pairs


def swap_cores(array):
    return lax.ppermute(array, "c", [(0, 1), (1, 0)])


def shift_perm(axis, by):
    if axis != "y":
        return axis, [(p, (p + by) % 4) for p in range(4)]
    index = lambda p: (p % 2) * 2 + p // 2
    return ("yl", "yh"), [(index(p), index((p + by) % 4)) for p in range(4)]


class Sums:
    def __init__(self, colours):
        self.terms = [array for array, _, _ in colours]
        self.orders = [order for _, order, _ in colours]
        self.after = [after for _, _, after in colours]
        self.way = 1 - 2 * lax.axis_index("c")
        self.place = {
            "x": lax.axis_index("x"),
            "y": 2 * lax.axis_index("yh") + lax.axis_index("yl"),
            "z": lax.axis_index("z"),
        }
        self.phase = 0
        self.step = 0
        self.first_blocks()

    def local(self, colour, block):
        return lax.dynamic_index_in_dim(self.terms[colour], block % 4, 0, False)

    def axes(self):
        return list(enumerate(order[self.phase] for order in self.orders))

    def first_blocks(self):
        self.sent = [self.local(k, self.place[a] - self.way) for k, a in self.axes()]

    def start(self):
        if self.phase < 2:
            self.flight = [
                lax.ppermute(self.sent[k], *ring_perm(a)) for k, a in self.axes()
            ]
            return
        self.flight = [
            [
                lax.ppermute(self.local(k, self.place[a] + by), *shift_perm(a, by))
                for by in (1, 2, 3)
            ]
            for k, a in self.axes()
        ]

    def land(self):
        if self.phase == 2:
            return [
                self.local(k, self.place[a]).astype(F32)
                + sum(part.astype(F32) for part in self.flight[k])
                for k, a in self.axes()
            ]
        self.sent = [
            (
                self.flight[k].astype(F32)
                + self.local(k, self.place[a] - self.way * (2 + self.step)).astype(F32)
            ).astype(BF16)
            for k, a in self.axes()
        ]
        self.step += 1
        if self.step == 3:
            self.terms = self.sent
            if self.phase == 0:
                self.terms = [after(t) for after, t in zip(self.after, self.terms)]
            self.step, self.phase = 0, self.phase + 1
            if self.phase < 2:
                self.first_blocks()
        return None

    def advance(self, other):
        self.flight, other = tie(self.flight, other)
        self.land()
        self.sent, other = tie(self.sent, other)
        self.start()
        return other

    def run(self):
        sums = self.land()
        while sums is None:
            self.start()
            sums = self.land()
        return sums


def tie(first, second):
    return lax.optimization_barrier((first, second))


def per_device(
    tokens,
    lengths,
    cotangent,
    ln1_gain,
    ln1_bias,
    w_qkv,
    q_bias,
    v_bias,
    w_proj,
    proj_bias,
    ln2_gain,
    ln2_bias,
    w_fc,
    fc_bias,
    w_out,
    out_bias,
):
    ctx_rank = lax.axis_index(CTX)
    core = lax.axis_index("c")
    seq_rank = ctx_rank // 4
    head_group = ctx_rank % 4
    tok = tokens.reshape(ROWS, D)
    cot = cotangent.reshape(ROWS, D)

    def exchange(array):
        return lax.all_to_all(array, CTX, 0, 0, tiled=True)

    w_cols = exchange(w_fc.reshape(10, CTX_N, COLS).transpose(1, 0, 2))

    vec_two = jnp.concatenate([proj_bias, ln2_gain, ln2_bias, out_bias, fc_bias])
    vec_two = jnp.pad(vec_two[None], ((0, PIECE - 21), (0, COLS - 80)))
    part = jnp.concatenate(
        [
            w_cols.reshape(BLK, COLS),
            w_out.reshape(40, 2, COLS).transpose(1, 0, 2).reshape(BLK, COLS),
            w_proj.reshape(10, 2, COLS).transpose(1, 0, 2).reshape(20, COLS),
            vec_two,
        ],
        axis=0,
    )
    part, w_qkv, tokens = lax.optimization_barrier((part, w_qkv, tokens))
    weights = lax.all_gather(part, PLACE, axis=0, tiled=False)

    groups = w_qkv.reshape(10, 3, 4, GROUP_W).transpose(2, 0, 1, 3)
    groups = groups.reshape(4, 10, HEADS_W)
    vec_one = jnp.concatenate([ln1_gain, ln1_bias, q_bias, v_bias])
    vec_one = jnp.pad(vec_one[None, None], ((0, 0), (0, 0), (0, HEADS_W - 40)))
    groups = jnp.concatenate([groups, jnp.broadcast_to(vec_one, (4, 1, HEADS_W))], axis=1)
    shards = exchange(jnp.concatenate([groups, groups], axis=0))
    w_group = jnp.concatenate(
        [shards[:, :10].reshape(BLK, HEADS_W), shards[:, 10]], axis=0
    )
    w_group = jnp.broadcast_to(w_group[None], (8, BLK + 8, HEADS_W))
    w_group = lax.all_to_all(w_group, ("x", "yl"), 0, 0, tiled=True)
    sequence = jnp.broadcast_to(tokens[:, None], (SEQ_GRP, 4, SPAN, D))
    w_group, sequence = tie(w_group, sequence)
    other = swap_cores(w_group)
    first = jnp.where(core == 0, w_group, other)
    second = jnp.where(core == 0, other, w_group)
    w_group = jnp.stack([first, second], axis=1).reshape(16, BLK + 8, HEADS_W)
    sequence = exchange(sequence.reshape(CTX_N, SPAN, D)).reshape(LEN, D)

    vecs = w_group[:, BLK:, :40].reshape(128, 4, 10).transpose(1, 0, 2)
    vecs = vecs.reshape(4, D).astype(F32)
    own = lax.dynamic_slice_in_dim(vecs[2:], head_group * GROUP_W, GROUP_W, 1)
    bias = jnp.concatenate([own[0:1], jnp.zeros((1, GROUP_W), F32), own[1:2]], axis=1)
    length = lax.dynamic_slice_in_dim(lengths, seq_rank, 1)
    qkv, att, lse = attend_call(length, sequence, vecs[:2], bias, w_group)
    att = exchange(att).reshape(SEQ_GRP, D, SPAN)

    more = weights[:, 2 * BLK + 20, :80].reshape(4, 2, 2, 4, 2, 80)
    more = more.transpose(3, 2, 4, 0, 1, 5).reshape(128, 80).astype(F32)
    fc_shift = more[:, 40:].reshape(1, 4 * D)
    more = more[:, :40].reshape(128, 4, 10).transpose(1, 0, 2).reshape(4, D)
    info = jnp.concatenate([lengths, jnp.stack([ctx_rank * SPAN, core]).astype(jnp.int32)])
    layer_out, g_res, g_att, d_vecs, d_fc_bias, rows, turned, turned_give = mlp_call(
        info, tok, cot, att, more, fc_shift, weights
    )

    turned_other = swap_cores(turned_give)
    rows_other = swap_cores(rows)
    g_att = exchange(g_att.reshape(CTX_N, GROUP_W, SPAN))
    d_fc = fc_grad_call(turned, turned_other, rows, rows_other)
    d_one, d_two = out_grad_call(turned, turned_other, rows, rows_other)

    def to_owners(array):
        array = array.reshape(8, 2, 4, 2, 10, COLS).transpose(3, 1, 2, 0, 4, 5)
        return array.reshape(4, 4, BLK, COLS)

    same = lambda array: array
    sums = Sums(
        [
            (d_fc, "xyz", to_owners),
            (d_one.reshape(4, 4, 4, 40, COLS), "yzx", same),
            (d_two.reshape(4, 4, 4, 40 + LAST, COLS), "zxy", same),
        ]
    )
    sums.sent, g_att = tie(sums.sent, g_att)
    sums.start()
    g_qkv = attend_back_call(length, qkv, g_att, lse)
    g_qkv = sums.advance(g_qkv)
    g_norm = exchange(norm_grad_call(w_group, g_qkv))
    group_keep, group_give, d_bias = qkv_grad_call(info, sequence, vecs[:2], g_qkv)
    group_give = sums.advance(group_give)
    group_given = swap_cores(group_give)
    input_grad, d_norm = norm_back_call(tok, vecs[:1], g_res, g_norm)
    d_norm = sums.advance(d_norm)

    d_heads = jnp.zeros((2, D), F32)
    d_heads = lax.dynamic_update_slice(
        d_heads,
        jnp.concatenate([d_bias[:1, :GROUP_W], d_bias[:1, 2 * GROUP_W :]], axis=0),
        (0, head_group * GROUP_W),
    )
    d_small = jnp.concatenate([d_norm, d_heads, d_vecs], axis=0)
    d_small = d_small.reshape(8, 128, 10).transpose(1, 0, 2).reshape(128, 80)
    d_small = jnp.concatenate([d_small, d_fc_bias.reshape(128, 40)], axis=1)
    d_small = d_small.reshape(8, 2, 8, 120).astype(BF16)
    small_keep = lax.dynamic_index_in_dim(d_small, core, 1, False)
    small_given = swap_cores(lax.dynamic_index_in_dim(d_small, 1 - core, 1, False))
    d_group = (group_keep.astype(F32) + group_given.astype(F32)).astype(BF16)
    d_small = (small_keep.astype(F32) + small_given.astype(F32)).astype(BF16)
    d_small = jnp.pad(d_small, ((0, 0), (0, 0), (0, HEADS_W - 120)))
    d_group = jnp.concatenate([d_group, d_small], axis=1)
    d_group = lax.all_to_all(d_group, ("x", "yl"), 0, 0, tiled=True)
    d_group = jnp.sum(d_group.astype(F32), axis=0).astype(BF16)
    d_group = jnp.concatenate(
        [d_group[:BLK].reshape(CTX_N, 10, HEADS_W), d_group[BLK:, None]], axis=1
    )
    d_group = exchange(d_group).astype(F32)
    d_qkv = (d_group[:4, :10] + d_group[4:, :10]).reshape(4, 10, 3, GROUP_W)
    d_qkv = d_qkv.transpose(1, 2, 0, 3).reshape(10, 3 * D)
    small = jnp.sum(d_group[:, 10, :120], axis=0)

    fc_sum, one_sum, two_sum = sums.run()
    d_fc = fc_sum.reshape(CTX_N, 10, COLS).transpose(1, 0, 2).reshape(10, CTX_N * COLS)
    d_out = jnp.concatenate([one_sum, two_sum[:40]], axis=1)
    d_proj = two_sum[40:60].reshape(2, 10, COLS).transpose(1, 0, 2).reshape(10, D)
    names = ["g1", "b1", "q", "v", "proj", "g2", "b2", "out"]
    vec = {n: small[10 * k : 10 * (k + 1)] for k, n in enumerate(names)}

    return (
        layer_out.reshape(tokens.shape),
        input_grad.reshape(tokens.shape),
        vec["g1"],
        vec["b1"],
        d_qkv,
        vec["q"],
        vec["v"],
        d_proj,
        vec["proj"],
        vec["g2"],
        vec["b2"],
        d_fc,
        small[80:120],
        d_out,
        vec["out"],
    )


def solution(mesh):
    fine = Mesh(mesh.devices.reshape(SIZES), AXES)
    rows = P(DP, CTX, None)
    mat = P(AXES, None)
    vec = P(AXES)
    in_specs = (
        rows,
        P(DP),
        rows,
        vec,
        vec,
        mat,
        vec,
        vec,
        mat,
        vec,
        vec,
        vec,
        mat,
        vec,
        mat,
        vec,
    )
    out_specs = (
        rows,
        rows,
        vec,
        vec,
        mat,
        vec,
        vec,
        mat,
        vec,
        vec,
        vec,
        mat,
        vec,
        mat,
        vec,
    )
    return jax.shard_map(
        per_device, mesh=fine, in_specs=in_specs, out_specs=out_specs, check_vma=False
    )
```

time: 518 us -> 453 us (0.87)
  waiting for transfers between devices: 180 us -> 144 us
  starting transfers between devices: 86.1 us -> 61.6 us
  other arithmetic: 58.2 us -> 42.4 us
  local copies, waits for them, and re-layouts: 27.6 us -> 41.3 us
  blocking collectives: 45.8 us -> 35.6 us
  Pallas kernels: 95.8 us -> 104 us
    all_to_all x7 -> x6, waiting for transfers between devices: 96.1 us -> 53.9 us  [exchange(): return lax.all_to_all(array, CTX, 0, 0, tiled=True)]
    all_gather x1, waiting for transfers between devices: 0.01 us -> 38.6 us  [per_device(): weights = lax.all_gather(part, PLACE, axis=0, tiled=False)]
    ppermute x18, waiting for transfers between devices: 77.6 us -> 41.4 us  [start(): lax.ppermute(self.sent[k], *ring_perm(a))]
    pallas_call x0 -> x4, Pallas kernels: none -> 33.9 us  [the longest x1 10.9 us: out_grad_call(): pl.pallas_call(out_grad_kernel, grid=(8,), in_specs=[act_block, act_block...]
    ppermute x18, starting transfers between devices: 33.5 us -> 13.3 us  [start(): lax.ppermute(self.sent[k], *ring_perm(a))]
    pallas_call x1, Pallas kernels: 28.4 us -> 14.5 us  [attend_back_call(): pl.pallas_call(attend_back_kernel, grid=(GROUP_HEADS,), in_specs=[pl.Bloc...]
    convert_element_type x23 -> x20, other arithmetic: 47.3 us -> 34.5 us  [the longest x18 32.6 us: land(): self.sent = [(self.flight[k].astype(F32) + self.local(k, self.place[a] -...]
    pallas_call x1, Pallas kernels: 46.6 us -> 35.7 us  [mlp_call(): pl.pallas_call(mlp_kernel, grid=(8,), in_specs=[pl.BlockSpec(memory_space...]
  transfers between devices with their start and end apart: 39 -> 40, of which waited for: 15 -> 21; matrix products, arithmetic and copies ran while one was open for 13% -> 10% of each run, Pallas kernels for 9% -> 15%
where the time goes in v3:
time: 453 us; the launch traced here: 444 us
  waiting for transfers between devices  144 us (32%)
  Pallas kernels  104 us (23%)
  starting transfers between devices  61.6 us (14%)
  other arithmetic  42.4 us (9%)
  local copies, waits for them, and re-layouts  41.3 us (9%)
  blocking collectives  35.6 us (8%)
  between operations  15.2 us (3%)
    all_to_all x6, waiting for transfers between devices, exchange(): return lax.all_to_all(array, CTX, 0, 0, tiled=True)  53.9 us
    ppermute x18, waiting for transfers between devices, start(): lax.ppermute(self.sent[k], *ring_perm(a))  41.4 us
    all_gather x1, waiting for transfers between devices, per_device(): weights = lax.all_gather(part, PLACE, axis=0, tiled=False)  38.6 us
    pallas_call x1, Pallas kernels, mlp_call(): pl.pallas_call(mlp_kernel, grid=(8,), in_specs=[pl.BlockSpec(memory_space...  35.7 us
    all_to_all x6, starting transfers between devices, exchange(): return lax.all_to_all(array, CTX, 0, 0, tiled=True)  34.2 us
    convert_element_type x18, other arithmetic, land(): self.sent = [(self.flight[k].astype(F32) + self.local(k, self.place[a] -...  32.6 us
    all_to_all x1, blocking collectives, per_device(): w_group = lax.all_to_all(w_group, ('x', 'yl'), 0, 0, tiled=True)  22.9 us
    pallas_call x1, Pallas kernels, attend_call(): pl.pallas_call(attend_kernel, grid=(GROUP_HEADS,), in_specs=[pl.BlockSpec...  18 us
  transfers between devices with their start and end apart: 40, of which 21 were waited for; matrix products, arithmetic and copies ran while one was open for 10% of the time, Pallas kernels for 15%

profile of v3, /device:TPU:0, one launch (start us, length us, event | category | flops | bytes accessed | tf_op | source)
XLA Modules:
  0.0 444.3 jit_solution(12034659543894886163)
XLA Ops:
  8.9 8.0 %all-to-all-start = ((bf16[8,10,640]{2,1,0:T(8,128)(2,1)}), bf16[8,10,640]{2,1,0:T(8,128)(2,1)S(1)}, u32[]{:S(2)}, u32[]{:S(2)}) async-start(bf16[8,10,640]{2,1,0:T(8,128)(2,1)} %bitcast.174), calls=%async_computation | async-start | bytes 327680 | tf_op jit(solution)/shard_map/all_to_all | solution.py:713
  18.8 3.4 concatenate.50
  26.8 12.7 %all_to_all.45 = bf16[8,11,960]{2,1,0:T(8,128)(2,1)S(1)} all-to-all(bf16[8,11,960]{2,1,0:T(8,128)(2,1)S(1)} %copy.82), channel_id=1, replica_groups=mesh['x'=4,'yl'=2,'c'=2,'z'=4,'yh'=2] {'z','yh'}, dimensions={0} | all-to-all | bytes 337920 | tf_op jit(solution)/shard_map/all_to_all | solution.py:713
  39.8 22.9 %all_to_all.46 = bf16[8,88,960]{2,1,0:T(8,128)(2,1)S(1)} all-to-all(bf16[8,88,960]{2,1,0:T(8,128)(2,1)S(1)} %broadcast_in_dim.38), channel_id=1, replica_groups=mesh['x'=4,'yl'=2,'c'=2,'z'=4,'yh'=2] {'x','yl'}, dimensions={0} | all-to-all | bytes 2703360 | tf_op jit(solution)/shard_map/all_to_all | solution.py:741
  64.4 4.5 %all-to-all-start.3 = ((bf16[8,128,1280]{2,1,0:T(8,128)(2,1)}), bf16[8,128,1280]{2,1,0:T(8,128)(2,1)}, u32[]{:S(2)}, u32[]{:S(2)}) async-start(bf16[8,128,1280]{2,1,0:T(8,128)(2,1)} %bitcast.12), calls=%async_computation.3 | async-start | bytes 5242880 | tf_op jit(solution)/shard_map/all_to_all | solution.py:713
  72.4 33.3 %all-to-all-done.3 = bf16[8,128,1280]{2,1,0:T(8,128)(2,1)} async-done(((bf16[8,128,1280]{2,1,0:T(8,128)(2,1)}), bf16[8,128,1280]{2,1,0:T(8,128)(2,1)}, u32[]{:S(2)}, u32[]{:S(2)}) %all-to-all-start.3) | async-done | bytes 2621472 | tf_op jit(solution)/shard_map/all_to_all | solution.py:713
  105.8 18.0 %attend.1 = (bf16[3,5,64,1024]{3,2,1,0:T(8,128)(2,1)}, bf16[8,320,128]{2,1,0:T(8,128)(2,1)}, f32[5,1,1024]{2,1,0:T(1,128)}) custom-call(s32[1]{0:T(128)} %dynamic_slice.130.len_ref, bf16[1024,1280]{1,0:T(8,128)(2,1)} %bitcast.13.tok_ref, f32[2,1280]{1,0:T(2,128)} %slice.101.norm_ref, f32[1,960]{1,0:T(1,128)} %pad_maximum_fusion.5.bias_ref, ...), custom_call_target="tpu_custom_call" | custom-call | flops 4127195136 | bytes 8388608 | tf_op jit(solution)/shard_map/attend/pallas_call | solution.py:142
  123.7 3.7 all-to-all-start.4
  128.0 38.6 %all-gather.3.cloned.1.call-done = bf16[24576,640]{1,0:T(8,128)(2,1)} async-done(((bf16[192,640]{1,0:T(8,128)(2,1)}), bf16[24576,640]{1,0:T(8,128)(2,1)}) %all-gather.3.cloned.1.call-update) | async-done | bytes 31457296 | tf_op jit(solution)/shard_map/all_gather | solution.py:729
  170.3 35.7 %mlp.1 = (bf16[256,1280]{1,0:T(8,128)(2,1)}, bf16[256,1280]{1,0:T(8,128)(2,1)}, bf16[2,1280,128]{2,1,0:T(8,128)(2,1)}, f32[4,1280]{1,0:T(4,128)}, f32[1,5120]{1,...) custom-call(s32[4]{0:T(128)} %pad_add_fusion.info_ref, ...), custom_call_target="tpu_custom_call" | custom-call | flops 15099494400 | bytes 39845888 | tf_op jit(solution)/shard_map/mlp/pallas_call | solution.py:445
  206.7 5.0 %all-to-all-start.5 = ((bf16[8,320,128]{2,1,0:T(8,128)(2,1)}), bf16[8,320,128]{2,1,0:T(8,128)(2,1)S(1)}, u32[]{:S(2)}, u32[]{:S(2)}) async-start(bf16[8,320,128]{2,1,0:T(8,128)(2,1)} %bitcast.214), calls=%async_computation.5 | async-start | bytes 1310720 | tf_op jit(solution)/shard_map/all_to_all | solution.py:713
  211.6 4.1 collective-permute-done.1.n2_other_ref.act_other_ref.att_other_ref
  219.8 10.9 %out_grad.1 = (bf16[2,2,4,4,40,640]{5,4,3,2,1,0:T(8,128)(2,1)S(1)}, bf16[4,4,2,2,64,640]{5,4,3,2,1,0:T(8,128)(2,1)}) custom-call(bf16[48,80,256]{2,1,0:T(8,128)(2,1)S(1)} %copy-done, bf16[48,80,256]{2,1,0:T(8,128)(2,1)S(1)} %collective-permute-done.1.n2_other_ref.act_other_ref.att_other_ref, bf16[48,80,256]{2,1,0:T(8,128)(2,1)S(1)} %copy-done, ...), custom_call_target="tpu_custom_call" | custom-call | flops 4194304000 | bytes 14680064 | tf_op jit(solution)/shard_map/out_grad/pallas_call | solution.py:558
  230.7 3.4 dynamic-slice_bitcast_fusion.1
  234.2 9.2 %fc_grad.1 = bf16[4,8,2,80,640]{4,3,2,1,0:T(8,128)(2,1)} custom-call(bf16[48,80,256]{2,1,0:T(8,128)(2,1)S(1)} %copy-done, bf16[48,80,256]{2,1,0:T(8,128)(2,1)S(1)} %collective-permute-done.1.n2_other_ref.act_other_ref.att_other_ref, bf16[256,7680]{1,0:T(8,128)(2,1)S(1)} %copy-done.1, bf16[256,7680]{1,0:T(8,128)(2,1)} %collective-permute-done.2.g_other_ref), custom_call_target="tpu_custom_call" | custom-call | flops 3355443200 | bytes 12582912 | tf_op jit(solution)/shard_map/fc_grad/pallas_call | solution.py:510
  251.0 14.5 %attend_back.1.g_ref = bf16[3,5,64,1024]{3,2,1,0:T(8,128)(2,1)S(1)} custom-call(s32[1]{0:T(128)} %dynamic_slice.130.len_ref, bf16[3,5,64,1024]{3,2,1,0:T(8,128)(2,1)S(1)} %copy-done.13, bf16[8,320,128]{2,1,0:T(8,128)(2,1)S(1)} %all-to-all-done.5.grad_ref, f32[5,1,1024]{2,1,0:T(1,128)S(1)} %copy-done.14), custom_call_target="tpu_custom_call" | custom-call | flops 4026531840 | bytes 5242880 | tf_op jit(solution)/shard_map/attend_back/pallas_call | solution.py:204
  268.8 3.6 fusion.2
  274.9 3.1 fusion.6
  279.8 5.7 %norm_grad.1 = bf16[8,128,1280]{2,1,0:T(8,128)(2,1)S(1)} custom-call(bf16[16,88,960]{2,1,0:T(8,128)(2,1)} %bitcast.204, bf16[3,5,64,1024]{3,2,1,0:T(8,128)(2,1)S(1)} %attend_back.1.g_ref), custom_call_target="tpu_custom_call" | custom-call | flops 2516582400 | bytes 8388608 | tf_op jit(solution)/shard_map/norm_grad/pallas_call | solution.py:231
  287.0 6.8 %all-to-all-start.6 = ((bf16[8,128,1280]{2,1,0:T(8,128)(2,1)}), bf16[8,128,1280]{2,1,0:T(8,128)(2,1)S(1)}, u32[]{:S(2)}, u32[]{:S(2)}) async-start(bf16[8,128,1280]{2,1,0:T(8,128)(2,1)} %copy-done.5), calls=%async_computation.6 | async-start | bytes 5242880 | tf_op jit(solution)/shard_map/all_to_all | solution.py:713
  295.3 8.0 %qkv_grad.1 = (bf16[8,80,960]{2,1,0:T(8,128)(2,1)S(1)}, bf16[8,80,960]{2,1,0:T(8,128)(2,1)}, f32[8,960]{1,0:T(8,128)S(1)}) custom-call(s32[4]{0:T(128)S(1)} %copy-done.10, bf16[1024,1280]{1,0:T(8,128)(2,1)} %bitcast.13.tok_ref, f32[2,1280]{1,0:T(2,128)S(1)} %copy-done.9, bf16[3,5,64,1024]{3,2,1,0:T(8,128)(2,1)S(1)} %copy-done.12), custom_call_target="tpu_custom_call" | custom-call | flops 2516582400 | bytes 8388608 | tf_op jit(solution)/shard_map/qkv_grad/pallas_call | solution.py:269
  306.3 3.2 fusion.5
  309.5 3.6 fusion.1
  318.5 9.7 %all-to-all-done.6.part_ref = bf16[8,128,1280]{2,1,0:T(8,128)(2,1)S(1)} async-done(((bf16[8,128,1280]{2,1,0:T(8,128)(2,1)}), bf16[8,128,1280]{2,1,0:T(8,128)(2,1)S(1)}, u32[]{:S(2)}, u32[]{:S(2)}) %all-to-all-start.6) | async-done | bytes 2621472 | tf_op jit(solution)/shard_map/all_to_all | solution.py:713
  335.7 5.2 %collective-permute-done.12 = bf16[4,4,64,640]{3,2,1,0:T(8,128)(2,1)} collective-permute-done((bf16[4,4,64,640]{3,2,1,0:T(8,128)(2,1)}, bf16[4,4,64,640]{3,2,1,0:T(8,128)(2,1)}, u32[]{:S(2)}, u32[]{:S(2)}) %collective-permute-start.12) | collective-permute-done | bytes 1310752 | tf_op jit(solution)/shard_map/ppermute | solution.py:633
  354.5 4.5 %collective-permute-done.26 = bf16[4,40,640]{2,1,0:T(8,128)(2,1)} collective-permute-done((bf16[4,40,640]{2,1,0:T(8,128)(2,1)}, bf16[4,40,640]{2,1,0:T(8,128)(2,1)}, u32[]{:S(2)}, u32[]{:S(2)}) %collective-permute-start.26) | collective-permute-done | bytes 204832 | tf_op jit(solution)/shard_map/ppermute | solution.py:633
  362.2 3.9 all-to-all-start.7
  370.8 5.3 %collective-permute-done.28 = bf16[4,40,640]{2,1,0:T(8,128)(2,1)S(1)} collective-permute-done((bf16[4,40,640]{2,1,0:T(8,128)(2,1)S(1)}, bf16[4,40,640]{2,1,0:T(8,128)(2,1)S(1)}, u32[]{:S(2)}, u32[]{:S(2)}) %collective-permute-start.28) | collective-permute-done | bytes 204832 | tf_op jit(solution)/shard_map/ppermute | solution.py:633
  380.9 11.1 %collective-permute-done.15 = bf16[4,64,640]{2,1,0:T(8,128)(2,1)S(1)} collective-permute-done((bf16[4,64,640]{2,1,0:T(8,128)(2,1)S(1)}, bf16[4,64,640]{2,1,0:T(8,128)(2,1)S(1)}, u32[]{:S(2)}, u32[]{:S(2)}) %collective-permute-start.15) | collective-permute-done | bytes 327712 | tf_op jit(solution)/shard_map/ppermute | solution.py:633
  395.6 4.9 %collective-permute-done.16 = bf16[4,64,640]{2,1,0:T(8,128)(2,1)S(1)} collective-permute-done((bf16[4,64,640]{2,1,0:T(8,128)(2,1)S(1)}, bf16[4,64,640]{2,1,0:T(8,128)(2,1)S(1)}, u32[]{:S(2)}, u32[]{:S(2)}) %collective-permute-start.16) | collective-permute-done | bytes 327712 | tf_op jit(solution)/shard_map/ppermute | solution.py:633
  419.9 6.1 %all-to-all-start.8 = ((bf16[8,11,960]{2,1,0:T(8,128)(2,1)}), bf16[8,11,960]{2,1,0:T(8,128)(2,1)S(1)}, u32[]{:S(2)}, u32[]{:S(2)}) async-start(bf16[8,11,960]{2,1,0:T(8,128)(2,1)} %pad_maximum_fusion.1), calls=%async_computation.8 | async-start | bytes 524288 | tf_op jit(solution)/shard_map/all_to_all | solution.py:713
  427.0 7.8 %all-to-all-done.8 = bf16[8,11,960]{2,1,0:T(8,128)(2,1)S(1)} async-done(((bf16[8,11,960]{2,1,0:T(8,128)(2,1)}), bf16[8,11,960]{2,1,0:T(8,128)(2,1)S(1)}, u32[]{:S(2)}, u32[]{:S(2)}) %all-to-all-start.8) | async-done | bytes 168992 | tf_op jit(solution)/shard_map/all_to_all | solution.py:713
  (243 shorter events, 108.7 us)
Async XLA Ops:
  8.9 16.4 %all-to-all-start = ((bf16[8,10,640]{2,1,0:T(8,128)(2,1)}), bf16[8,10,640]{2,1,0:T(8,128)(2,1)S(1)}, u32[]{:S(2)}, u32[]{:S(2)}) async-start(bf16[8,10,640]{2,1,0:T(8,128)(2,1)} %bitcast.174), calls=%async_computation | async-start | bytes 327680 | tf_op jit(solution)/shard_map/all_to_all | solution.py:713
  17.0 149.6 %all-gather.3.cloned.1.call-start = ((), (), s32[]{:S(2)}) async-start(), calls=%async_computation.9 | async-start | bytes 31703040 | tf_op jit(solution)/shard_map/all_gather | solution.py:729
  64.4 41.4 %all-to-all-start.3 = ((bf16[8,128,1280]{2,1,0:T(8,128)(2,1)}), bf16[8,128,1280]{2,1,0:T(8,128)(2,1)}, u32[]{:S(2)}, u32[]{:S(2)}) async-start(bf16[8,128,1280]{2,1,0:T(8,128)(2,1)} %bitcast.12), calls=%async_computation.3 | async-start | bytes 5242880 | tf_op jit(solution)/shard_map/all_to_all | solution.py:713
  123.7 45.8 %all-to-all-start.4 = ((bf16[8,320,128]{2,1,0:T(8,128)(2,1)}), bf16[8,320,128]{2,1,0:T(8,128)(2,1)S(1)}, u32[]{:S(2)}, u32[]{:S(2)}) async-start(bf16[8,320,128]{2,1,0:T(8,128)(2,1)} %get-tuple-element.70), calls=%async_computation.4 | async-start | bytes 1310720 | tf_op jit(solution)/shard_map/all_to_all | solution.py:713
  206.1 10.0 %collective-permute-start.2 = (bf16[256,7680]{1,0:T(8,128)(2,1)}, bf16[256,7680]{1,0:T(8,128)(2,1)}, u32[]{:S(2)}, u32[]{:S(2)}) collective-permute-start(bf16[256,7680]{1,0:T(8,128)(2,1)} %get-tuple-element.76.g_ref), channel_id=1, source_target_pairs={{0,8},{8,0},{1,9},{9,1},{2,10},{10,2},{3,11},{11,3},{4,12},{12,4},... | collective-permute-start | bytes 11796488 | tf_op jit(solution)/shard_map/ppermute | solution.py:596
  206.4 9.3 %collective-permute-start.1 = (bf16[48,80,256]{2,1,0:T(8,128)(2,1)}, bf16[48,80,256]{2,1,0:T(8,128)(2,1)S(1)}, u32[]{:S(2)}, u32[]{:S(2)}) collective-permute-start(bf16[48,80,256]{2,1,0:T(8,128)(2,1)} %get-tuple-element.75), channel_id=1, source_target_pairs={{0,8},{8,0},{1,9},{9,1},{2,10},{10,2},{3,11},{11,3},{4,12},{12,4},... | collective-permute-start | bytes 5898248 | tf_op jit(solution)/shard_map/ppermute | solution.py:596
  206.7 39.5 %all-to-all-start.5 = ((bf16[8,320,128]{2,1,0:T(8,128)(2,1)}), bf16[8,320,128]{2,1,0:T(8,128)(2,1)S(1)}, u32[]{:S(2)}, u32[]{:S(2)}) async-start(bf16[8,320,128]{2,1,0:T(8,128)(2,1)} %bitcast.214), calls=%async_computation.5 | async-start | bytes 1310720 | tf_op jit(solution)/shard_map/all_to_all | solution.py:713
  246.2 22.6 %collective-permute-start.3 = (bf16[8,2,80,640]{3,2,1,0:T(8,128)(2,1)}, bf16[8,2,80,640]{3,2,1,0:T(8,128)(2,1)}, u32[]{:S(2)}, u32[]{:S(2)}) collective-permute-start(bf16[8,2,80,640]{3,2,1,0:T(8,128)(2,1)} %dynamic-slice_bitcast_fusion), channel_id=1, source_target_pairs={{0,32},{32,64},{64,96},{96,0},{8,104},{40,8},{72,40},{104,72},{1,3... | collective-permute-start | bytes 4915208 | tf_op jit(solution)/shard_map/ppermute | solution.py:633
  247.6 19.1 %collective-permute-start.5 = (bf16[4,4,64,640]{3,2,1,0:T(8,128)(2,1)}, bf16[4,4,64,640]{3,2,1,0:T(8,128)(2,1)}, u32[]{:S(2)}, u32[]{:S(2)}) collective-permute-start(bf16[4,4,64,640]{3,2,1,0:T(8,128)(2,1)} %dynamic-slice_bitcast_fusion.1), channel_id=1, source_target_pairs={{0,2},{2,4},{4,6},{6,0},{8,14},{10,8},{12,10},{14,12},{1,3},{3,5},... | collective-permute-start | bytes 3932168 | tf_op jit(solution)/shard_map/ppermute | solution.py:633
  248.1 17.4 %collective-permute-start.4 = (bf16[4,4,40,640]{3,2,1,0:T(8,128)(2,1)S(1)}, bf16[4,4,40,640]{3,2,1,0:T(8,128)(2,1)}, u32[]{:S(2)}, u32[]{:S(2)}) collective-permute-start(bf16[4,4,40,640]{3,2,1,0:T(8,128)(2,1)S(1)} %dynamic-slice_bitcast_fusion.2), channel_id=1, source_target_pairs={{0,16},{16,1},{1,17},{17,0},{8,25},{24,8},{9,24},{25,9},{2,18},{18... | collective-permute-start | bytes 2457608 | tf_op jit(solution)/shard_map/ppermute | solution.py:633
  278.1 25.3 %collective-permute-start.6 = (bf16[8,2,80,640]{3,2,1,0:T(8,128)(2,1)}, bf16[8,2,80,640]{3,2,1,0:T(8,128)(2,1)}, u32[]{:S(2)}, u32[]{:S(2)}) collective-permute-start(bf16[8,2,80,640]{3,2,1,0:T(8,128)(2,1)} %fusion.2), channel_id=1, source_target_pairs={{0,32},{32,64},{64,96},{96,0},{8,104},{40,8},{72,40},{104,72},{1,3... | collective-permute-start | bytes 4915208 | tf_op jit(solution)/shard_map/ppermute | solution.py:633
  278.3 25.0 %collective-permute-start.8 = (bf16[4,4,64,640]{3,2,1,0:T(8,128)(2,1)}, bf16[4,4,64,640]{3,2,1,0:T(8,128)(2,1)}, u32[]{:S(2)}, u32[]{:S(2)}) collective-permute-start(bf16[4,4,64,640]{3,2,1,0:T(8,128)(2,1)} %fusion.6), channel_id=1, source_target_pairs={{0,2},{2,4},{4,6},{6,0},{8,14},{10,8},{12,10},{14,12},{1,3},{3,5},... | collective-permute-start | bytes 3932168 | tf_op jit(solution)/shard_map/ppermute | solution.py:633
  278.8 24.5 %collective-permute-start.7 = (bf16[4,4,40,640]{3,2,1,0:T(8,128)(2,1)}, bf16[4,4,40,640]{3,2,1,0:T(8,128)(2,1)}, u32[]{:S(2)}, u32[]{:S(2)}) collective-permute-start(bf16[4,4,40,640]{3,2,1,0:T(8,128)(2,1)} %fusion.9), channel_id=1, source_target_pairs={{0,16},{16,1},{1,17},{17,0},{8,25},{24,8},{9,24},{25,9},{2,18},{18... | collective-permute-start | bytes 2457608 | tf_op jit(solution)/shard_map/ppermute | solution.py:633
  287.0 41.2 %all-to-all-start.6 = ((bf16[8,128,1280]{2,1,0:T(8,128)(2,1)}), bf16[8,128,1280]{2,1,0:T(8,128)(2,1)S(1)}, u32[]{:S(2)}, u32[]{:S(2)}) async-start(bf16[8,128,1280]{2,1,0:T(8,128)(2,1)} %copy-done.5), calls=%async_computation.6 | async-start | bytes 5242880 | tf_op jit(solution)/shard_map/all_to_all | solution.py:713
  313.1 27.7 %collective-permute-start.10 = (bf16[8,2,80,640]{3,2,1,0:T(8,128)(2,1)}, bf16[8,2,80,640]{3,2,1,0:T(8,128)(2,1)}, u32[]{:S(2)}, u32[]{:S(2)}) collective-permute-start(bf16[8,2,80,640]{3,2,1,0:T(8,128)(2,1)} %fusion.1), channel_id=1, source_target_pairs={{0,32},{32,64},{64,96},{96,0},{8,104},{40,8},{72,40},{104,72},{1,3... | collective-permute-start | bytes 4915208 | tf_op jit(solution)/shard_map/ppermute | solution.py:633
  314.6 17.0 %collective-permute-start.9 = (bf16[8,80,960]{2,1,0:T(8,128)(2,1)}, bf16[8,80,960]{2,1,0:T(8,128)(2,1)}, u32[]{:S(2)}, u32[]{:S(2)}) collective-permute-start(bf16[8,80,960]{2,1,0:T(8,128)(2,1)} %get-tuple-element.101), channel_id=1, source_target_pairs={{0,8},{8,0},{1,9},{9,1},{2,10},{10,2},{3,11},{11,3},{4,12},{12,4},... | collective-permute-start | bytes 3686408 | tf_op jit(solution)/shard_map/ppermute | solution.py:596
  314.6 26.3 %collective-permute-start.12 = (bf16[4,4,64,640]{3,2,1,0:T(8,128)(2,1)}, bf16[4,4,64,640]{3,2,1,0:T(8,128)(2,1)}, u32[]{:S(2)}, u32[]{:S(2)}) collective-permute-start(bf16[4,4,64,640]{3,2,1,0:T(8,128)(2,1)} %fusion.5), channel_id=1, source_target_pairs={{0,2},{2,4},{4,6},{6,0},{8,14},{10,8},{12,10},{14,12},{1,3},{3,5},... | collective-permute-start | bytes 3932168 | tf_op jit(solution)/shard_map/ppermute | solution.py:633
  316.8 18.9 %collective-permute-start.11 = (bf16[4,4,40,640]{3,2,1,0:T(8,128)(2,1)}, bf16[4,4,40,640]{3,2,1,0:T(8,128)(2,1)}, u32[]{:S(2)}, u32[]{:S(2)}) collective-permute-start(bf16[4,4,40,640]{3,2,1,0:T(8,128)(2,1)} %fusion.8), channel_id=1, source_target_pairs={{0,16},{16,1},{1,17},{17,0},{8,25},{24,8},{9,24},{25,9},{2,18},{18... | collective-permute-start | bytes 2457608 | tf_op jit(solution)/shard_map/ppermute | solution.py:633
  353.3 15.9 %collective-permute-start.14 = (bf16[4,64,640]{2,1,0:T(8,128)(2,1)}, bf16[4,64,640]{2,1,0:T(8,128)(2,1)}, u32[]{:S(2)}, u32[]{:S(2)}) collective-permute-start(bf16[4,64,640]{2,1,0:T(8,128)(2,1)} %dynamic-slice_bitcast_fusion.4), channel_id=1, source_target_pairs={{0,32},{32,64},{64,96},{96,0},{8,104},{40,8},{72,40},{104,72},{1,3... | collective-permute-start | bytes 983048 | tf_op jit(solution)/shard_map/ppermute | solution.py:633
  353.4 38.9 %collective-permute-start.20 = (bf16[4,80,640]{2,0,1:T(4,128)(2,1)}, bf16[4,80,640]{2,0,1:T(4,128)(2,1)S(1)}, u32[]{:S(2)}, u32[]{:S(2)}) collective-permute-start(bf16[4,80,640]{2,0,1:T(4,128)(2,1)} %dynamic-slice_bitcast_fusion.3), channel_id=1, source_target_pairs={{0,16},{16,1},{1,17},{17,0},{8,25},{24,8},{9,24},{25,9},{2,18},{18... | collective-permute-start | bytes 1228808 | tf_op jit(solution)/shard_map/ppermute | solution.py:633
  362.2 49.2 %all-to-all-start.7 = ((bf16[8,88,960]{2,1,0:T(8,128)(2,1)}), bf16[8,88,960]{2,1,0:T(8,128)(2,1)S(1)}, u32[]{:S(2)}, u32[]{:S(2)}) async-start(bf16[8,88,960]{2,1,0:T(8,128)(2,1)} %fusion.10), calls=%async_computation.7 | async-start | bytes 2883584 | tf_op jit(solution)/shard_map/all_to_all | solution.py:812
  370.4 21.7 %collective-permute-start.15 = (bf16[4,64,640]{2,1,0:T(8,128)(2,1)S(1)}, bf16[4,64,640]{2,1,0:T(8,128)(2,1)S(1)}, u32[]{:S(2)}, u32[]{:S(2)}) collective-permute-start(bf16[4,64,640]{2,1,0:T(8,128)(2,1)S(1)} %fusion.16), channel_id=1, source_target_pairs={{0,32},{32,64},{64,96},{96,0},{8,104},{40,8},{72,40},{104,72},{1,3... | collective-permute-start | bytes 983048 | tf_op jit(solution)/shard_map/ppermute | solution.py:633
  377.2 17.0 %collective-permute-start.29 = (bf16[40,640]{1,0:T(8,128)(2,1)S(1)}, bf16[40,640]{1,0:T(8,128)(2,1)S(1)}, u32[]{:S(2)}, u32[]{:S(2)}) collective-permute-start(bf16[40,640]{1,0:T(8,128)(2,1)S(1)} %get-tuple-element.128), channel_id=1, source_target_pairs={{0,32},{32,64},{64,96},{96,0},{1,33},{33,65},{65,97},{97,1},{2,34}... | collective-permute-start | bytes 153608 | tf_op jit(solution)/shard_map/ppermute | solution.py:638
  377.6 16.6 %collective-permute-start.31 = (bf16[40,640]{1,0:T(8,128)(2,1)S(1)}, bf16[40,640]{1,0:T(8,128)(2,1)S(1)}, u32[]{:S(2)}, u32[]{:S(2)}) collective-permute-start(bf16[40,640]{1,0:T(8,128)(2,1)S(1)} %get-tuple-element.129), channel_id=1, source_target_pairs={{0,96},{32,0},{64,32},{96,64},{1,97},{33,1},{65,33},{97,65},{2,98}... | collective-permute-start | bytes 153608 | tf_op jit(solution)/shard_map/ppermute | solution.py:638
  380.5 15.1 %collective-permute-start.30 = (bf16[40,640]{1,0:T(8,128)(2,1)S(1)}, bf16[40,640]{1,0:T(8,128)(2,1)S(1)}, u32[]{:S(2)}, u32[]{:S(2)}) collective-permute-start(bf16[40,640]{1,0:T(8,128)(2,1)S(1)} %get-tuple-element.130), channel_id=1, source_target_pairs={{0,64},{32,96},{64,0},{96,32},{1,65},{33,97},{65,1},{97,33},{2,66}... | collective-permute-start | bytes 153608 | tf_op jit(solution)/shard_map/ppermute | solution.py:638
  392.2 8.4 %collective-permute-start.16 = (bf16[4,64,640]{2,1,0:T(8,128)(2,1)S(1)}, bf16[4,64,640]{2,1,0:T(8,128)(2,1)S(1)}, u32[]{:S(2)}, u32[]{:S(2)}) collective-permute-start(bf16[4,64,640]{2,1,0:T(8,128)(2,1)S(1)} %fusion.15), channel_id=1, source_target_pairs={{0,32},{32,64},{64,96},{96,0},{8,104},{40,8},{72,40},{104,72},{1,3... | collective-permute-start | bytes 983048 | tf_op jit(solution)/shard_map/ppermute | solution.py:633
  392.5 11.8 %collective-permute-start.21 = (bf16[4,80,640]{2,0,1:T(4,128)(2,1)S(1)}, bf16[4,80,640]{2,0,1:T(4,128)(2,1)S(1)}, u32[]{:S(2)}, u32[]{:S(2)}) collective-permute-start(bf16[4,80,640]{2,0,1:T(4,128)(2,1)S(1)} %fusion.13), channel_id=1, source_target_pairs={{0,16},{16,1},{1,17},{17,0},{8,25},{24,8},{9,24},{25,9},{2,18},{18... | collective-permute-start | bytes 1228808 | tf_op jit(solution)/shard_map/ppermute | solution.py:633
  405.3 9.5 %collective-permute-start.22 = (bf16[4,80,640]{2,0,1:T(4,128)(2,1)}, bf16[4,80,640]{2,0,1:T(4,128)(2,1)}, u32[]{:S(2)}, u32[]{:S(2)}) collective-permute-start(bf16[4,80,640]{2,0,1:T(4,128)(2,1)} %fusion.12), channel_id=1, source_target_pairs={{0,16},{16,1},{1,17},{17,0},{8,25},{24,8},{9,24},{25,9},{2,18},{18... | collective-permute-start | bytes 1228808 | tf_op jit(solution)/shard_map/ppermute | solution.py:633
  416.9 9.1 %collective-permute-start.24 = (bf16[80,640]{1,0:T(8,128)(2,1)S(1)}, bf16[80,640]{1,0:T(8,128)(2,1)S(1)}, u32[]{:S(2)}, u32[]{:S(2)}) collective-permute-start(bf16[80,640]{1,0:T(8,128)(2,1)S(1)} %bitcast.229), channel_id=1, source_target_pairs={{0,4},{2,6},{4,0},{6,2},{1,5},{3,7},{5,1},{7,3},{8,12},{10,14},{12... | collective-permute-start | bytes 307208 | tf_op jit(solution)/shard_map/ppermute | solution.py:638
  417.0 9.0 %collective-permute-start.25 = (bf16[80,640]{1,0:T(8,128)(2,1)S(1)}, bf16[80,640]{1,0:T(8,128)(2,1)S(1)}, u32[]{:S(2)}, u32[]{:S(2)}) collective-permute-start(bf16[80,640]{1,0:T(8,128)(2,1)S(1)} %bitcast.228), channel_id=1, source_target_pairs={{0,6},{2,0},{4,2},{6,4},{1,7},{3,1},{5,3},{7,5},{8,14},{10,8},{12,... | collective-permute-start | bytes 307208 | tf_op jit(solution)/shard_map/ppermute | solution.py:638
  417.7 8.3 %collective-permute-start.23 = (bf16[80,640]{1,0:T(8,128)(2,1)S(1)}, bf16[80,640]{1,0:T(8,128)(2,1)S(1)}, u32[]{:S(2)}, u32[]{:S(2)}) collective-permute-start(bf16[80,640]{1,0:T(8,128)(2,1)S(1)} %bitcast.227), channel_id=1, source_target_pairs={{0,2},{2,4},{4,6},{6,0},{1,3},{3,5},{5,7},{7,1},{8,10},{10,12},{12... | collective-permute-start | bytes 307208 | tf_op jit(solution)/shard_map/ppermute | solution.py:638
  419.9 14.9 %all-to-all-start.8 = ((bf16[8,11,960]{2,1,0:T(8,128)(2,1)}), bf16[8,11,960]{2,1,0:T(8,128)(2,1)S(1)}, u32[]{:S(2)}, u32[]{:S(2)}) async-start(bf16[8,11,960]{2,1,0:T(8,128)(2,1)} %pad_maximum_fusion.1), calls=%async_computation.8 | async-start | bytes 524288 | tf_op jit(solution)/shard_map/all_to_all | solution.py:713
  (37 other events, 383.7 us)
Sparse Core Ops, SparseCore 0:
  26.2 140.3 all-gather.2

commit v4 on v3

v4 whole, which is shorter than its diff:
```python
import functools
import math

import jax
import jax.numpy as jnp
from jax import lax
from jax.experimental import pallas as pl
from jax.experimental.pallas import tpu as pltpu
from jax.sharding import Mesh
from jax.sharding import PartitionSpec as P

HEADS = 20
NORM_EPS = 1e-05
MASKED = -1000000000.0

F32 = jnp.float32
BF16 = jnp.bfloat16

AXES = ("x", "yl", "c", "z", "yh")
SIZES = (4, 2, 2, 4, 2)
DP = ("x", "yl", "c")
CTX = ("z", "yh")
PLACE = ("z", "yh", "yl", "x", "c")

D = 1280
SPAN = 128
SEQ_GRP = 2
ROWS = SEQ_GRP * SPAN
CTX_N = 8
LEN = CTX_N * SPAN
HEAD_DIM = D // HEADS
GROUP_HEADS = 5
GROUP_W = GROUP_HEADS * HEAD_DIM
COLS = 640
BLK = 80
SCALE = 1.0 / math.sqrt(HEAD_DIM)
Q_BLOCK = 256
HEADS_W = 3 * GROUP_W
PIECE = 32
LAST = 24
MB = 1 << 20
SHORT = 1000


def place_of(dp):
    x, yl, c = dp // 4, (dp // 2) % 2, dp % 2
    return (yl * 4 + x) * 2 + c


def dot(left, right):
    return lax.dot_general(
        left, right, (((1,), (0,)), ((), ())), preferred_element_type=F32
    )


def dot_nt(left, right):
    return lax.dot_general(
        left, right, (((1,), (1,)), ((), ())), preferred_element_type=F32
    )


def norm_stats(rows):
    centre = jnp.mean(rows, axis=-1, keepdims=True)
    centred = rows - centre
    spread = jnp.mean(centred * centred, axis=-1, keepdims=True)
    scale = lax.rsqrt(spread + NORM_EPS)
    return centred * scale, scale


def norm_back(normed, scale, gain, grad):
    scaled = gain * grad
    mean_one = jnp.mean(scaled, axis=-1, keepdims=True)
    mean_two = jnp.mean(scaled * normed, axis=-1, keepdims=True)
    return (scaled - mean_one - normed * mean_two) * scale


def stack_rows(ref, *lead):
    return jnp.concatenate([ref[(*lead, place_of(dp))] for dp in range(16)], axis=0)


def params(vmem_mb):
    return pltpu.CompilerParams(vmem_limit_bytes=vmem_mb * MB)


def cost(flops, nbytes, trans=0):
    return pl.CostEstimate(
        flops=flops // SHORT, bytes_accessed=nbytes // SHORT, transcendentals=trans // SHORT
    )


def whole(shape):
    return pl.BlockSpec(shape, lambda *i: (0,) * len(shape))


def turn(block):
    return block.astype(F32).T.astype(BF16)


def allowed_of(length, first_query, key_count, query_count):
    key_pos = lax.broadcasted_iota(jnp.int32, (key_count, query_count), 0)
    query_pos = first_query + lax.broadcasted_iota(
        jnp.int32, (key_count, query_count), 1
    )
    return (key_pos <= query_pos) & (key_pos < length)


def attend_kernel(
    len_ref, tok_ref, norm_ref, bias_ref, w_ref, qkv_ref, out_ref, lse_ref
):
    head = pl.program_id(0)

    @pl.when(head == 0)
    def _():
        weight = w_ref[...].reshape(D, HEADS_W)
        for block in range(LEN // Q_BLOCK):
            cut = slice(block * Q_BLOCK, (block + 1) * Q_BLOCK)
            normed, _ = norm_stats(tok_ref[cut].astype(F32))
            normed = (normed * norm_ref[0:1] + norm_ref[1:2]).astype(BF16)
            turned = (dot(normed, weight) + bias_ref[...]).T.astype(BF16)
            for row in range(3 * GROUP_HEADS):
                qkv_ref[row // GROUP_HEADS, row % GROUP_HEADS, :, cut] = turned[
                    row * HEAD_DIM : (row + 1) * HEAD_DIM
                ]

    length = len_ref[0]
    query = qkv_ref[0, head]
    key = turn(qkv_ref[1, head])
    value = qkv_ref[2, head]
    for block in range(LEN // Q_BLOCK):
        first = block * Q_BLOCK
        last = first + Q_BLOCK
        scores = dot(key[:last], query[:, first:last]) * SCALE
        scores = jnp.where(allowed_of(length, first, last, Q_BLOCK), scores, MASKED)
        top = jnp.max(scores, axis=0, keepdims=True)
        weights = jnp.exp(scores - top)
        total = jnp.sum(weights, axis=0, keepdims=True)
        result = dot(value[:, :last], weights.astype(BF16)) / total
        lse_ref[0, :, first:last] = top + jnp.log(total)
        result = result.astype(BF16)
        for part in range(Q_BLOCK // SPAN):
            out_ref[first // SPAN + part] = result[:, part * SPAN : (part + 1) * SPAN]


def attend_call(length, tok, norm, bias, w_qkv):
    return pl.pallas_call(
        attend_kernel,
        grid=(GROUP_HEADS,),
        in_specs=[
            pl.BlockSpec(memory_space=pltpu.SMEM),
            whole((LEN, D)),
            whole((2, D)),
            whole((1, HEADS_W)),
            whole((16, BLK, HEADS_W)),
        ],
        out_specs=[
            whole((3, GROUP_HEADS, HEAD_DIM, LEN)),
            pl.BlockSpec((CTX_N, HEAD_DIM, SPAN), lambda h: (0, h, 0)),
            pl.BlockSpec((1, 1, LEN), lambda h: (h, 0, 0)),
        ],
        out_shape=[
            jax.ShapeDtypeStruct((3, GROUP_HEADS, HEAD_DIM, LEN), BF16),
            jax.ShapeDtypeStruct((CTX_N, GROUP_W, SPAN), BF16),
            jax.ShapeDtypeStruct((GROUP_HEADS, 1, LEN), F32),
        ],
        compiler_params=params(60),
        cost_estimate=cost(
            6 * LEN * LEN * 4 * HEAD_DIM + 2 * LEN * D * HEADS_W, 8 * MB, 3 * LEN * LEN
        ),
        name="attend",
    )(length, tok, norm, bias, w_qkv)


def attend_back_kernel(len_ref, qkv_ref, grad_ref, lse_ref, g_ref, gk_ref, gv_ref):
    length = len_ref[0]
    query = qkv_ref[0, 0]
    key_t = qkv_ref[1, 0]
    key = turn(key_t)
    value = turn(qkv_ref[2, 0])
    grad = jnp.concatenate([grad_ref[p] for p in range(CTX_N)], axis=1)
    gk_ref[...] = jnp.zeros_like(gk_ref)
    gv_ref[...] = jnp.zeros_like(gv_ref)
    for block in range(LEN // Q_BLOCK):
        first = block * Q_BLOCK
        last = first + Q_BLOCK
        query_b = query[:, first:last]
        grad_b = grad[:, first:last]
        scores = dot(key[:last], query_b) * SCALE
        probs = jnp.where(
            allowed_of(length, first, last, Q_BLOCK),
            jnp.exp(scores - lse_ref[0, :, first:last]),
            0.0,
        )
        grad_probs = dot(value[:last], grad_b)
        delta = jnp.sum(probs * grad_probs, axis=0, keepdims=True)
        grad_scores = (probs * (grad_probs - delta)).astype(BF16)
        g_ref[0, 0, :, first:last] = (dot(key_t[:, :last], grad_scores) * SCALE).astype(
            BF16
        )
        gk_ref[:, :last] += dot_nt(query_b, grad_scores)
        gv_ref[:, :last] += dot_nt(grad_b, probs.astype(BF16))
    g_ref[1, 0] = (gk_ref[...] * SCALE).astype(BF16)
    g_ref[2, 0] = gv_ref[...].astype(BF16)


def attend_back_call(length, qkv, grad, lse):
    heads = pl.BlockSpec((3, 1, HEAD_DIM, LEN), lambda h: (0, h, 0, 0))
    return pl.pallas_call(
        attend_back_kernel,
        grid=(GROUP_HEADS,),
        in_specs=[
            pl.BlockSpec(memory_space=pltpu.SMEM),
            heads,
            pl.BlockSpec((CTX_N, HEAD_DIM, SPAN), lambda h: (0, h, 0)),
            pl.BlockSpec((1, 1, LEN), lambda h: (h, 0, 0)),
        ],
        out_specs=heads,
        out_shape=jax.ShapeDtypeStruct((3, GROUP_HEADS, HEAD_DIM, LEN), BF16),
        scratch_shapes=[pltpu.VMEM((HEAD_DIM, LEN), F32)] * 2,
        compiler_params=params(60),
        cost_estimate=cost(15 * LEN * LEN * 4 * HEAD_DIM, 5 * MB, 3 * LEN * LEN),
        name="attend_back",
    )(length, qkv, grad, lse)


def norm_grad_kernel(tok_ref, w_ref, g_ref, out_ref, d_norm_ref):
    weight = w_ref[...].reshape(D, HEADS_W)
    grads = turn(g_ref[...].reshape(HEADS_W, Q_BLOCK))
    g_norm = dot_nt(grads, weight)
    normed, _ = norm_stats(tok_ref[...].astype(F32))

    @pl.when(pl.program_id(0) == 0)
    def _():
        d_norm_ref[...] = jnp.zeros_like(d_norm_ref)

    d_norm_ref[0:1] += jnp.sum(g_norm * normed, axis=0, keepdims=True)
    d_norm_ref[1:2] += jnp.sum(g_norm, axis=0, keepdims=True)
    g_norm = g_norm.astype(BF16)
    for part in range(Q_BLOCK // SPAN):
        out_ref[part] = g_norm[part * SPAN : (part + 1) * SPAN]


def norm_grad_call(tok, w_qkv, g_qkv):
    return pl.pallas_call(
        norm_grad_kernel,
        grid=(LEN // Q_BLOCK,),
        in_specs=[
            pl.BlockSpec((Q_BLOCK, D), lambda i: (i, 0)),
            whole((16, BLK, HEADS_W)),
            pl.BlockSpec((3, GROUP_HEADS, HEAD_DIM, Q_BLOCK), lambda i: (0, 0, 0, i)),
        ],
        out_specs=[
            pl.BlockSpec((Q_BLOCK // SPAN, SPAN, D), lambda i: (i, 0, 0)),
            whole((2, D)),
        ],
        out_shape=[
            jax.ShapeDtypeStruct((CTX_N, SPAN, D), BF16),
            jax.ShapeDtypeStruct((2, D), F32),
        ],
        compiler_params=params(60),
        cost_estimate=cost(2 * LEN * D * HEADS_W, 10 * MB),
        name="norm_grad",
    )(tok, w_qkv, g_qkv)


def qkv_grad_kernel(
    info_ref,
    tok_ref,
    norm_ref,
    g_ref,
    d_norm_ref,
    d_vec_ref,
    d_fc_bias_ref,
    keep_ref,
    give_ref,
    n1t_ref,
    small_ref,
):
    core = info_ref[SEQ_GRP + 1]
    for block in range(LEN // Q_BLOCK):
        cut = slice(block * Q_BLOCK, (block + 1) * Q_BLOCK)
        normed, _ = norm_stats(tok_ref[cut].astype(F32))
        turned = (normed * norm_ref[0:1] + norm_ref[1:2]).T.astype(BF16)
        for dp in range(16):
            n1t_ref[dp % 2, dp // 2, :, cut] = turned[dp * BLK : (dp + 1) * BLK]
    grads = g_ref[...].reshape(HEADS_W, LEN)

    d_bias = dot_nt(jnp.ones((8, LEN), BF16), grads)
    own = lax.broadcasted_iota(jnp.int32, (1, D), 1) // GROUP_W == info_ref[SEQ_GRP + 4]
    vectors = [d_norm_ref[0:1], d_norm_ref[1:2]]
    for third in (0, 2):
        part = d_bias[0:1, third * GROUP_W : (third + 1) * GROUP_W]
        vectors.append(jnp.where(own, jnp.concatenate([part] * 4, axis=1), 0.0))
    vectors += [d_vec_ref[k : k + 1] for k in range(4)]
    small = None
    for k, vector in enumerate(vectors + [d_fc_bias_ref[...]]):
        each = 10 if k < 8 else 40
        width = 128 * each
        owner = lax.broadcasted_iota(jnp.int32, (128, width), 1) // each
        mask = owner == lax.broadcasted_iota(jnp.int32, (128, width), 0)
        feature = lax.broadcasted_iota(jnp.int32, (width, 128), 0) % each
        lane = lax.broadcasted_iota(jnp.int32, (width, 128), 1)
        place = (feature + 10 * k == lane).astype(F32).astype(BF16)
        part = dot(jnp.where(mask, vector, 0.0).astype(BF16), place)
        small = part if small is None else small + part
    for dp in range(16):
        small_ref[dp % 2, dp // 2] = small[dp * 8 : (dp + 1) * 8]

    for side, ref in ((core, keep_ref), (1 - core, give_ref)):
        for half in range(2):
            rows = n1t_ref[side, 4 * half : 4 * half + 4].reshape(4 * BLK, LEN)
            ref[4 * half : 4 * half + 4, :BLK] = (
                dot_nt(rows, grads).astype(BF16).reshape(4, BLK, HEADS_W)
            )
        ref[:, BLK:] = jnp.zeros((8, 16, HEADS_W), BF16)
        ref[:, BLK : BLK + 8, :128] = small_ref[side].astype(BF16)


def qkv_grad_call(info, tok, norm, g_qkv, d_norm, d_vecs, d_fc_bias):
    half = jax.ShapeDtypeStruct((8, BLK + 16, HEADS_W), BF16)
    vmem = pl.BlockSpec(memory_space=pltpu.VMEM)
    return pl.pallas_call(
        qkv_grad_kernel,
        in_specs=[pl.BlockSpec(memory_space=pltpu.SMEM)] + [vmem] * 6,
        out_specs=[vmem, vmem],
        out_shape=[half, half],
        scratch_shapes=[
            pltpu.VMEM((2, 8, BLK, LEN), BF16),
            pltpu.VMEM((2, 8, 8, 128), F32),
        ],
        compiler_params=params(60),
        cost_estimate=cost(2 * LEN * D * HEADS_W, 8 * MB),
        name="qkv_grad",
    )(info, tok, norm, g_qkv, d_norm, d_vecs, d_fc_bias)


def norm_back_kernel(
    seq_ref, tok_ref, gain_ref, g_res_ref, own_ref, other_ref, in_grad_ref
):
    for seq, ref in ((seq_ref[0], own_ref), (1 - seq_ref[0], other_ref)):
        cut = pl.ds(pl.multiple_of(seq * SPAN, SPAN), SPAN)
        normed, scale = norm_stats(tok_ref[cut].astype(F32))
        in_grad_ref[cut] = g_res_ref[cut].astype(F32) + norm_back(
            normed, scale, gain_ref[...], ref[...].astype(F32)
        )


def norm_back_call(seq, tok, gain, g_res, own, other):
    vmem = pl.BlockSpec(memory_space=pltpu.VMEM)
    return pl.pallas_call(
        norm_back_kernel,
        in_specs=[pl.BlockSpec(memory_space=pltpu.SMEM)] + [vmem] * 5,
        out_specs=vmem,
        out_shape=jax.ShapeDtypeStruct((ROWS, D), F32),
        compiler_params=params(60),
        cost_estimate=cost(40 * ROWS * D, 4 * MB),
        name="norm_back",
    )(seq, tok, gain, g_res, own, other)


def mlp_kernel(
    info_ref,
    tok_ref,
    cot_ref,
    att_ref,
    vec_ref,
    fc_bias_ref,
    wp_ref,
    wf_ref,
    wo_ref,
    out_ref,
    g_res_ref,
    g_att_ref,
    d_vec_ref,
    d_fc_bias_ref,
    rows_ref,
    keep_ref,
    give_ref,
    n2_ref,
    g_out_ref,
    res_ref,
    acc_ref,
    gn_ref,
    wp_all_ref,
    turned_ref,
):
    step = pl.program_id(0)
    core = info_ref[SEQ_GRP + 1]
    proj_shift, gain, shift, out_shift = (vec_ref[k : k + 1] for k in range(4))

    def by_core(turned, first):
        for dp in range(16):
            turned_ref[dp % 2, place_of(dp) // 2] = turned[dp * BLK : (dp + 1) * BLK]
        keep_ref[first : first + 8] = turned_ref[core]
        give_ref[first : first + 8] = turned_ref[1 - core]

    @pl.when(step == 0)
    def _():
        turned = jnp.concatenate(
            [
                jnp.concatenate([att_ref[g, s] for g in range(4)], axis=0)
                for s in range(SEQ_GRP)
            ],
            axis=1,
        )
        att = turn(turned)
        for half in range(2):
            cut = slice(half * COLS, (half + 1) * COLS)
            pack = pack_of(half, PIECE, (BLK, CTX_N * PIECE), 0, 1)
            for dp in range(16):
                pieces = wp_ref[:, place_of(dp)].reshape(CTX_N * PIECE, COLS)
                wp_all_ref[dp * BLK : (dp + 1) * BLK, cut] = dot(pack, pieces).astype(
                    BF16
                )
        residual = tok_ref[...].astype(F32) + dot(att, wp_all_ref[...]) + proj_shift
        res_ref[...] = residual
        normed, _ = norm_stats(residual)
        normed = normed * gain + shift
        n2_ref[...] = normed.astype(BF16)
        by_core(normed.T.astype(BF16), 32)
        by_core(turned, 40)
        for seq in range(SEQ_GRP):
            cut = slice(seq * SPAN, (seq + 1) * SPAN)
            pos = info_ref[SEQ_GRP] + lax.broadcasted_iota(jnp.int32, (SPAN, D), 0)
            g_out_ref[cut] = jnp.where(
                pos < info_ref[seq], cot_ref[cut], jnp.zeros((SPAN, D), BF16)
            )
        rows_ref[:, 4 * D : 5 * D] = g_out_ref[...]
        acc_ref[...] = residual + out_shift
        gn_ref[...] = jnp.zeros_like(gn_ref)

    w_fc = jnp.concatenate([stack_rows(wf_ref, 0), stack_rows(wf_ref, 1)], axis=1)
    pre = dot(n2_ref[...], w_fc) + fc_bias_ref[...]
    root = math.sqrt(2.0 / math.pi)
    square = pre * pre
    bend = jnp.tanh(root * pre * (1.0 + 0.044715 * square))
    gate = 0.5 * (1.0 + bend)
    slope = gate + 0.5 * pre * (1.0 - bend * bend) * root * (
        1.0 + 3.0 * 0.044715 * square
    )
    act = pre * gate
    act_t = act.T.astype(BF16).reshape(2, 2, 4, BLK, ROWS)
    act = act.astype(BF16)
    for c in range(2):
        turned_ref[c] = act_t[:, c].reshape(8, BLK, ROWS)
    keep_ref[pl.ds(step * 8, 8)] = turned_ref[core]
    give_ref[pl.ds(step * 8, 8)] = turned_ref[1 - core]
    w_out = jnp.concatenate(
        [
            jnp.concatenate(
                [
                    wo_ref[z, yh, yl, 0, c, half * 40 : (half + 1) * 40]
                    for yl in range(2)
                    for c in range(2)
                    for z in range(4)
                    for yh in range(2)
                ],
                axis=0,
            )
            for half in range(2)
        ],
        axis=1,
    )
    acc_ref[...] += dot(act, w_out)
    g_act = dot_nt(g_out_ref[...], w_out)
    g_pre = (g_act * slope).astype(BF16)
    rows_ref[:, pl.ds(pl.multiple_of(step * D, D), D)] = g_pre
    d_fc_bias_ref[...] = jnp.sum(g_pre.astype(F32), axis=0, keepdims=True)
    gn_ref[...] += dot_nt(g_pre, w_fc)

    @pl.when(step == pl.num_programs(0) - 1)
    def _():
        out_ref[...] = acc_ref[...].astype(BF16)
        normed, scale = norm_stats(res_ref[...])
        g_norm = gn_ref[...]
        g_out = g_out_ref[...].astype(F32)
        g_res = (g_out + norm_back(normed, scale, gain, g_norm)).astype(BF16)
        g_res_ref[...] = g_res
        rows_ref[:, 5 * D :] = g_res
        d_vec_ref[0:1] = jnp.sum(g_res.astype(F32), axis=0, keepdims=True)
        d_vec_ref[1:2] = jnp.sum(g_norm * normed, axis=0, keepdims=True)
        d_vec_ref[2:3] = jnp.sum(g_norm, axis=0, keepdims=True)
        d_vec_ref[3:4] = jnp.sum(g_out, axis=0, keepdims=True)
        g_att = dot_nt(g_res, wp_all_ref[...])
        for seq in range(SEQ_GRP):
            turned = g_att[seq * SPAN : (seq + 1) * SPAN].T.astype(BF16)
            for g in range(4):
                g_att_ref[g, seq] = turned[g * GROUP_W : (g + 1) * GROUP_W]


def pack_of(half, piece, shape, row_dim, piece_dim):
    row = lax.broadcasted_iota(jnp.int32, shape, row_dim)
    place = lax.broadcasted_iota(jnp.int32, shape, piece_dim)
    offset = place - (piece - 10) * (row // 10) - 10 * half
    return (offset == row).astype(F32).astype(BF16)


def mlp_call(info, tok, cot, att, vecs, fc_bias, weights):
    by_ctx = weights.reshape(CTX_N, 16, 2 * BLK + PIECE, COLS)
    by_chip = weights.reshape(4, 2, 2, 4, 2, 2 * BLK + PIECE, COLS)
    rows = jax.ShapeDtypeStruct((ROWS, D), BF16)
    turned = jax.ShapeDtypeStruct((48, BLK, ROWS), BF16)
    return pl.pallas_call(
        mlp_kernel,
        grid=(4,),
        in_specs=[
            pl.BlockSpec(memory_space=pltpu.SMEM),
            whole((ROWS, D)),
            whole((ROWS, D)),
            whole((4, SEQ_GRP, GROUP_W, SPAN)),
            whole((4, D)),
            pl.BlockSpec((1, D), lambda j: (0, j)),
            pl.BlockSpec((CTX_N, 16, PIECE, COLS), lambda j: (0, 0, 5, 0)),
            pl.BlockSpec((2, 16, BLK, COLS), lambda j: (j, 0, 0, 0)),
            pl.BlockSpec(
                (4, 2, 2, 1, 2, BLK, COLS), lambda j: (0, 0, 0, j, 0, 1, 0)
            ),
        ],
        out_specs=[
            whole((ROWS, D)),
            whole((ROWS, D)),
            whole((4, SEQ_GRP, GROUP_W, SPAN)),
            whole((4, D)),
            pl.BlockSpec((1, D), lambda j: (0, j)),
            whole((ROWS, 6 * D)),
            whole((48, BLK, ROWS)),
            whole((48, BLK, ROWS)),
        ],
        out_shape=[
            rows,
            rows,
            jax.ShapeDtypeStruct((4, SEQ_GRP, GROUP_W, SPAN), BF16),
            jax.ShapeDtypeStruct((4, D), F32),
            jax.ShapeDtypeStruct((1, 4 * D), F32),
            jax.ShapeDtypeStruct((ROWS, 6 * D), BF16),
            turned,
            turned,
        ],
        scratch_shapes=[
            pltpu.VMEM((ROWS, D), BF16),
            pltpu.VMEM((ROWS, D), BF16),
            pltpu.VMEM((ROWS, D), F32),
            pltpu.VMEM((ROWS, D), F32),
            pltpu.VMEM((ROWS, D), F32),
            pltpu.VMEM((D, D), BF16),
            pltpu.VMEM((2, 8, BLK, ROWS), BF16),
        ],
        compiler_params=params(60),
        cost_estimate=cost(2 * ROWS * D * (16 * D + 2 * D), 38 * MB, 2 * ROWS * 4 * D),
        name="mlp",
    )(info, tok, cot, att, vecs, fc_bias, by_ctx, by_ctx, by_chip)


def both(ref, other_ref, axis):
    return jnp.concatenate([ref[...], other_ref[...]], axis=axis)


def fc_grad_kernel(
    n2_ref,
    n2_other_ref,
    g_ref,
    g_other_ref,
    att_ref,
    att_other_ref,
    g_res_ref,
    g_res_other_ref,
    out_ref,
    proj_ref,
):
    step = pl.program_id(0)

    @pl.when(step == 0)
    def _():
        att = both(att_ref, att_other_ref, 2).reshape(D // 2, 2 * ROWS)
        d_w = dot(att, both(g_res_ref, g_res_other_ref, 0)).astype(BF16)
        for chip in range(8):
            piece = None
            for half in range(2):
                unpack = pack_of(half, LAST, (CTX_N * LAST, BLK), 1, 0)
                part = dot(
                    unpack,
                    d_w[
                        chip * BLK : (chip + 1) * BLK, half * COLS : (half + 1) * COLS
                    ],
                )
                piece = part if piece is None else piece + part
            proj_ref[:, chip] = piece.astype(BF16).reshape(CTX_N, LAST, COLS)

    left = both(n2_ref, n2_other_ref, 2).reshape(D // 2, 2 * ROWS)
    d_w = dot(left, both(g_ref, g_other_ref, 0)).astype(BF16)
    for chip in range(8):
        for part in range(2):
            out_ref[chip % 4, part, chip // 4, :BLK] = d_w[
                chip * BLK : (chip + 1) * BLK, part * COLS : (part + 1) * COLS
            ]
            out_ref[chip % 4, part, chip // 4, BLK:] = proj_ref[2 * step + part, chip]


def fc_grad_call(turned, turned_other, rows, rows_other):
    n2_block = pl.BlockSpec((8, BLK, ROWS), lambda j: (4, 0, 0))
    g_block = pl.BlockSpec((ROWS, D), lambda j: (0, j))
    att_block = pl.BlockSpec((8, BLK, ROWS), lambda j: (5, 0, 0))
    g_res_block = pl.BlockSpec((ROWS, D), lambda j: (0, 5))
    last = BLK + LAST
    return pl.pallas_call(
        fc_grad_kernel,
        grid=(4,),
        in_specs=[
            n2_block,
            n2_block,
            g_block,
            g_block,
            att_block,
            att_block,
            g_res_block,
            g_res_block,
        ],
        out_specs=pl.BlockSpec((4, 2, 2, last, COLS), lambda j: (0, j, 0, 0, 0)),
        out_shape=jax.ShapeDtypeStruct((4, 8, 2, last, COLS), BF16),
        scratch_shapes=[pltpu.VMEM((CTX_N, 8, LAST, COLS), BF16)],
        compiler_params=params(60),
        cost_estimate=cost(10 * ROWS * D * D, 16 * MB),
        name="fc_grad",
    )(
        turned, turned_other, rows, rows_other, turned, turned_other, rows, rows_other
    )


def owners_kernel(place_ref, in_ref, out_ref, first_ref):
    rows = 8 * BLK
    row = lax.broadcasted_iota(jnp.int32, (rows, rows), 0)
    source = lax.broadcasted_iota(jnp.int32, (rows, rows), 1)
    wanted = (row // 10) % 8 * BLK + row // BLK * 10 + row % 10
    turn_rows = (source == wanted).astype(F32).astype(BF16)
    result = dot(turn_rows, in_ref[:, 0, :BLK].reshape(rows, COLS)).astype(BF16)
    for z in range(4):
        for yh in range(2):
            ctx = z * 2 + yh
            out_ref[yh, 0, z, :BLK] = result[ctx * BLK : (ctx + 1) * BLK]
            out_ref[yh, 0, z, BLK:] = in_ref[ctx, 0, BLK:]

    @pl.when(pl.program_id(0) == place_ref[0] % 2)
    def _():
        first_ref[...] = out_ref[place_ref[0] // 2, 0]


def owners_call(place, array):
    last = BLK + LAST
    return pl.pallas_call(
        owners_kernel,
        grid=(2,),
        in_specs=[
            pl.BlockSpec(memory_space=pltpu.SMEM),
            pl.BlockSpec((8, 1, last, COLS), lambda i: (0, i, 0, 0)),
        ],
        out_specs=[
            pl.BlockSpec((2, 1, 4, last, COLS), lambda i: (0, i, 0, 0, 0)),
            whole((4, last, COLS)),
        ],
        out_shape=[
            jax.ShapeDtypeStruct((2, 2, 4, last, COLS), BF16),
            jax.ShapeDtypeStruct((4, last, COLS), BF16),
        ],
        compiler_params=params(60),
        cost_estimate=cost(4 * 640**3, 5 * MB),
        name="owners",
    )(place, array)


def out_grad_kernel(
    info_ref, act_ref, act_other_ref, g_ref, g_other_ref, out_ref, first_ref
):
    act = both(act_ref, act_other_ref, 2).reshape(8 * BLK, 2 * ROWS)
    d_w = dot(act, both(g_ref, g_other_ref, 0)).astype(BF16)
    for yl in range(2):
        for z in range(4):
            for yh in range(2):
                row = yl * 4 * BLK + (z * 2 + yh) * 40
                out_ref[yh, yl, z, 0, :40] = d_w[row : row + 40, :COLS]
                out_ref[yh, yl, z, 0, 40:] = d_w[row : row + 40, COLS:]
    first = info_ref[SEQ_GRP + 2]
    first_ref[...] = out_ref[first // 2, first % 2]


def out_grad_call(info, turned, turned_other, rows, rows_other):
    act_block = pl.BlockSpec((8, BLK, ROWS), lambda j: (j, 0, 0))
    g_block = pl.BlockSpec((ROWS, D), lambda j: (0, 4))
    return pl.pallas_call(
        out_grad_kernel,
        grid=(4,),
        in_specs=[
            pl.BlockSpec(memory_space=pltpu.SMEM),
            act_block,
            act_block,
            g_block,
            g_block,
        ],
        out_specs=[
            pl.BlockSpec((2, 2, 4, 1, BLK, COLS), lambda j: (0, 0, 0, j, 0, 0)),
            pl.BlockSpec((4, 1, BLK, COLS), lambda j: (0, j, 0, 0)),
        ],
        out_shape=[
            jax.ShapeDtypeStruct((2, 2, 4, 4, BLK, COLS), BF16),
            jax.ShapeDtypeStruct((4, 4, BLK, COLS), BF16),
        ],
        compiler_params=params(60),
        cost_estimate=cost(8 * ROWS * D * D, 16 * MB),
        name="out_grad",
    )(info, turned, turned_other, rows, rows_other)


def add_kernel(mode, at, place_ref, arrived_ref, terms_ref, *refs):
    total = (arrived_ref[...].astype(F32) + terms_ref[0].astype(F32)).astype(BF16)
    if mode == "plain":
        refs[0][...] = total
    elif mode == "spread":
        *blocks, held = refs
        held[...] = total
        for by in range(4):
            blocks[by][...] = held[(place_ref[at + 1] + by) % 4]
    else:
        out_ref, first_ref = refs
        out_ref[...] = total

        @pl.when(pl.program_id(0) == place_ref[at + 1] // 2)
        def _():
            first_ref[...] = out_ref[pl.ds(place_ref[at + 1] % 2 * 4, 4)]


def add_call(place, at, arrived, terms, mode):
    tall, rows, cols = arrived.shape
    part = min(tall, 8)

    def spec(count):
        return pl.BlockSpec((part, count, cols), lambda i, place: (i, 0, 0))

    like = jax.ShapeDtypeStruct
    in_specs = [
        spec(rows),
        pl.BlockSpec((1, part, rows, cols), lambda i, place: (place[at], i, 0, 0)),
    ]
    scratch = []
    if mode == "spread":
        out_specs = [pl.BlockSpec((rows, cols), lambda i, place: (0, 0))] * 4
        out_shape = [like((rows, cols), BF16)] * 4
        scratch = [pltpu.VMEM((part, rows, cols), BF16)]
    elif mode == "first":
        out_specs = [spec(rows), pl.BlockSpec((4, rows, cols), lambda i, place: (0, 0, 0))]
        out_shape = [like((tall, rows, cols), BF16), like((4, rows, cols), BF16)]
    else:
        out_specs = [spec(rows)]
        out_shape = [like((tall, rows, cols), BF16)]
    nbytes = 6 * tall * rows * cols
    return pl.pallas_call(
        functools.partial(add_kernel, mode, at),
        grid_spec=pltpu.PrefetchScalarGridSpec(
            num_scalar_prefetch=1,
            grid=(tall // part,),
            in_specs=in_specs,
            out_specs=out_specs,
            scratch_shapes=scratch,
        ),
        out_shape=out_shape,
        compiler_params=params(60),
        cost_estimate=cost(nbytes // 4, nbytes),
        name="add_blocks",
    )(place, arrived, terms)


def ring_perm(axis):
    pairs = []
    for core in range(2):
        for pos in range(4):
            to = (pos + (1 if core == 0 else -1)) % 4
            if axis == "x":
                index = lambda p: p * 2 + core
            elif axis == "z":
                index = lambda p: core * 4 + p
            else:
                index = lambda p: ((p % 2) * 2 + core) * 2 + p // 2
            pairs.append((index(pos), index(to)))
    return {"x": ("x", "c"), "z": ("c", "z"), "y": ("yl", "c", "yh")}[axis], pairs


def swap_cores(array):
    return lax.ppermute(array, "c", [(0, 1), (1, 0)])


def shift_perm(axis, by):
    if axis != "y":
        return axis, [(p, (p + by) % 4) for p in range(4)]
    index = lambda p: (p % 2) * 2 + p // 2
    return ("yl", "yh"), [(index(p), index((p + by) % 4)) for p in range(4)]


RINGS = [
    (order, phase, step)
    for order in ("yzx", "yz")
    for phase in range(len(order) - 1)
    for step in range(3)
]


def index_of(order, phase, step):
    return RINGS.index((order, phase, step))


def ring_places():
    way = 1 - 2 * lax.axis_index("c")
    place = {
        "x": lax.axis_index("x"),
        "y": 2 * lax.axis_index("yh") + lax.axis_index("yl"),
        "z": lax.axis_index("z"),
    }
    numbers = []
    for order, phase, step in RINGS:
        last = phase == len(order) - 2
        numbers.append((place[order[phase]] - way * (2 + step)) % 4)
        numbers.append((place[order[phase + 1]] - (0 if last else way)) % 4)
    return jnp.stack(numbers).astype(jnp.int32)


class Sum:
    def __init__(self, terms, first, order, place):
        self.terms = terms
        self.sent = first
        self.order = order
        self.place = place
        self.phase = 0
        self.step = 0

    def start(self):
        axis = self.order[self.phase]
        if self.phase < len(self.order) - 1:
            self.flight = lax.ppermute(self.sent, *ring_perm(axis))
        else:
            self.flight = [
                lax.ppermute(self.sent[by], *shift_perm(axis, by)) for by in (1, 2, 3)
            ]

    def land(self):
        if self.phase == len(self.order) - 1:
            return self.sent[0].astype(F32) + sum(f.astype(F32) for f in self.flight)
        mode = "plain"
        if self.step == 2:
            mode = "first" if self.phase == 0 and len(self.order) == 3 else "spread"
        at = 2 * index_of(self.order, self.phase, self.step)
        outs = add_call(self.place, at, self.flight, self.terms, mode)
        self.step += 1
        if mode == "plain":
            self.sent = outs[0]
            return None
        self.step, self.phase = 0, self.phase + 1
        if mode == "first":
            self.terms = outs[0].reshape(4, 4, *outs[0].shape[1:])
            self.sent = outs[1]
        else:
            self.sent = outs
        return None

    def advance(self, other):
        self.flight, other = tie(self.flight, other)
        self.land()
        self.sent, other = tie(self.sent, other)
        self.start()
        return other


def tie(first, second):
    return lax.optimization_barrier((first, second))


def per_device(
    tokens,
    lengths,
    cotangent,
    ln1_gain,
    ln1_bias,
    w_qkv,
    q_bias,
    v_bias,
    w_proj,
    proj_bias,
    ln2_gain,
    ln2_bias,
    w_fc,
    fc_bias,
    w_out,
    out_bias,
):
    ctx_rank = lax.axis_index(CTX)
    core = lax.axis_index("c")
    seq_rank = lax.axis_index("yh")
    head_group = lax.axis_index("z")
    tok = tokens.reshape(ROWS, D)
    cot = cotangent.reshape(ROWS, D)

    def exchange(array):
        return lax.all_to_all(array, CTX, 0, 0, tiled=True)

    w_cols = exchange(w_fc.reshape(10, CTX_N, COLS).transpose(1, 0, 2))

    vec_two = jnp.concatenate([proj_bias, ln2_gain, ln2_bias, out_bias, fc_bias])
    vec_two = jnp.pad(vec_two[None], ((0, PIECE - 21), (0, COLS - 80)))
    part = jnp.concatenate(
        [
            w_cols.reshape(BLK, COLS),
            w_out.reshape(40, 2, COLS).transpose(1, 0, 2).reshape(BLK, COLS),
            w_proj.reshape(10, 2, COLS).transpose(1, 0, 2).reshape(20, COLS),
            vec_two,
        ],
        axis=0,
    )
    part, w_qkv, tokens = lax.optimization_barrier((part, w_qkv, tokens))
    weights = lax.all_gather(part, PLACE, axis=0, tiled=False)

    theirs = lax.dynamic_index_in_dim(tokens, 1 - seq_rank, 0, False)
    mine = lax.dynamic_index_in_dim(tokens, seq_rank, 0, False)
    theirs = lax.ppermute(theirs, "yh", [(0, 1), (1, 0)])
    sequence = jnp.where(
        seq_rank == 0, jnp.stack([mine, theirs]), jnp.stack([theirs, mine])
    )
    sequence = jnp.broadcast_to(sequence[None], (4, 2, SPAN, D))
    groups = w_qkv.reshape(10, 3, 4, GROUP_W).transpose(2, 0, 1, 3)
    groups = groups.reshape(4, 10, HEADS_W)
    vec_one = jnp.concatenate([ln1_gain, ln1_bias, q_bias, v_bias])
    vec_one = jnp.pad(vec_one[None, None], ((0, 0), (0, 0), (0, HEADS_W - 40)))
    groups = jnp.concatenate([groups, jnp.broadcast_to(vec_one, (4, 1, HEADS_W))], axis=1)
    groups = jnp.broadcast_to(groups[:, None], (4, 2, 11, HEADS_W))
    shards = exchange(groups.reshape(CTX_N, 11, HEADS_W))
    w_group = jnp.concatenate(
        [shards[:, :10].reshape(BLK, HEADS_W), shards[:, 10]], axis=0
    )
    w_group = jnp.broadcast_to(w_group[None], (8, BLK + 8, HEADS_W))
    w_group = lax.all_to_all(w_group, ("x", "yl"), 0, 0, tiled=True)
    w_group, sequence = tie(w_group, sequence)
    other = swap_cores(w_group)
    first = jnp.where(core == 0, w_group, other)
    second = jnp.where(core == 0, other, w_group)
    w_group = jnp.stack([first, second], axis=1).reshape(16, BLK + 8, HEADS_W)
    sequence = lax.all_to_all(sequence, "z", 0, 0, tiled=True).reshape(LEN, D)

    vecs = w_group[:, BLK:, :40].reshape(128, 4, 10).transpose(1, 0, 2)
    vecs = vecs.reshape(4, D).astype(F32)
    own = lax.dynamic_slice_in_dim(vecs[2:], head_group * GROUP_W, GROUP_W, 1)
    bias = jnp.concatenate([own[0:1], jnp.zeros((1, GROUP_W), F32), own[1:2]], axis=1)
    length = lax.dynamic_slice_in_dim(lengths, seq_rank, 1)
    qkv, att, lse = attend_call(length, sequence, vecs[:2], bias, w_group)
    att = exchange(att).reshape(4, SEQ_GRP, GROUP_W, SPAN)

    more = weights[:, 2 * BLK + 20, :80].reshape(4, 2, 2, 4, 2, 80)
    more = more.transpose(3, 2, 4, 0, 1, 5).reshape(128, 80).astype(F32)
    fc_shift = more[:, 40:].reshape(1, 4 * D)
    more = more[:, :40].reshape(128, 4, 10).transpose(1, 0, 2).reshape(4, D)
    way = 1 - 2 * core
    chip_y = 2 * lax.axis_index("yh") + lax.axis_index("yl")
    first_sent = [(p - way) % 4 for p in (chip_y, lax.axis_index("z"))]
    first_y = first_sent[0].astype(jnp.int32)[None]
    info = jnp.stack([ctx_rank * SPAN, core, *first_sent, head_group]).astype(jnp.int32)
    info = jnp.concatenate([lengths, info])
    layer_out, g_res, g_att, d_vecs, d_fc_bias, rows, turned, turned_give = mlp_call(
        info, tok, cot, att, more, fc_shift, weights
    )

    turned_other = swap_cores(turned_give)
    rows_other = swap_cores(rows)
    g_att = exchange(g_att.reshape(CTX_N, GROUP_W, SPAN))
    g_att, rows_other = tie(g_att, rows_other)
    d_fc = fc_grad_call(turned, turned_other, rows, rows_other)
    d_fc, rows_other = tie(d_fc, rows_other)
    d_fc = lax.psum_scatter(d_fc, "x", scatter_dimension=0, tiled=False)
    d_out, first = out_grad_call(info, turned, turned_other, rows, rows_other)
    places = ring_places()
    out_sum = Sum(
        d_out.reshape(4, 16, BLK, COLS), first.reshape(16, BLK, COLS), "yzx", places
    )
    out_sum.sent, g_att = tie(out_sum.sent, g_att)
    out_sum.start()
    g_qkv = attend_back_call(length, qkv, g_att, lse)
    g_qkv = out_sum.advance(g_qkv)
    g_norm, d_norm = norm_grad_call(sequence, w_group, g_qkv)
    d_norm, g_qkv = tie(d_norm, g_qkv)
    g_norm = lax.all_to_all(
        g_norm.reshape(4, 2, SPAN, D), "z", 0, 0, tiled=True
    )
    group_keep, group_give = qkv_grad_call(
        info, sequence, vecs[:2], g_qkv, d_norm, d_vecs, d_fc_bias
    )
    group_keep, group_give = out_sum.advance((group_keep, group_give))
    group_given = swap_cores(group_give)
    d_group = (group_keep.astype(F32) + group_given.astype(F32)).astype(BF16)
    g_norm = jnp.sum(g_norm.astype(F32), axis=0).astype(BF16)
    g_own = lax.dynamic_index_in_dim(g_norm, seq_rank, 0, False)
    g_give = lax.dynamic_index_in_dim(g_norm, 1 - seq_rank, 0, False)
    g_other = lax.ppermute(g_give, "yh", [(0, 1), (1, 0)])
    d_group = out_sum.advance(d_group)
    d_group = lax.all_to_all(d_group, ("x", "yl"), 0, 0, tiled=True)
    input_grad = norm_back_call(
        seq_rank.astype(jnp.int32)[None], tok, vecs[:1], g_res, g_own, g_other
    )
    d_fc = out_sum.advance(d_fc)
    d_fc, first_fc = owners_call(first_y, d_fc)
    last = BLK + LAST
    fc_sum = Sum(
        d_fc.reshape(4, 4, last, COLS), first_fc, "yz", places
    )
    fc_sum.start()
    out_sum.advance(())
    fc_sum.advance(())
    out_sum.advance(())
    fc_sum.advance(())
    last_sum = out_sum.land()
    fc_sum.advance(())
    d_fc = fc_sum.land()
    d_group = jnp.sum(d_group.astype(F32), axis=0).astype(BF16)
    d_group = jnp.concatenate(
        [d_group[:BLK].reshape(CTX_N, 10, HEADS_W), d_group[BLK : BLK + 8, None]], axis=1
    )
    d_group = exchange(d_group)
    d_group = d_group.astype(F32)
    d_qkv = jnp.sum(d_group[:, :10].reshape(4, 2, 10, HEADS_W), axis=1)
    d_qkv = d_qkv.reshape(4, 10, 3, GROUP_W)
    d_qkv = d_qkv.transpose(1, 2, 0, 3).reshape(10, 3 * D)
    small = jnp.sum(d_group[:, 10, :120], axis=0)

    d_proj = d_fc[BLK : BLK + 20].reshape(2, 10, COLS).transpose(1, 0, 2).reshape(10, D)
    d_fc = d_fc[:BLK].reshape(CTX_N, 10, COLS).transpose(1, 0, 2)
    d_fc = d_fc.reshape(10, CTX_N * COLS)
    d_out = jnp.concatenate([last_sum[:40], last_sum[40:BLK]], axis=1)
    names = ["g1", "b1", "q", "v", "proj", "g2", "b2", "out"]
    vec = {n: small[10 * k : 10 * (k + 1)] for k, n in enumerate(names)}

    return (
        layer_out.reshape(tokens.shape),
        input_grad.reshape(tokens.shape),
        vec["g1"],
        vec["b1"],
        d_qkv,
        vec["q"],
        vec["v"],
        d_proj,
        vec["proj"],
        vec["g2"],
        vec["b2"],
        d_fc,
        small[80:120],
        d_out,
        vec["out"],
    )


def solution(mesh):
    fine = Mesh(mesh.devices.reshape(SIZES), AXES)
    rows = P(DP, CTX, None)
    mat = P(AXES, None)
    vec = P(AXES)
    in_specs = (
        rows,
        P(DP),
        rows,
        vec,
        vec,
        mat,
        vec,
        vec,
        mat,
        vec,
        vec,
        vec,
        mat,
        vec,
        mat,
        vec,
    )
    out_specs = (
        rows,
        rows,
        vec,
        vec,
        mat,
        vec,
        vec,
        mat,
        vec,
        vec,
        vec,
        mat,
        vec,
        mat,
        vec,
    )
    return jax.shard_map(
        per_device, mesh=fine, in_specs=in_specs, out_specs=out_specs, check_vma=False
    )
```

time: 453 us -> 428 us (0.945)
  the two profiles are of different devices: /device:TPU:0 before, /device:TPU:2 now
where the time goes in v4:
time: 428 us; the launch traced here: 420 us
  Pallas kernels  141 us (33%)
  waiting for transfers between devices  128 us (30%)
  starting transfers between devices  55 us (13%)
  blocking collectives  34.6 us (8%)
  local copies, waits for them, and re-layouts  33 us (8%)
  between operations  14.9 us (3%)
  other arithmetic  13.4 us (3%)
    all_to_all x1, waiting for transfers between devices, per_device(): sequence = lax.all_to_all(sequence, 'z', 0, 0, tiled=True).reshape(LEN, D)  42 us
    ppermute x9, waiting for transfers between devices, start(): self.flight = lax.ppermute(self.sent, *ring_perm(axis))  35.9 us
    all_to_all x2, blocking collectives, exchange(): return lax.all_to_all(array, CTX, 0, 0, tiled=True)  34.6 us
    pallas_call x1, Pallas kernels, mlp_call(): pl.pallas_call(mlp_kernel, grid=(4,), in_specs=[pl.BlockSpec(memory_space...  31 us
    pallas_call x9, Pallas kernels, add_call(): pl.pallas_call(functools.partial(add_kernel, mode, at), grid_spec=pltpu.P...  27.8 us
    ppermute x1, waiting for transfers between devices, per_device(): theirs = lax.ppermute(theirs, 'yh', [(0, 1), (1, 0)])  21.5 us
    pallas_call x1, Pallas kernels, attend_call(): pl.pallas_call(attend_kernel, grid=(GROUP_HEADS,), in_specs=[pl.BlockSpec...  18.5 us
    pallas_call x1, Pallas kernels, attend_back_call(): pl.pallas_call(attend_back_kernel, grid=(GROUP_HEADS,), in_specs=[pl.Bloc...  16.1 us
  transfers between devices with their start and end apart: 30, of which 14 were waited for; matrix products, arithmetic and copies ran while one was open for 7% of the time, Pallas kernels for 23%

profile of v4, /device:TPU:2, one launch (start us, length us, event | category | flops | bytes accessed | tf_op | source)
XLA Modules:
  0.0 419.8 jit_solution(11344893405810765491)
XLA Ops:
  8.9 7.9 %all-to-all-start = ((bf16[8,10,640]{2,1,0:T(8,128)(2,1)}), bf16[8,10,640]{2,1,0:T(8,128)(2,1)S(1)}, u32[]{:S(2)}, u32[]{:S(2)}) async-start(bf16[8,10,640]{2,1,0:T(8,128)(2,1)} %bitcast.91), calls=%async_computation | async-start | bytes 327680 | tf_op jit(solution)/shard_map/all_to_all | solution.py:898
  18.7 3.4 concatenate.36
  26.6 12.7 %all_to_all.45 = bf16[8,11,960]{2,1,0:T(8,128)(2,1)S(1)} all-to-all(bf16[8,11,960]{2,1,0:T(8,128)(2,1)S(1)} %bitcast.127), channel_id=1, replica_groups=mesh['x'=4,'yl'=2,'c'=2,'z'=4,'yh'=2] {'z','yh'}, dimensions={0} | all-to-all | bytes 337920 | tf_op jit(solution)/shard_map/all_to_all | solution.py:898
  40.8 5.1 %all-to-all-start.2 = ((bf16[8,88,960]{2,1,0:T(8,128)(2,1)}), bf16[8,88,960]{2,1,0:T(8,128)(2,1)}, u32[]{:S(2)}, u32[]{:S(2)}) async-start(bf16[8,88,960]{2,1,0:T(8,128)(2,1)} %broadcast_in_dim.46), calls=%async_computation.2 | async-start | bytes 2883584 | tf_op jit(solution)/shard_map/all_to_all | solution.py:934
  47.4 21.5 %collective-permute-done = bf16[128,1280]{1,0:T(8,128)(2,1)S(1)} collective-permute-done((bf16[128,1280]{1,0:T(8,128)(2,1)S(1)}, bf16[128,1280]{1,0:T(8,128)(2,1)S(1)}, u32[]{:S(2)}, u32[]{:S(2)}) %collective-permute-start) | collective-permute-done | bytes 327712 | tf_op jit(solution)/shard_map/ppermute | solution.py:918
  70.7 3.7 all-to-all-start.3
  81.0 42.0 %all-to-all-done.3 = bf16[4,2,128,1280]{3,2,1,0:T(8,128)(2,1)S(1)} async-done(((bf16[4,2,128,1280]{3,2,1,0:T(8,128)(2,1)}), bf16[4,2,128,1280]{3,2,1,0:T(8,128)(2,1)S(1)}, u32[]{:S(2)}, u32[]{:S(2)}) %all-to-all-start.3) | async-done | bytes 2621472 | tf_op jit(solution)/shard_map/all_to_all | solution.py:940
  124.4 18.5 %attend.1 = (bf16[3,5,64,1024]{3,2,1,0:T(8,128)(2,1)}, bf16[8,320,128]{2,1,0:T(8,128)(2,1)}, f32[5,1,1024]{2,1,0:T(1,128)}) custom-call(s32[1]{0:T(128)} %dynamic_slice.19.len_ref, bf16[1024,1280]{1,0:T(8,128)(2,1)} %bitcast.104, f32[2,1280]{1,0:T(2,128)} %slice.98.norm_ref, f32[1,960]{1,0:T(1,128)} %pad_maximum_fusion.5.bias_ref, bf16[16,88,960]{2,1,0:T(8,128)(2,1)} %bitcast.108), custom_call_target="tpu_custom_call" | custom-call | flops 4127195 | bytes 8388 | tf_op jit(solution)/shard_map/attend/pallas_call | solution.py:145
  143.0 4.3 %all-to-all-start.4 = ((bf16[8,320,128]{2,1,0:T(8,128)(2,1)}), bf16[8,320,128]{2,1,0:T(8,128)(2,1)S(1)}, u32[]{:S(2)}, u32[]{:S(2)}) async-start(bf16[8,320,128]{2,1,0:T(8,128)(2,1)} %get-tuple-element.79), calls=%async_computation.4 | async-start | bytes 1310720 | tf_op jit(solution)/shard_map/all_to_all | solution.py:898
  148.2 11.4 %all-gather.3.cloned.1.call-done = bf16[24576,640]{1,0:T(8,128)(2,1)} async-done(((bf16[192,640]{1,0:T(8,128)(2,1)}), bf16[24576,640]{1,0:T(8,128)(2,1)}) %all-gather.3.cloned.1.call-update) | async-done | bytes 31457296 | tf_op jit(solution)/shard_map/all_gather | solution.py:914
  163.3 31.0 %mlp.1 = (bf16[256,1280]{1,0:T(8,128)(2,1)}, bf16[256,1280]{1,0:T(8,128)(2,1)}, bf16[4,2,320,128]{3,2,1,0:T(8,128)(2,1)}, f32[4,1280]{1,0:T(4,128)}, f32[1,5120]...) custom-call(s32[7]{0:T(128)} %concatenate.35.info_ref, ...), custom_call_target="tpu_custom_call" | custom-call | flops 15099494 | bytes 39845 | tf_op jit(solution)/shard_map/mlp/pallas_call | solution.py:502
  194.9 21.9 %all_to_all.46.grad_ref = bf16[8,320,128]{2,1,0:T(8,128)(2,1)} all-to-all(bf16[8,320,128]{2,1,0:T(8,128)(2,1)} %bitcast.130), channel_id=1, replica_groups=mesh['x'=4,'yl'=2,'c'=2,'z'=4,'yh'=2] {'z','yh'}, dimensions={0} | all-to-all | bytes 1310720 | tf_op jit(solution)/shard_map/all_to_all | solution.py:898
  218.8 11.3 %fc_grad.1 = bf16[4,8,2,104,640]{4,3,2,1,0:T(8,128)(2,1)} custom-call(bf16[48,80,256]{2,1,0:T(8,128)(2,1)} %get-tuple-element.83.n2_ref.att_ref.act_ref, bf16[48,80,256]{2,1,0:T(8,128)(2,1)} %collective-permute-done.2.n2_other_ref.att_other_ref.act_other_ref, bf16[256,7680]{1,0:T(8,128)(2,1)} %get-tuple-element.85.g_ref.g_res_ref, ...), custom_call_target="tpu_custom_call" | custom-call | flops 4194304 | bytes 16777 | tf_op jit(solution)/shard_map/fc_grad/pallas_call | solution.py:604
  230.1 7.9 %out_grad.1 = (bf16[2,2,4,4,80,640]{5,4,3,2,1,0:T(8,128)(2,1)}, bf16[4,4,80,640]{3,2,1,0:T(8,128)(2,1)}) custom-call(s32[7]{0:T(128)} %concatenate.35.info_ref, bf16[48,80,256]{2,1,0:T(8,128)(2,1)} %get-tuple-element.83.n2_ref.att_ref.act_ref, bf16[48,80,256]{2,1,0:T(8,128)(2,1)} %collective-permute-done.2.n2_other_ref.att_other_ref.act_other_ref, ...), custom_call_target="tpu_custom_call" | custom-call | flops 3355443 | bytes 16777 | tf_op jit(solution)/shard_map/out_grad/pallas_call | solution.py:687
  239.2 16.1 %attend_back.1.g_ref = bf16[3,5,64,1024]{3,2,1,0:T(8,128)(2,1)} custom-call(s32[1]{0:T(128)} %dynamic_slice.19.len_ref, bf16[3,5,64,1024]{3,2,1,0:T(8,128)(2,1)} %get-tuple-element.92.qkv_ref, bf16[8,320,128]{2,1,0:T(8,128)(2,1)} %all_to_all.46.grad_ref, f32[5,1,1024]{2,1,0:T(1,128)} %get-tuple-element.94.lse_ref), custom_call_target="tpu_custom_call" | custom-call | flops 4026531 | bytes 5242 | tf_op jit(solution)/shard_map/attend_back/pallas_call | solution.py:207
  255.3 5.2 %collective-permute-done.4.arrived_ref = bf16[16,80,640]{2,1,0:T(8,128)(2,1)S(1)} collective-permute-done((bf16[16,80,640]{2,1,0:T(8,128)(2,1)}, bf16[16,80,640]{2,1,0:T(8,128)(2,1)S(1)}, u32[]{:S(2)}, u32[]{:S(2)}) %collective-permute-start.4) | collective-permute-done | bytes 1638432 | tf_op jit(solution)/shard_map/ppermute | solution.py:834
  261.7 3.7 add_blocks.9
  265.4 8.7 %norm_grad.1 = (bf16[8,128,1280]{2,1,0:T(8,128)(2,1)}, f32[2,1280]{1,0:T(2,128)}) custom-call(bf16[1024,1280]{1,0:T(8,128)(2,1)} %bitcast.105, bf16[16,88,960]{2,1,0:T(8,128)(2,1)} %bitcast.109, bf16[3,5,64,1024]{3,2,1,0:T(8,128)(2,1)} %attend_back.1.g_ref), custom_call_target="tpu_custom_call" | custom-call | flops 2516582 | bytes 10485 | tf_op jit(solution)/shard_map/norm_grad/pallas_call | solution.py:243
  274.1 3.8 all-to-all-start.6
  277.9 11.5 %qkv_grad.1 = (bf16[8,96,960]{2,1,0:T(8,128)(2,1)}, bf16[8,96,960]{2,1,0:T(8,128)(2,1)}) custom-call(s32[7]{0:T(128)} %concatenate.35.info_ref, bf16[1024,1280]{1,0:T(8,128)(2,1)} %bitcast.106, f32[2,1280]{1,0:T(2,128)} %slice.98.norm_ref, bf16[3,5,64,1024]{3,2,1,0:T(8,128)(2,1)} %attend_back.1.g_ref, f32[2,1280]{1,0:T(2,128)} %get-tuple-element.103.d_norm_ref, ...), custom_call_target="tpu_custom_call" | custom-call | flops 2516582 | bytes 8388 | tf_op jit(solution)/shard_map/qkv_grad/pallas_call | solution.py:321
  289.5 3.8 add_blocks.10
  293.2 3.6 collective-permute-done.8
  296.8 3.3 add_convert_fusion
  300.1 15.7 %collective-permute-done.7.arrived_ref = bf16[16,80,640]{2,1,0:T(8,128)(2,1)} collective-permute-done((bf16[16,80,640]{2,1,0:T(8,128)(2,1)}, bf16[16,80,640]{2,1,0:T(8,128)(2,1)}, u32[]{:S(2)}, u32[]{:S(2)}) %collective-permute-start.7) | collective-permute-done | bytes 1638432 | tf_op jit(solution)/shard_map/ppermute | solution.py:834
  315.9 3.8 add_blocks.11
  319.7 5.0 %all-to-all-start.7 = ((bf16[8,96,960]{2,1,0:T(8,128)(2,1)}), bf16[8,96,960]{2,1,0:T(8,128)(2,1)}, u32[]{:S(2)}, u32[]{:S(2)}) async-start(bf16[8,96,960]{2,1,0:T(8,128)(2,1)} %add_convert_fusion), calls=%async_computation.7 | async-start | bytes 3145728 | tf_op jit(solution)/shard_map/all_to_all | solution.py:996
  326.6 7.3 %collective-permute-done.9.arrived_ref = bf16[4,80,640]{2,1,0:T(8,128)(2,1)S(1)} collective-permute-done((bf16[4,80,640]{2,1,0:T(8,128)(2,1)S(1)}, bf16[4,80,640]{2,1,0:T(8,128)(2,1)S(1)}, u32[]{:S(2)}, u32[]{:S(2)}) %collective-permute-start.9) | collective-permute-done | bytes 409632 | tf_op jit(solution)/shard_map/ppermute | solution.py:834
  337.3 4.6 %owners.1 = (bf16[2,2,4,104,640]{4,3,2,1,0:T(8,128)(2,1)}, bf16[4,104,640]{2,1,0:T(8,128)(2,1)}) custom-call(s32[1]{0:T(128)} %bitcast.2.place_ref, bf16[8,2,104,640]{3,2,1,0:T(8,128)(2,1)} %bitcast.120), custom_call_target="tpu_custom_call" | custom-call | flops 1048576 | bytes 5242 | tf_op jit(solution)/shard_map/owners/pallas_call | solution.py:648
  345.1 7.6 %collective-permute-done.10.arrived_ref = bf16[4,104,640]{2,1,0:T(8,128)(2,1)} collective-permute-done((bf16[4,104,640]{2,1,0:T(8,128)(2,1)}, bf16[4,104,640]{2,1,0:T(8,128)(2,1)}, u32[]{:S(2)}, u32[]{:S(2)}) %collective-permute-start.10) | collective-permute-done | bytes 532512 | tf_op jit(solution)/shard_map/ppermute | solution.py:834
  362.1 3.5 all-to-all-start.8
  375.4 3.4 norm_back.1
  404.9 4.5 %collective-permute-done.13 = bf16[104,640]{1,0:T(8,128)(2,1)S(1)} collective-permute-done((bf16[104,640]{1,0:T(8,128)(2,1)}, bf16[104,640]{1,0:T(8,128)(2,1)S(1)}, u32[]{:S(2)}, u32[]{:S(2)}) %collective-permute-start.13) | collective-permute-done | bytes 133152 | tf_op jit(solution)/shard_map/ppermute | solution.py:837
  (177 shorter events, 87.0 us)
Async XLA Ops:
  7.2 19.0 %copy-start.13 = (bf16[10,3840]{1,0:T(8,128)(2,1)S(1)}, bf16[10,3840]{1,0:T(8,128)(2,1)}, u32[]{:S(2)}) copy-start(bf16[10,3840]{1,0:T(8,128)(2,1)} %param.21) | copy-start | bytes 230404
  8.9 16.3 %all-to-all-start = ((bf16[8,10,640]{2,1,0:T(8,128)(2,1)}), bf16[8,10,640]{2,1,0:T(8,128)(2,1)S(1)}, u32[]{:S(2)}, u32[]{:S(2)}) async-start(bf16[8,10,640]{2,1,0:T(8,128)(2,1)} %bitcast.91), calls=%async_computation | async-start | bytes 327680 | tf_op jit(solution)/shard_map/all_to_all | solution.py:898
  16.9 142.7 %all-gather.3.cloned.1.call-start = ((), (), s32[]{:S(2)}) async-start(), calls=%async_computation.11 | async-start | bytes 31703040 | tf_op jit(solution)/shard_map/all_gather | solution.py:914
  40.8 28.2 %all-to-all-start.2 = ((bf16[8,88,960]{2,1,0:T(8,128)(2,1)}), bf16[8,88,960]{2,1,0:T(8,128)(2,1)}, u32[]{:S(2)}, u32[]{:S(2)}) async-start(bf16[8,88,960]{2,1,0:T(8,128)(2,1)} %broadcast_in_dim.46), calls=%async_computation.2 | async-start | bytes 2883584 | tf_op jit(solution)/shard_map/all_to_all | solution.py:934
  45.9 23.0 %collective-permute-start = (bf16[128,1280]{1,0:T(8,128)(2,1)S(1)}, bf16[128,1280]{1,0:T(8,128)(2,1)S(1)}, u32[]{:S(2)}, u32[]{:S(2)}) collective-permute-start(bf16[128,1280]{1,0:T(8,128)(2,1)S(1)} %get-tuple-element.140), channel_id=1, source_target_pairs={{0,1},{1,0},{2,3},{3,2},{4,5},{5,4},{6,7},{7,6},{8,9},{9,8},{10,11... | collective-permute-start | bytes 983048 | tf_op jit(solution)/shard_map/ppermute | solution.py:918
  70.7 4.4 %collective-permute-start.1 = (bf16[8,88,960]{2,1,0:T(8,128)(2,1)}, bf16[8,88,960]{2,1,0:T(8,128)(2,1)}, u32[]{:S(2)}, u32[]{:S(2)}) collective-permute-start(bf16[8,88,960]{2,1,0:T(8,128)(2,1)} %all-to-all-done.2), channel_id=1, source_target_pairs={{0,8},{8,0},{1,9},{9,1},{2,10},{10,2},{3,11},{11,3},{4,12},{12,4},... | collective-permute-start | bytes 4055048 | tf_op jit(solution)/shard_map/ppermute | solution.py:785
  70.7 52.3 %all-to-all-start.3 = ((bf16[4,2,128,1280]{3,2,1,0:T(8,128)(2,1)}), bf16[4,2,128,1280]{3,2,1,0:T(8,128)(2,1)S(1)}, u32[]{:S(2)}, u32[]{:S(2)}) async-start(bf16[4,2,128,1280]{3,2,1,0:T(8,128)(2,1)} %broadcast_in_dim.47), calls=%async_computation.3 | async-start | bytes 5242880 | tf_op jit(solution)/shard_map/all_to_all | solution.py:940
  79.2 63.7 %copy-start.6 = (f32[128,4,10]{2,1,0:T(4,128)}, f32[128,4,10]{2,1,0:T(4,128)S(1)}, u32[]{:S(2)}) copy-start(f32[128,4,10]{2,1,0:T(4,128)S(1)} %reshape.223) | copy-start | bytes 61444
  143.0 19.5 %all-to-all-start.4 = ((bf16[8,320,128]{2,1,0:T(8,128)(2,1)}), bf16[8,320,128]{2,1,0:T(8,128)(2,1)S(1)}, u32[]{:S(2)}, u32[]{:S(2)}) async-start(bf16[8,320,128]{2,1,0:T(8,128)(2,1)} %get-tuple-element.79), calls=%async_computation.4 | async-start | bytes 1310720 | tf_op jit(solution)/shard_map/all_to_all | solution.py:898
  147.3 186.6 %reduce-scatter.2.cloned.1.call-start = ((), (), s32[]{:S(2)}) async-start(), calls=%async_computation.10 | async-start | bytes 10649600 | tf_op jit(solution)/shard_map/reduce_scatter | solution.py:970
  194.4 22.5 %collective-permute-start.3 = (bf16[256,7680]{1,0:T(8,128)(2,1)}, bf16[256,7680]{1,0:T(8,128)(2,1)S(1)}, u32[]{:S(2)}, u32[]{:S(2)}) collective-permute-start(bf16[256,7680]{1,0:T(8,128)(2,1)} %get-tuple-element.85.g_ref.g_res_ref), channel_id=1, source_target_pairs={{0,8},{8,0},{1,9},{9,1},{2,10},{10,2},{3,11},{11,3},{4,12},{12,4},... | collective-permute-start | bytes 11796488 | tf_op jit(solution)/shard_map/ppermute | solution.py:785
  194.7 22.2 %collective-permute-start.2 = (bf16[48,80,256]{2,1,0:T(8,128)(2,1)}, bf16[48,80,256]{2,1,0:T(8,128)(2,1)}, u32[]{:S(2)}, u32[]{:S(2)}) collective-permute-start(bf16[48,80,256]{2,1,0:T(8,128)(2,1)} %get-tuple-element.84), channel_id=1, source_target_pairs={{0,8},{8,0},{1,9},{9,1},{2,10},{10,2},{3,11},{11,3},{4,12},{12,4},... | collective-permute-start | bytes 5898248 | tf_op jit(solution)/shard_map/ppermute | solution.py:785
  238.0 22.5 %collective-permute-start.4 = (bf16[16,80,640]{2,1,0:T(8,128)(2,1)}, bf16[16,80,640]{2,1,0:T(8,128)(2,1)S(1)}, u32[]{:S(2)}, u32[]{:S(2)}) collective-permute-start(bf16[16,80,640]{2,1,0:T(8,128)(2,1)} %bitcast.148), channel_id=1, source_target_pairs={{0,16},{16,1},{1,17},{17,0},{8,25},{24,8},{9,24},{25,9},{2,18},{18... | collective-permute-start | bytes 4915208 | tf_op jit(solution)/shard_map/ppermute | solution.py:834
  265.4 24.0 %collective-permute-start.6 = (bf16[16,80,640]{2,1,0:T(8,128)(2,1)}, bf16[16,80,640]{2,1,0:T(8,128)(2,1)}, u32[]{:S(2)}, u32[]{:S(2)}) collective-permute-start(bf16[16,80,640]{2,1,0:T(8,128)(2,1)} %add_blocks.9), channel_id=1, source_target_pairs={{0,16},{16,1},{1,17},{17,0},{8,25},{24,8},{9,24},{25,9},{2,18},{18... | collective-permute-start | bytes 4915208 | tf_op jit(solution)/shard_map/ppermute | solution.py:834
  274.1 45.6 %all-to-all-start.6 = ((bf16[4,2,128,1280]{3,2,1,0:T(8,128)(2,1)}), bf16[4,2,128,1280]{3,2,1,0:T(8,128)(2,1)S(1)}, u32[]{:S(2)}, u32[]{:S(2)}) async-start(bf16[4,2,128,1280]{3,2,1,0:T(8,128)(2,1)} %bitcast.119), calls=%async_computation.6 | async-start | bytes 5242880 | tf_op jit(solution)/shard_map/all_to_all | solution.py:982
  293.2 3.6 collective-permute-start.8
  293.2 22.6 %collective-permute-start.7 = (bf16[16,80,640]{2,1,0:T(8,128)(2,1)}, bf16[16,80,640]{2,1,0:T(8,128)(2,1)}, u32[]{:S(2)}, u32[]{:S(2)}) collective-permute-start(bf16[16,80,640]{2,1,0:T(8,128)(2,1)} %add_blocks.10), channel_id=1, source_target_pairs={{0,16},{16,1},{1,17},{17,0},{8,25},{24,8},{9,24},{25,9},{2,18},{18... | collective-permute-start | bytes 4915208 | tf_op jit(solution)/shard_map/ppermute | solution.py:834
  319.7 39.8 %all-to-all-start.7 = ((bf16[8,96,960]{2,1,0:T(8,128)(2,1)}), bf16[8,96,960]{2,1,0:T(8,128)(2,1)}, u32[]{:S(2)}, u32[]{:S(2)}) async-start(bf16[8,96,960]{2,1,0:T(8,128)(2,1)} %add_convert_fusion), calls=%async_computation.7 | async-start | bytes 3145728 | tf_op jit(solution)/shard_map/all_to_all | solution.py:996
  324.7 9.2 %collective-permute-start.9 = (bf16[4,80,640]{2,1,0:T(8,128)(2,1)S(1)}, bf16[4,80,640]{2,1,0:T(8,128)(2,1)S(1)}, u32[]{:S(2)}, u32[]{:S(2)}) collective-permute-start(bf16[4,80,640]{2,1,0:T(8,128)(2,1)S(1)} %copy-done.20), channel_id=1, source_target_pairs={{0,2},{2,4},{4,6},{6,0},{8,14},{10,8},{12,10},{14,12},{1,3},{3,5},... | collective-permute-start | bytes 1228808 | tf_op jit(solution)/shard_map/ppermute | solution.py:834
  341.9 10.8 %collective-permute-start.10 = (bf16[4,104,640]{2,1,0:T(8,128)(2,1)}, bf16[4,104,640]{2,1,0:T(8,128)(2,1)}, u32[]{:S(2)}, u32[]{:S(2)}) collective-permute-start(bf16[4,104,640]{2,1,0:T(8,128)(2,1)} %get-tuple-element.124), channel_id=1, source_target_pairs={{0,16},{16,1},{1,17},{17,0},{8,25},{24,8},{9,24},{25,9},{2,18},{18... | collective-permute-start | bytes 1597448 | tf_op jit(solution)/shard_map/ppermute | solution.py:834
  344.2 21.5 %collective-permute-start.16 = (bf16[4,80,640]{2,1,0:T(8,128)(2,1)}, bf16[4,80,640]{2,1,0:T(8,128)(2,1)S(1)}, u32[]{:S(2)}, u32[]{:S(2)}) collective-permute-start(bf16[4,80,640]{2,1,0:T(8,128)(2,1)} %add_blocks.12), channel_id=1, source_target_pairs={{0,2},{2,4},{4,6},{6,0},{8,14},{10,8},{12,10},{14,12},{1,3},{3,5},... | collective-permute-start | bytes 1228808 | tf_op jit(solution)/shard_map/ppermute | solution.py:834
  355.5 23.3 %collective-permute-start.11 = (bf16[4,104,640]{2,1,0:T(8,128)(2,1)}, bf16[4,104,640]{2,1,0:T(8,128)(2,1)S(1)}, u32[]{:S(2)}, u32[]{:S(2)}) collective-permute-start(bf16[4,104,640]{2,1,0:T(8,128)(2,1)} %add_blocks.13), channel_id=1, source_target_pairs={{0,16},{16,1},{1,17},{17,0},{8,25},{24,8},{9,24},{25,9},{2,18},{18... | collective-permute-start | bytes 1597448 | tf_op jit(solution)/shard_map/ppermute | solution.py:834
  356.5 18.1 %collective-permute-start.5 = (bf16[128,1280]{1,0:T(8,128)(2,1)S(1)}, bf16[128,1280]{1,0:T(8,128)(2,1)S(1)}, u32[]{:S(2)}, u32[]{:S(2)}) collective-permute-start(bf16[128,1280]{1,0:T(8,128)(2,1)S(1)} %get-tuple-element.137), channel_id=1, source_target_pairs={{0,1},{1,0},{2,3},{3,2},{4,5},{5,4},{6,7},{7,6},{8,9},{9,8},{10,11... | collective-permute-start | bytes 983048 | tf_op jit(solution)/shard_map/ppermute | solution.py:994
  362.1 16.7 %all-to-all-start.8 = ((bf16[8,11,960]{2,1,0:T(8,128)(2,1)}), bf16[8,11,960]{2,1,0:T(8,128)(2,1)S(1)}, u32[]{:S(2)}, u32[]{:S(2)}) async-start(bf16[8,11,960]{2,1,0:T(8,128)(2,1)} %pad_maximum_fusion.1), calls=%async_computation.8 | async-start | bytes 524288 | tf_op jit(solution)/shard_map/all_to_all | solution.py:898
  369.0 14.0 %collective-permute-start.17 = (bf16[4,80,640]{2,1,0:T(8,128)(2,1)}, bf16[4,80,640]{2,1,0:T(8,128)(2,1)S(1)}, u32[]{:S(2)}, u32[]{:S(2)}) collective-permute-start(bf16[4,80,640]{2,1,0:T(8,128)(2,1)} %add_blocks.16), channel_id=1, source_target_pairs={{0,2},{2,4},{4,6},{6,0},{8,14},{10,8},{12,10},{14,12},{1,3},{3,5},... | collective-permute-start | bytes 1228808 | tf_op jit(solution)/shard_map/ppermute | solution.py:834
  382.5 13.9 %collective-permute-start.12 = (bf16[4,104,640]{2,1,0:T(8,128)(2,1)}, bf16[4,104,640]{2,1,0:T(8,128)(2,1)S(1)}, u32[]{:S(2)}, u32[]{:S(2)}) collective-permute-start(bf16[4,104,640]{2,1,0:T(8,128)(2,1)} %add_blocks.14), channel_id=1, source_target_pairs={{0,16},{16,1},{1,17},{17,0},{8,25},{24,8},{9,24},{25,9},{2,18},{18... | collective-permute-start | bytes 1597448 | tf_op jit(solution)/shard_map/ppermute | solution.py:834
  386.5 5.9 %collective-permute-start.18 = (bf16[80,640]{1,0:T(8,128)(2,1)}, bf16[80,640]{1,0:T(8,128)(2,1)S(1)}, u32[]{:S(2)}, u32[]{:S(2)}) collective-permute-start(bf16[80,640]{1,0:T(8,128)(2,1)} %get-tuple-element.132), channel_id=1, source_target_pairs={{0,32},{32,64},{64,96},{96,0},{1,33},{33,65},{65,97},{97,1},{2,34}... | collective-permute-start | bytes 307208 | tf_op jit(solution)/shard_map/ppermute | solution.py:837
  388.0 7.5 %collective-permute-start.19 = (bf16[80,640]{1,0:T(8,128)(2,1)}, bf16[80,640]{1,0:T(8,128)(2,1)S(1)}, u32[]{:S(2)}, u32[]{:S(2)}) collective-permute-start(bf16[80,640]{1,0:T(8,128)(2,1)} %get-tuple-element.133), channel_id=1, source_target_pairs={{0,64},{32,96},{64,0},{96,32},{1,65},{33,97},{65,1},{97,33},{2,66}... | collective-permute-start | bytes 307208 | tf_op jit(solution)/shard_map/ppermute | solution.py:837
  389.1 7.1 %collective-permute-start.20 = (bf16[80,640]{1,0:T(8,128)(2,1)}, bf16[80,640]{1,0:T(8,128)(2,1)S(1)}, u32[]{:S(2)}, u32[]{:S(2)}) collective-permute-start(bf16[80,640]{1,0:T(8,128)(2,1)} %get-tuple-element.134), channel_id=1, source_target_pairs={{0,96},{32,0},{64,32},{96,64},{1,97},{33,1},{65,33},{97,65},{2,98}... | collective-permute-start | bytes 307208 | tf_op jit(solution)/shard_map/ppermute | solution.py:837
  400.0 9.5 %collective-permute-start.13 = (bf16[104,640]{1,0:T(8,128)(2,1)}, bf16[104,640]{1,0:T(8,128)(2,1)S(1)}, u32[]{:S(2)}, u32[]{:S(2)}) collective-permute-start(bf16[104,640]{1,0:T(8,128)(2,1)} %get-tuple-element.127), channel_id=1, source_target_pairs={{0,2},{2,4},{4,6},{6,0},{1,3},{3,5},{5,7},{7,1},{8,10},{10,12},{12... | collective-permute-start | bytes 399368 | tf_op jit(solution)/shard_map/ppermute | solution.py:837
  400.1 9.3 %collective-permute-start.14 = (bf16[104,640]{1,0:T(8,128)(2,1)}, bf16[104,640]{1,0:T(8,128)(2,1)S(1)}, u32[]{:S(2)}, u32[]{:S(2)}) collective-permute-start(bf16[104,640]{1,0:T(8,128)(2,1)} %get-tuple-element.128), channel_id=1, source_target_pairs={{0,4},{2,6},{4,0},{6,2},{1,5},{3,7},{5,1},{7,3},{8,12},{10,14},{12... | collective-permute-start | bytes 399368 | tf_op jit(solution)/shard_map/ppermute | solution.py:837
  402.6 7.4 %collective-permute-start.15 = (bf16[104,640]{1,0:T(8,128)(2,1)}, bf16[104,640]{1,0:T(8,128)(2,1)S(1)}, u32[]{:S(2)}, u32[]{:S(2)}) collective-permute-start(bf16[104,640]{1,0:T(8,128)(2,1)} %get-tuple-element.129), channel_id=1, source_target_pairs={{0,6},{2,0},{4,2},{6,4},{1,7},{3,1},{5,3},{7,5},{8,14},{10,8},{12,... | collective-permute-start | bytes 399368 | tf_op jit(solution)/shard_map/ppermute | solution.py:837
  (19 other events, 110.4 us)
Sparse Core Ops, SparseCore 0:
  26.1 133.4 all-gather.2
  230.2 77.3 reduce-scatter.1
